TPU v7x, 32 devices: a whole 2x2x4 slice. The times are simulated.
32 devices in a mesh: dp: 2 (over x), expert: 16 (over z, y, core).
Axes of the slice: x: 2, y: 2, z: 4, core: 2. Of those that a mesh axis runs over, the one named last changes fastest.
Arguments:
- tokens: bfloat16 [64, 2048], P(('dp', 'expert')), may hold values from -6 to 6
- combine: bfloat16 [64], P(('dp', 'expert')), may hold values from 0.099609375 to 1
- routes: int32 [64], P(('dp', 'expert')), may hold values from 0 to 1, as said below
- capacity_slot: int32 [64], P(('dp', 'expert')), may hold values from -1 to 19, as said below
- readout: float32 [2048], replicated, may hold values from -6 to 6
- weight_in: bfloat16 [2, 2048, 14336], P('dp', None, 'expert'), may hold values from -0.125 to 0.125
- weight_out: bfloat16 [2, 14336, 2048], P('dp', 'expert'), may hold values from -0.046875 to 0.046875
Outputs:
- r2_grad: bfloat16 [64, 2048], P(('dp', 'expert'))
- grad_in: bfloat16 [2, 2048, 14336], P('dp', None, 'expert')
- grad_out: bfloat16 [2, 14336, 2048], P('dp', 'expert')
Inputs may be any that keep to these rules, and one draw needn't show every extreme that they name: `routes`: each token's expert. `capacity_slot`: in each aligned block of 32 tokens, the tokens routed to one expert carry slots 0, 1, 2, ... in token order while fewer than 20 came before them, and -1 after; in every block some expert receives 30 tokens or more, so its 20 slots are full.
All inputs are finite; a program needn't handle non-finite values.
Results may differ from a plain program's by a relative error of at most 0.006.
Values may be sent and summed in bfloat16 or wider, within the bound.
No kernel may reach another device: no remote copies, remote signals or barrier semaphores. Data moves between devices by JAX's collectives and lax.ppermute only.
A program may use at most 64 MiB of HBM per device.

v0:
```python
import jax
import jax.numpy as jnp
from jax import lax
from jax.sharding import PartitionSpec as P


def contract_rows(left, right):
    return lax.dot_general(
        left, right, (((0,), (0,)), ((), ())), preferred_element_type=jnp.float32
    )


def contract_cols(left, right):
    return lax.dot_general(
        left, right, (((1,), (1,)), ((), ())), preferred_element_type=jnp.float32
    )


def shards(tokens, combine, routes, capacity_slot, readout, weight_in, weight_out):
    group_x, group_c = (
        lax.all_gather(tokens, "expert", axis=0, tiled=True),
        lax.all_gather(combine, "expert", axis=0, tiled=True),
    )
    group_r, group_s = (
        lax.all_gather(routes, "expert", axis=0, tiled=True),
        lax.all_gather(capacity_slot, "expert", axis=0, tiled=True),
    )
    experts = lax.axis_size("dp")
    capacity = 5 * group_x.shape[0] // (4 * experts)
    slot_total = experts * capacity
    slot_index = lax.iota(jnp.int32, slot_total)
    slot_place = group_r * capacity + group_s
    onehot = ((slot_index[:, None] == slot_place[None, :]) & (group_s >= 0)[None, :]).astype(
        jnp.bfloat16
    )
    packed = jnp.dot(onehot, group_x, preferred_element_type=jnp.float32).astype(jnp.bfloat16)
    packed_c = jnp.dot(onehot, group_c, preferred_element_type=jnp.float32).astype(jnp.bfloat16)
    rows_in, rows_c = (
        lax.all_to_all(packed, "dp", split_axis=0, concat_axis=0, tiled=True),
        lax.all_to_all(packed_c, "dp", split_axis=0, concat_axis=0, tiled=True),
    )
    matrix_in = weight_in[0]
    matrix_out = weight_out[0]
    combine_col = rows_c.astype(jnp.float32)[:, None]
    head_row = readout[None, :]
    share_width = rows_in.shape[1] // lax.axis_size("expert")
    offset = lax.axis_index("expert") * share_width

    def column_share(values):
        return lax.dynamic_slice_in_dim(values, offset, share_width, 1)

    def shared_sum(term):
        return lax.psum_scatter(term, "expert", scatter_dimension=1, tiled=True)

    def regather(values):
        return lax.all_gather(values, "expert", axis=1, tiled=True)

    pre_act = jnp.dot(rows_in, matrix_in, preferred_element_type=jnp.float32)
    sigm = jax.nn.sigmoid(pre_act)
    slope_act = sigm * (1.0 + pre_act * (1.0 - sigm))
    bend_act = sigm * (1.0 - sigm) * (2.0 + pre_act * (1.0 - 2.0 * sigm))
    hidden = (pre_act * sigm).astype(jnp.bfloat16)
    term_mix = combine_col * jnp.dot(hidden, matrix_out, preferred_element_type=jnp.float32)
    head_part = column_share(head_row)
    tangent = jnp.tanh(column_share(rows_in).astype(jnp.float32) + shared_sum(term_mix))
    sech_sq = 1.0 - tangent * tangent
    upstream = head_part * sech_sq
    upstream_rows = regather(upstream.astype(jnp.bfloat16))
    back_hidden = combine_col * contract_cols(upstream_rows, matrix_out)
    back_pre = (back_hidden * slope_act).astype(jnp.bfloat16)
    term_grad = contract_cols(back_pre, matrix_in)
    grad_rows = regather((upstream + shared_sum(term_grad)).astype(jnp.bfloat16))
    second = jnp.dot(grad_rows, matrix_in, preferred_element_type=jnp.float32)
    push_rows = (combine_col * second * slope_act).astype(jnp.bfloat16)
    term_push = jnp.dot(push_rows, matrix_out, preferred_element_type=jnp.float32)
    total_push = column_share(grad_rows).astype(jnp.float32) + shared_sum(term_push)
    curve_term = total_push * head_part * (-2.0 * tangent * sech_sq)
    echo_rows = regather((combine_col * curve_term).astype(jnp.bfloat16))
    back_second = contract_cols(echo_rows, matrix_out)
    final_pre = (back_second * slope_act + second * back_hidden * bend_act).astype(jnp.bfloat16)
    grad_in = (contract_rows(grad_rows, back_pre) + contract_rows(rows_in, final_pre)).astype(
        jnp.bfloat16
    )
    grad_out = (contract_rows(push_rows, upstream_rows) + contract_rows(hidden, echo_rows)).astype(
        jnp.bfloat16
    )
    home_rows = lax.all_to_all(grad_rows, "dp", split_axis=0, concat_axis=0, tiled=True)
    own_place = jnp.clip(routes * capacity + capacity_slot, 0, slot_total - 1)
    picked = jnp.take(home_rows, own_place, axis=0)
    tangent_home = jnp.tanh(tokens.astype(jnp.float32))
    dropped = (head_row * (1.0 - tangent_home * tangent_home)).astype(jnp.bfloat16)
    r2_grad = jnp.where((capacity_slot >= 0)[:, None], picked, dropped)
    return (r2_grad, grad_in[None], grad_out[None])


def solution(mesh):
    placed = (
        P(("dp", "expert"), None),
        P(("dp", "expert")),
        P(("dp", "expert")),
        P(("dp", "expert")),
        P(),
        P("dp", None, "expert"),
        P("dp", "expert", None),
    )
    return jax.shard_map(
        shards,
        mesh=mesh,
        in_specs=placed,
        out_specs=(P(("dp", "expert"), None), P("dp", None, "expert"), P("dp", "expert", None)),
        check_vma=False,
    )
```

profile of v0, /device:TPU:0, one launch (start us, length us, event | category | flops | bytes accessed | tf_op | source)
XLA Modules:
  0.0 347.7 jit_solution(12817786850809937098)
XLA Ops:
  7.2 1.2 dynamic-slice.4
  10.8 13.7 %all-reduce.3 = (s32[32]{0:T(128)S(1)}, s32[32]{0:T(128)S(1)}) all-reduce(s32[32]{0:T(128)S(1)} %dynamic-update-slice.1, s32[32]{0:T(128)S(1)} %dynamic-update-slice), channel_id=1, replica_groups=mesh['dp'=2,'expert'=16] {'expert'}, use_global_device_ids=true, to_apply=%add.1 | all-reduce | flops 64 | bytes 512
  25.4 29.5 %all-reduce.2 = bf16[32]{0:T(256)(128)(2,1)S(1)} all-reduce(bf16[32]{0:T(256)(128)(2,1)S(1)} %dynamic-update-slice.2), channel_id=1, replica_groups=mesh['dp'=2,'expert'=16] {'expert'}, use_global_device_ids=true, to_apply=%add.2 | all-reduce | flops 32 | bytes 128
  55.7 3.2 all-to-all-start.1
  58.9 17.8 %all-gather = bf16[16,2,2048]{2,1,0:T(2,128)(2,1)S(1)} all-gather(bf16[1,2,2048]{2,1,0:T(2,128)(2,1)} %bitcast.58), channel_id=1, replica_groups=mesh['dp'=2,'expert'=16] {'expert'}, dimensions={0}, use_global_device_ids=true | all-gather | bytes 139264 | tf_op jit(solution)/shard_map/all_gather | solution.py:21
  77.6 3.4 all-to-all-start
  81.2 5.3 %all-to-all-done = bf16[2,20,2048]{2,1,0:T(8,128)(2,1)S(1)} async-done(((bf16[2,20,2048]{2,1,0:T(8,128)(2,1)}), bf16[2,20,2048]{2,1,0:T(8,128)(2,1)S(1)}, u32[]{:S(2)}, u32[]{:S(2)}) %all-to-all-start) | async-done | bytes 163872 | tf_op jit(solution)/shard_map/all_to_all | solution.py:39
  86.6 2.9 fusion.12
  89.7 1.5 fusion.16
  91.3 50.8 %reduce-scatter.4.cloned.1.call-done = f32[40,128]{1,0:T(8,128)} async-done(((f32[40,2048]{1,0:T(8,128)}), f32[40,128]{1,0:T(8,128)}) %reduce-scatter.4.cloned.1.call-update) | async-done | bytes 20496 | tf_op jit(solution)/shard_map/reduce_scatter | solution.py:53
  143.0 20.0 %all_gather.25 = bf16[40,2048]{1,0:T(8,128)(2,1)S(1)} all-gather(bf16[40,128]{1,0:T(8,128)(2,1)S(1)} %fusion.50), channel_id=1, replica_groups=mesh['dp'=2,'expert'=16] {'expert'}, dimensions={1}, use_global_device_ids=true | all-gather | bytes 174080 | tf_op jit(solution)/shard_map/all_gather | solution.py:56
  163.0 3.3 multiply_convert_fusion.1
  166.3 2.1 fusion.10
  168.4 50.4 %reduce-scatter.6.cloned.1.call-done = f32[40,128]{1,0:T(8,128)} async-done(((f32[40,2048]{1,0:T(8,128)}), f32[40,128]{1,0:T(8,128)}) %reduce-scatter.6.cloned.1.call-update) | async-done | bytes 20496 | tf_op jit(solution)/shard_map/reduce_scatter | solution.py:53
  219.6 19.9 %all_gather.26 = bf16[40,2048]{1,0:T(8,128)(2,1)S(1)} all-gather(bf16[40,128]{1,0:T(8,128)(2,1)S(1)} %add_convert_fusion.2), channel_id=1, replica_groups=mesh['dp'=2,'expert'=16] {'expert'}, dimensions={1}, use_global_device_ids=true | all-gather | bytes 174080 | tf_op jit(solution)/shard_map/all_gather | solution.py:56
  240.2 2.7 multiply_convert_fusion
  242.9 4.1 %fusion.59 = f32[2048,896]{1,0:T(8,128)} fusion(bf16[40,2048]{1,0:T(8,128)(2,1)S(1)} %all_gather.26, bf16[40,896]{1,0:T(8,128)(2,1)S(1)} %get-tuple-element.8), kind=kOutput, calls=%fused_computation.69 | convolution fusion | flops 146800640 | bytes 7575552 | tf_op jit(solution)/shard_map/dot_general | solution.py:8
  247.0 3.4 all-to-all-start.2
  250.5 3.5 %fusion.2 = f32[40,2048]{1,0:T(8,128)} fusion(bf16[40,896]{1,0:T(8,128)(2,1)S(1)} %get-tuple-element.10, bf16[1,896,2048]{2,1,0:T(8,128)(2,1)} %param.13), kind=kOutput, calls=%fused_computation.5 | convolution fusion | flops 146800640 | bytes 4069376 | tf_op jit(solution)/shard_map/dot_general | solution.py:75
  254.1 4.1 %fusion.60 = f32[896,2048]{1,0:T(8,128)} fusion(bf16[40,896]{1,0:T(8,128)(2,1)S(1)} %get-tuple-element.10, bf16[40,2048]{1,0:T(8,128)(2,1)S(1)} %all_gather.25), kind=kOutput, calls=%fused_computation.70 | convolution fusion | flops 146800640 | bytes 7575552 | tf_op jit(solution)/shard_map/dot_general | solution.py:8
  259.5 46.6 %reduce-scatter.8.cloned.1.call-done = f32[40,128]{1,0:T(8,128)} async-done(((f32[40,2048]{1,0:T(8,128)}), f32[40,128]{1,0:T(8,128)}) %reduce-scatter.8.cloned.1.call-update) | async-done | bytes 20496 | tf_op jit(solution)/shard_map/reduce_scatter | solution.py:53
  307.0 19.9 %all_gather.27 = bf16[40,2048]{1,0:T(8,128)(2,1)S(1)} all-gather(bf16[40,128]{1,0:T(8,128)(2,1)S(1)} %multiply_convert_fusion.3), channel_id=1, replica_groups=mesh['dp'=2,'expert'=16] {'expert'}, dimensions={1}, use_global_device_ids=true | all-gather | bytes 174080 | tf_op jit(solution)/shard_map/all_gather | solution.py:56
  326.8 6.1 %fusion.15 = bf16[1,896,2048]{2,1,0:T(8,128)(2,1)} fusion(f32[896,2048]{1,0:T(8,128)} %fusion.60, bf16[40,2048]{1,0:T(8,128)(2,1)S(1)} %all_gather.27, f32[40,896]{1,0:T(8,128)S(1)} %fusion.12), kind=kOutput, calls=%fused_computation.18 | convolution fusion | flops 150649856 | bytes 11317248 | tf_op jit(solution)/shard_map/dot_general | solution.py:8
  332.9 8.2 %fusion.14 = bf16[1,2048,896]{2,1,0:T(8,128)(2,1)} fusion(f32[2048,896]{1,0:T(8,128)} %fusion.59, bf16[40,2048]{1,0:T(8,128)(2,1)S(1)} %all_to_all.24, bf16[40,2048]{1,0:T(8,128)(2,1)S(1)} %all_gather.27, bf16[1,896,2048]{2,1,0:T(8,128)(2,1)} %param.13, f32[40,896]{1,0:T(8,128)S(1)} %fusion.12, f32[40,896]{1,0:T(8,128)S(1)} %get-tuple-element.11, ...), kind=kOutput, calls=%fused_computation.17 | convolution fusion | flops 297916416 | bytes 15437824 | tf_op jit(solution)/shard_map/dot_general | solution.py:8
  (48 shorter events, 9.4 us)
Async XLA Ops:
  55.7 21.9 %all-to-all-start.1 = ((bf16[2,20,1]{1,2,0:T(2,128)(2,1)}), bf16[2,20,1]{1,2,0:T(2,128)(2,1)S(1)}, u32[]{:S(2)}, u32[]{:S(2)}) async-start(bf16[2,20,1]{1,2,0:T(2,128)(2,1)} %all_to_all.30), calls=%async_computation.1 | async-start | bytes 2048 | tf_op jit(solution)/shard_map/all_to_all | solution.py:40
  77.6 8.9 %all-to-all-start = ((bf16[2,20,2048]{2,1,0:T(8,128)(2,1)}), bf16[2,20,2048]{2,1,0:T(8,128)(2,1)S(1)}, u32[]{:S(2)}, u32[]{:S(2)}) async-start(bf16[2,20,2048]{2,1,0:T(8,128)(2,1)} %all_to_all.22), calls=%async_computation | async-start | bytes 393216 | tf_op jit(solution)/shard_map/all_to_all | solution.py:39
  81.1 61.1 %reduce-scatter.4.cloned.1.call-start = ((), (), s32[]{:S(2)}) async-start(), calls=%async_computation.6 | async-start | bytes 348160 | tf_op jit(solution)/shard_map/reduce_scatter | solution.py:53
  86.6 3.1 copy-start
  86.6 4.7 %copy-start.4 = (f32[2048]{0:T(1024)S(1)}, f32[2048]{0:T(1024)}, u32[]{:S(2)}) copy-start(f32[2048]{0:T(1024)} %param.11) | copy-start | bytes 24580
  91.2 127.6 %reduce-scatter.6.cloned.1.call-start = ((), (), s32[]{:S(2)}) async-start(), calls=%async_computation.7 | async-start | bytes 348160 | tf_op jit(solution)/shard_map/reduce_scatter | solution.py:53
  142.1 24.2 %copy-start.1 = (bf16[1,2048,896]{2,1,0:T(8,128)(2,1)S(1)}, bf16[1,2048,896]{2,1,0:T(8,128)(2,1)}, u32[]{:S(2)}) copy-start(bf16[1,2048,896]{2,1,0:T(8,128)(2,1)} %param.12) | copy-start | bytes 11010052
  163.0 5.4 %copy-start.5 = (s32[2]{0:T(128)S(1)}, s32[2]{0:T(128)}, u32[]{:S(2)}) copy-start(s32[2]{0:T(128)} %param.10) | copy-start | bytes 28
  163.0 5.4 %copy-start.6 = (s32[2]{0:T(128)S(1)}, s32[2]{0:T(128)}, u32[]{:S(2)}) copy-start(s32[2]{0:T(128)} %param.9) | copy-start | bytes 28
  163.0 55.9 %copy-start.2 = (f32[40,128]{1,0:T(8,128)S(1)}, f32[40,128]{1,0:T(8,128)}, u32[]{:S(2)}) copy-start(f32[40,128]{1,0:T(8,128)} %reduce-scatter.4.cloned.1.call-done) | copy-start | bytes 61444
  247.0 11.2 %all-to-all-start.2 = ((bf16[2,20,2048]{2,1,0:T(8,128)(2,1)}), bf16[2,20,2048]{2,1,0:T(8,128)(2,1)S(1)}, u32[]{:S(2)}, u32[]{:S(2)}) async-start(bf16[2,20,2048]{2,1,0:T(8,128)(2,1)} %all_to_all.27), calls=%async_computation.4 | async-start | bytes 393216 | tf_op jit(solution)/shard_map/all_to_all | solution.py:87
  250.5 55.7 %reduce-scatter.8.cloned.1.call-start = ((), (), s32[]{:S(2)}) async-start(), calls=%async_computation.8 | async-start | bytes 348160 | tf_op jit(solution)/shard_map/reduce_scatter | solution.py:53
  254.1 4.8 %copy-start.3 = (bf16[2,2048]{1,0:T(2,128)(2,1)S(1)}, bf16[2,2048]{1,0:T(2,128)(2,1)}, u32[]{:S(2)}) copy-start(bf16[2,2048]{1,0:T(2,128)(2,1)} %param.7) | copy-start | bytes 24580
Sparse Core Ops, SparseCore 0:
  91.3 50.7 reduce-scatter.3
  168.5 50.3 reduce-scatter.5
  255.3 50.8 reduce-scatter.7
where the time goes:
time: 348 us
  waiting for transfers between devices  153 us (44%)
  blocking collectives  121 us (35%)
  matrix products  38.8 us (11%)
  between operations  14.6 us (4%)
  starting transfers between devices  10.2 us (3%)
  local copies, waits for them, and re-layouts  7.02 us (2%)
    reduce_scatter x3, waiting for transfers between devices, shared_sum(): return lax.psum_scatter(term, 'expert', scatter_dimension=1, tiled=True)  148 us
    all_gather x3, blocking collectives, regather(): return lax.all_gather(values, 'expert', axis=1, tiled=True)  59.7 us
    unnamed x2, blocking collectives  43.2 us
    dot_general x4, matrix products, contract_rows(): lax.dot_general(left, right, (((0,), (0,)), ((), ())), preferred_element_...  22.6 us
    all_gather x1, blocking collectives, shards(): lax.all_gather(tokens, 'expert', axis=0, tiled=True)  17.8 us
  transfers between devices with their start and end apart: 6, of which 4 were waited for; matrix products, arithmetic and copies ran while one was open for 3% of the time, Pallas kernels for 0%

commit v1 on v0

v1 whole, which is shorter than its diff:
```python
import jax
import jax.numpy as jnp
from jax import lax
from jax.sharding import PartitionSpec as P

BF = jnp.bfloat16
F32 = jnp.float32


def contract_rows(left, right):
    return lax.dot_general(left, right, (((0,), (0,)), ((), ())), preferred_element_type=F32)


def contract_cols(left, right):
    return lax.dot_general(left, right, (((1,), (1,)), ((), ())), preferred_element_type=F32)


def dot(left, right):
    return jnp.dot(left, right, preferred_element_type=F32)


def digits(total):
    sizes = []
    rest = total
    if rest % 2 == 0:
        sizes.append(2)
        rest //= 2
    twos = 0
    while rest % 2 == 0:
        rest //= 2
        twos += 1
    sizes += [2] * (twos % 2) + [4] * (twos // 2)
    if rest > 1:
        sizes.append(rest)
    placed, stride = [], 1
    for size in sizes:
        placed.append((stride, size))
        stride *= size
    return placed


def moved(index, stride, size, offset):
    digit = (index // stride) % size
    if size & (size - 1) == 0:
        target = digit ^ offset
    else:
        target = (digit + offset) % size
    return index + (target - digit) * stride


def fetch(values, axis, stride, size, offset, back=False):
    total = lax.axis_size(axis)
    pairs = [(moved(i, stride, size, offset), i) for i in range(total)]
    if back:
        pairs = [(there, here) for here, there in pairs]
    return lax.ppermute(values, axis, pairs)


def gather_rows(values, axis, stride, size):
    parts = [values] + [fetch(values, axis, stride, size, k) for k in range(1, size)]
    return jnp.concatenate(parts, axis=0)


def shards(tokens, combine, routes, capacity_slot, readout, weight_in, weight_out):
    n_dp = lax.axis_size("dp")
    n_ex = lax.axis_size("expert")
    local, width = tokens.shape
    capacity = 5 * local * n_ex // (4 * n_dp)
    rows = n_dp * capacity
    me_dp = lax.axis_index("dp")
    splits = digits(n_ex)
    core, chips = splits[0], splits[1:]

    kept = capacity_slot >= 0
    place = jnp.where(kept, me_dp * capacity + capacity_slot, -1)
    expert_id = jnp.where(kept, routes, -1)
    meta = jnp.stack(
        [expert_id.astype(BF), (place // 128).astype(BF), (place % 128).astype(BF), combine],
        axis=1,
    )
    packed = jnp.concatenate([tokens, jnp.pad(meta, ((0, 0), (0, 124)))], axis=1)

    gathered = gather_rows(packed, "dp", 1, n_dp)
    for stride, size in chips + [core]:
        gathered = gather_rows(gathered, "expert", stride, size)

    all_meta = gathered[:, width:].astype(F32)
    all_expert = all_meta[:, 0].astype(jnp.int32)
    all_place = (all_meta[:, 1] * 128 + all_meta[:, 2]).astype(jnp.int32)
    row_of = jnp.where(all_expert == me_dp, all_place, -1)
    onehot = (lax.iota(jnp.int32, rows)[:, None] == row_of[None, :]).astype(BF)
    rows_all = dot(onehot, gathered).astype(BF)
    rows_in = rows_all[:, :width]
    combine_col = rows_all[:, width + 3 : width + 4].astype(F32)

    matrix_in = weight_in[0]
    matrix_out = weight_out[0]
    half = width // core[1]
    my_core = lax.axis_index("expert") % core[1]
    head_part = lax.dynamic_slice_in_dim(readout[None, :], my_core * half, half, 1)

    def core_part(values, offset):
        at = moved(my_core, 1, core[1], offset)
        return lax.dynamic_slice_in_dim(values, at * half, half, 1)

    def shared_sum(term):
        total = core_part(term, 0)
        for k in range(1, core[1]):
            total = total + fetch(core_part(term, k), "expert", *core, k, back=False)
        for stride, size in chips:
            own = total.astype(BF)
            parts = [own] + [fetch(own, "expert", stride, size, k) for k in range(1, size)]
            total = sum(part.astype(F32) for part in parts)
        return total

    def regather(values):
        full = jnp.zeros((values.shape[0], width), values.dtype)
        for k in range(core[1]):
            part = values if k == 0 else fetch(values, "expert", *core, k)
            at = moved(my_core, 1, core[1], k)
            full = lax.dynamic_update_slice_in_dim(full, part, at * half, 1)
        return full

    pre_act = dot(rows_in, matrix_in)
    sigm = jax.nn.sigmoid(pre_act)
    slope_act = sigm * (1.0 + pre_act * (1.0 - sigm))
    bend_act = sigm * (1.0 - sigm) * (2.0 + pre_act * (1.0 - 2.0 * sigm))
    hidden = (pre_act * sigm).astype(BF)
    mixed = shared_sum(combine_col * dot(hidden, matrix_out))
    tangent = jnp.tanh(core_part(rows_in, 0).astype(F32) + mixed)
    sech_sq = 1.0 - tangent * tangent
    upstream = head_part * sech_sq
    upstream_rows = regather(upstream.astype(BF))
    back_hidden = combine_col * contract_cols(upstream_rows, matrix_out)
    back_pre = (back_hidden * slope_act).astype(BF)
    grad_part = (upstream + shared_sum(contract_cols(back_pre, matrix_in))).astype(BF)
    grad_rows = regather(grad_part)
    second = dot(grad_rows, matrix_in)
    push_rows = (combine_col * second * slope_act).astype(BF)
    total_push = grad_part.astype(F32) + shared_sum(dot(push_rows, matrix_out))
    curve_term = total_push * head_part * (-2.0 * tangent * sech_sq)
    echo_rows = regather((combine_col * curve_term).astype(BF))
    back_second = contract_cols(echo_rows, matrix_out)
    final_pre = (back_second * slope_act + second * back_hidden * bend_act).astype(BF)
    grad_in = contract_rows(
        jnp.concatenate([grad_rows, rows_in], 0), jnp.concatenate([back_pre, final_pre], 0)
    ).astype(BF)
    grad_out = contract_rows(
        jnp.concatenate([push_rows, hidden], 0), jnp.concatenate([upstream_rows, echo_rows], 0)
    ).astype(BF)

    picked = jnp.zeros((local, width), F32)
    for k in range(n_dp):
        rows_wanted = row_of[k * local : (k + 1) * local]
        pick = (rows_wanted[:, None] == lax.iota(jnp.int32, rows)[None, :]).astype(BF)
        found = dot(pick, grad_rows).astype(BF)
        if k > 0:
            found = fetch(found, "dp", 1, n_dp, k, back=True)
        picked = picked + found.astype(F32)
    tangent_home = jnp.tanh(tokens.astype(F32))
    dropped = readout[None, :] * (1.0 - tangent_home * tangent_home)
    r2_grad = jnp.where(kept[:, None], picked, dropped).astype(BF)
    return (r2_grad, grad_in[None], grad_out[None])


def solution(mesh):
    placed = (
        P(("dp", "expert"), None),
        P(("dp", "expert")),
        P(("dp", "expert")),
        P(("dp", "expert")),
        P(),
        P("dp", None, "expert"),
        P("dp", "expert", None),
    )
    return jax.shard_map(
        shards,
        mesh=mesh,
        in_specs=placed,
        out_specs=(P(("dp", "expert"), None), P("dp", None, "expert"), P("dp", "expert", None)),
        check_vma=False,
    )
```

time: 348 us -> 92.7 us (0.27)
  blocking collectives: 121 us -> 0 us
  waiting for transfers between devices: 153 us -> 37.6 us
  matrix products: 38.8 us -> 18.2 us
  starting transfers between devices: 10.2 us -> 30.5 us
  between operations: 14.6 us -> 0.96 us
  local copies, waits for them, and re-layouts: 7.02 us -> 0.7 us
    reduce_scatter x3 -> x0, waiting for transfers between devices: 148 us -> none  [shared_sum(): return lax.psum_scatter(term, 'expert', scatter_dimension=1, tiled=True)]
    all_gather x4 -> x0, blocking collectives: 77.5 us -> none  [the longest x3 59.7 us: regather(): return lax.all_gather(values, 'expert', axis=1, tiled=True)]
    unnamed x2 -> x0, blocking collectives: 43.2 us -> none
    ppermute x0 -> x25, waiting for transfers between devices: none -> 37.6 us  [fetch(): return lax.ppermute(values, axis, pairs)]
    ppermute x0 -> x25, starting transfers between devices: none -> 30.5 us  [fetch(): return lax.ppermute(values, axis, pairs)]
    dot_general x4 -> x2, matrix products: 22.6 us -> 5.97 us  [contract_rows(): lax.dot_general(left, right, (((0,), (0,)), ((), ())), preferred_element_...]
    all_to_all x3 -> x0, starting transfers between devices: 10.1 us -> none  [the longest x1 3.43 us: shards(): lax.all_to_all(packed, 'dp', split_axis=0, concat_axis=0, tiled=True)]
    all_to_all x3 -> x0, waiting for transfers between devices: 5.33 us -> none  [the longest x1 5.33 us: shards(): lax.all_to_all(packed, 'dp', split_axis=0, concat_axis=0, tiled=True)]
  transfers between devices with their start and end apart: 6 -> 25, of which waited for: 4 -> 20; matrix products, arithmetic and copies ran while one was open for 3% -> 1% of each run, Pallas kernels for 0% -> 0%
where the time goes in v1:
time: 92.7 us; the launch traced here: 92.3 us
  waiting for transfers between devices  37.6 us (41%)
  starting transfers between devices  30.5 us (33%)
  matrix products  18.2 us (20%)
  other arithmetic  4.31 us (5%)
  between operations  0.96 us (1%)
    ppermute x25, waiting for transfers between devices, fetch(): return lax.ppermute(values, axis, pairs)  37.6 us
    ppermute x25, starting transfers between devices, fetch(): return lax.ppermute(values, axis, pairs)  30.5 us
    dot_general x7, matrix products, dot(): return jnp.dot(left, right, preferred_element_type=F32)  6.47 us
    dot_general x2, matrix products, contract_rows(): lax.dot_general(left, right, (((0,), (0,)), ((), ())), preferred_element_...  5.97 us
    dot_general x3, matrix products, contract_cols(): lax.dot_general(left, right, (((1,), (1,)), ((), ())), preferred_element_...  5.78 us
  transfers between devices with their start and end apart: 25, of which 20 were waited for; matrix products, arithmetic and copies ran while one was open for 1% of the time, Pallas kernels for 0%

profile of v1, /device:TPU:0, one launch (start us, length us, event | category | flops | bytes accessed | tf_op | source)
XLA Modules:
  0.0 92.3 jit_solution(18194187066180108174)
XLA Ops:
  2.8 3.0 %collective-permute-start = (bf16[2,2176]{1,0:T(2,128)(2,1)S(1)}, bf16[2,2176]{1,0:T(2,128)(2,1)S(1)}, u32[]{:S(2)}, u32[]{:S(2)}) collective-permute-start(bf16[2,2176]{1,0:T(2,128)(2,1)S(1)} %pad_maximum_fusion.2), channel_id=1, source_target_pairs={{16,0},{0,16},{17,1},{1,17},{18,2},{2,18},{19,3},{3,19},{20,4},{4,... | collective-permute-start | bytes 26120 | tf_op jit(solution)/shard_map/ppermute | solution.py:56
  5.8 1.6 %collective-permute-done = bf16[2,2176]{1,0:T(2,128)(2,1)S(1)} collective-permute-done((bf16[2,2176]{1,0:T(2,128)(2,1)S(1)}, bf16[2,2176]{1,0:T(2,128)(2,1)S(1)}, u32[]{:S(2)}, u32[]{:S(2)}) %collective-permute-start) | collective-permute-done | bytes 8736 | tf_op jit(solution)/shard_map/ppermute | solution.py:56
  8.2 2.1 %collective-permute-start.1 = (bf16[4,2176]{1,0:T(4,128)(2,1)S(1)}, bf16[4,2176]{1,0:T(4,128)(2,1)S(1)}, u32[]{:S(2)}, u32[]{:S(2)}) collective-permute-start(bf16[4,2176]{1,0:T(4,128)(2,1)S(1)} %pad_maximum_fusion.1), channel_id=1, source_target_pairs={{2,0},{3,1},{0,2},{1,3},{6,4},{7,5},{4,6},{5,7},{10,8},{11,9},{8,1... | collective-permute-start | bytes 52232 | tf_op jit(solution)/shard_map/ppermute | solution.py:56
  10.3 1.7 %collective-permute-done.1 = bf16[4,2176]{1,0:T(4,128)(2,1)S(1)} collective-permute-done((bf16[4,2176]{1,0:T(4,128)(2,1)S(1)}, bf16[4,2176]{1,0:T(4,128)(2,1)S(1)}, u32[]{:S(2)}, u32[]{:S(2)}) %collective-permute-start.1) | collective-permute-done | bytes 17440 | tf_op jit(solution)/shard_map/ppermute | solution.py:56
  12.8 4.2 %collective-permute-start.4 = (bf16[8,2176]{1,0:T(8,128)(2,1)S(1)}, bf16[8,2176]{1,0:T(8,128)(2,1)S(1)}, u32[]{:S(2)}, u32[]{:S(2)}) collective-permute-start(bf16[8,2176]{1,0:T(8,128)(2,1)S(1)} %pad_maximum_fusion), channel_id=1, source_target_pairs={{12,0},{13,1},{14,2},{15,3},{8,4},{9,5},{10,6},{11,7},{4,8},{5,9},... | collective-permute-start | bytes 104456 | tf_op jit(solution)/shard_map/ppermute | solution.py:56
  18.9 2.9 %collective-permute-done.3 = bf16[8,2176]{1,0:T(8,128)(2,1)S(1)} collective-permute-done((bf16[8,2176]{1,0:T(8,128)(2,1)S(1)}, bf16[8,2176]{1,0:T(8,128)(2,1)S(1)}, u32[]{:S(2)}, u32[]{:S(2)}) %collective-permute-start.3) | collective-permute-done | bytes 34848 | tf_op jit(solution)/shard_map/ppermute | solution.py:56
  24.1 3.1 %multiply_convert_fusion.3 = (bf16[40,896]{1,0:T(8,128)(2,1)S(1)}, f32[40,896]{1,0:T(8,128)S(1)}) fusion(bf16[1,2048,896]{2,1,0:T(8,128)(2,1)} %param.12, bf16[40,2176]{1,0:T(8,128)(2,1)S(1)} %convolution_convert_fusion), kind=kOutput, calls=%fused_computation.59 | convolution fusion | flops 146979840 | bytes 4048896 | tf_op jit(solution)/shard_map/dot_general | solution.py:19
  29.4 1.6 %collective-permute-start.7 = (bf16[40,1024]{1,0:T(8,128)(2,1)S(1)}, bf16[40,1024]{1,0:T(8,128)(2,1)S(1)}, u32[]{:S(2)}, u32[]{:S(2)}) collective-permute-start(bf16[40,1024]{1,0:T(8,128)(2,1)S(1)} %add_convert_fusion.6), channel_id=1, source_target_pairs={{2,0},{3,1},{0,2},{1,3},{6,4},{7,5},{4,6},{5,7},{10,8},{11,9},{8,1... | collective-permute-start | bytes 245768 | tf_op jit(solution)/shard_map/ppermute | solution.py:56
  31.0 3.0 %collective-permute-done.7 = bf16[40,1024]{1,0:T(8,128)(2,1)S(1)} collective-permute-done((bf16[40,1024]{1,0:T(8,128)(2,1)S(1)}, bf16[40,1024]{1,0:T(8,128)(2,1)S(1)}, u32[]{:S(2)}, u32[]{:S(2)}) %collective-permute-start.7) | collective-permute-done | bytes 81952 | tf_op jit(solution)/shard_map/ppermute | solution.py:56
  36.2 2.3 %collective-permute-start.8 = (bf16[40,1024]{1,0:T(8,128)(2,1)S(1)}, bf16[40,1024]{1,0:T(8,128)(2,1)S(1)}, u32[]{:S(2)}, u32[]{:S(2)}) collective-permute-start(bf16[40,1024]{1,0:T(8,128)(2,1)S(1)} %add_convert_fusion.5), channel_id=1, source_target_pairs={{4,0},{5,1},{6,2},{7,3},{0,4},{1,5},{2,6},{3,7},{12,8},{13,9},{14,... | collective-permute-start | bytes 245768 | tf_op jit(solution)/shard_map/ppermute | solution.py:56
  38.5 2.8 %collective-permute-done.10 = bf16[40,1024]{1,0:T(8,128)(2,1)S(1)} collective-permute-done((bf16[40,1024]{1,0:T(8,128)(2,1)S(1)}, bf16[40,1024]{1,0:T(8,128)(2,1)S(1)}, u32[]{:S(2)}, u32[]{:S(2)}) %collective-permute-start.10) | collective-permute-done | bytes 81952 | tf_op jit(solution)/shard_map/ppermute | solution.py:56
  41.2 2.5 %collective-permute-done.9 = bf16[40,1024]{1,0:T(8,128)(2,1)S(1)} collective-permute-done((bf16[40,1024]{1,0:T(8,128)(2,1)S(1)}, bf16[40,1024]{1,0:T(8,128)(2,1)S(1)}, u32[]{:S(2)}, u32[]{:S(2)}) %collective-permute-start.9) | collective-permute-done | bytes 81952 | tf_op jit(solution)/shard_map/ppermute | solution.py:56
  45.3 3.2 %multiply_convert_fusion.2 = (bf16[40,896]{1,0:T(8,128)(2,1)S(1)}, f32[40,896]{1,0:T(8,128)S(1)}) fusion(f32[40,896]{1,0:T(8,128)S(1)} %get-tuple-element.18, bf16[40,2048]{1,0:T(8,128)(2,1)S(1)} %constant_dynamic-update-slice_fusion.4, bf16[1,896,2048]{2,1,0:T(8,128)(2,1)} %param.13, f32[40]{0:T(128)S(1)} %convert_reduce_fusion), kind=kOutput, calls=%fused_computation.58 | convolution fusion | flops 147159040 | bytes 4192416 | tf_op jit(solution)/shard_map/dot_general | solution.py:15
  53.0 3.0 %collective-permute-done.13 = bf16[40,1024]{1,0:T(8,128)(2,1)S(1)} collective-permute-done((bf16[40,1024]{1,0:T(8,128)(2,1)S(1)}, bf16[40,1024]{1,0:T(8,128)(2,1)S(1)}, u32[]{:S(2)}, u32[]{:S(2)}) %collective-permute-start.13) | collective-permute-done | bytes 81952 | tf_op jit(solution)/shard_map/ppermute | solution.py:56
  56.0 2.2 %collective-permute-start.16 = (bf16[40,1024]{1,0:T(8,128)(2,1)S(1)}, bf16[40,1024]{1,0:T(8,128)(2,1)S(1)}, u32[]{:S(2)}, u32[]{:S(2)}) collective-permute-start(bf16[40,1024]{1,0:T(8,128)(2,1)S(1)} %add_convert_fusion.3), channel_id=1, source_target_pairs={{12,0},{13,1},{14,2},{15,3},{8,4},{9,5},{10,6},{11,7},{4,8},{5,9},... | collective-permute-start | bytes 245768 | tf_op jit(solution)/shard_map/ppermute | solution.py:56
  58.2 2.2 %collective-permute-start.14 = (bf16[40,1024]{1,0:T(8,128)(2,1)S(1)}, bf16[40,1024]{1,0:T(8,128)(2,1)S(1)}, u32[]{:S(2)}, u32[]{:S(2)}) collective-permute-start(bf16[40,1024]{1,0:T(8,128)(2,1)S(1)} %add_convert_fusion.3), channel_id=1, source_target_pairs={{4,0},{5,1},{6,2},{7,3},{0,4},{1,5},{2,6},{3,7},{12,8},{13,9},{14,... | collective-permute-start | bytes 245768 | tf_op jit(solution)/shard_map/ppermute | solution.py:56
  60.4 2.6 %collective-permute-done.16 = bf16[40,1024]{1,0:T(8,128)(2,1)S(1)} collective-permute-done((bf16[40,1024]{1,0:T(8,128)(2,1)S(1)}, bf16[40,1024]{1,0:T(8,128)(2,1)S(1)}, u32[]{:S(2)}, u32[]{:S(2)}) %collective-permute-start.16) | collective-permute-done | bytes 81952 | tf_op jit(solution)/shard_map/ppermute | solution.py:56
  63.0 2.0 %collective-permute-done.15 = bf16[40,1024]{1,0:T(8,128)(2,1)S(1)} collective-permute-done((bf16[40,1024]{1,0:T(8,128)(2,1)S(1)}, bf16[40,1024]{1,0:T(8,128)(2,1)S(1)}, u32[]{:S(2)}, u32[]{:S(2)}) %collective-permute-start.15) | collective-permute-done | bytes 81952 | tf_op jit(solution)/shard_map/ppermute | solution.py:56
  71.2 2.8 %collective-permute-done.20 = bf16[40,1024]{1,0:T(8,128)(2,1)S(1)} collective-permute-done((bf16[40,1024]{1,0:T(8,128)(2,1)S(1)}, bf16[40,1024]{1,0:T(8,128)(2,1)S(1)}, u32[]{:S(2)}, u32[]{:S(2)}) %collective-permute-start.20) | collective-permute-done | bytes 81952 | tf_op jit(solution)/shard_map/ppermute | solution.py:56
  74.1 2.2 %collective-permute-start.23 = (bf16[40,1024]{1,0:T(8,128)(2,1)S(1)}, bf16[40,1024]{1,0:T(8,128)(2,1)S(1)}, u32[]{:S(2)}, u32[]{:S(2)}) collective-permute-start(bf16[40,1024]{1,0:T(8,128)(2,1)S(1)} %add_convert_fusion), channel_id=1, source_target_pairs={{12,0},{13,1},{14,2},{15,3},{8,4},{9,5},{10,6},{11,7},{4,8},{5,9},... | collective-permute-start | bytes 245768 | tf_op jit(solution)/shard_map/ppermute | solution.py:56
  76.3 2.2 %collective-permute-start.21 = (bf16[40,1024]{1,0:T(8,128)(2,1)S(1)}, bf16[40,1024]{1,0:T(8,128)(2,1)S(1)}, u32[]{:S(2)}, u32[]{:S(2)}) collective-permute-start(bf16[40,1024]{1,0:T(8,128)(2,1)S(1)} %add_convert_fusion), channel_id=1, source_target_pairs={{4,0},{5,1},{6,2},{7,3},{0,4},{1,5},{2,6},{3,7},{12,8},{13,9},{14,... | collective-permute-start | bytes 245768 | tf_op jit(solution)/shard_map/ppermute | solution.py:56
  81.1 2.5 %collective-permute-done.22 = bf16[40,1024]{1,0:T(8,128)(2,1)S(1)} collective-permute-done((bf16[40,1024]{1,0:T(8,128)(2,1)S(1)}, bf16[40,1024]{1,0:T(8,128)(2,1)S(1)}, u32[]{:S(2)}, u32[]{:S(2)}) %collective-permute-start.22) | collective-permute-done | bytes 81952 | tf_op jit(solution)/shard_map/ppermute | solution.py:56
  85.1 3.0 %convert_bitcast_fusion = bf16[1,896,2048]{2,1,0:T(8,128)(2,1)} fusion(bf16[40,2048]{1,0:T(8,128)(2,1)S(1)} %constant_dynamic-update-slice_fusion, bf16[40,2048]{1,0:T(8,128)(2,1)S(1)} %constant_dynamic-update-slice_fusion.4, bf16[40,896]{1,0:T(8,128)(2,1)S(1)} %get-tuple-element.17, bf16[40,896]{1,0:T(8,128)(2,1)S(1)} %get-tuple-element.21), kind=kOutput, calls=%fused_computation.14 | convolution fusion | flops 296378368 | bytes 4141056 | tf_op jit(solution)/shard_map/dot_general | solution.py:11
  89.3 3.0 %convert_bitcast_fusion.1 = bf16[1,2048,896]{2,1,0:T(8,128)(2,1)} fusion(bf16[40,2048]{1,0:T(8,128)(2,1)S(1)} %slice.45, bf16[40,2048]{1,0:T(8,128)(2,1)S(1)} %constant_dynamic-update-slice_fusion.2, bf16[40,896]{1,0:T(8,128)(2,1)S(1)} %fusion.30, bf16[40,896]{1,0:T(8,128)(2,1)S(1)} %get-tuple-element.19), kind=kOutput, calls=%fused_computation.15 | convolution fusion | flops 296378368 | bytes 4141056 | tf_op jit(solution)/shard_map/dot_general | solution.py:11
  (85 shorter events, 29.5 us)
Async XLA Ops:
  2.8 4.6 %collective-permute-start = (bf16[2,2176]{1,0:T(2,128)(2,1)S(1)}, bf16[2,2176]{1,0:T(2,128)(2,1)S(1)}, u32[]{:S(2)}, u32[]{:S(2)}) collective-permute-start(bf16[2,2176]{1,0:T(2,128)(2,1)S(1)} %pad_maximum_fusion.2), channel_id=1, source_target_pairs={{16,0},{0,16},{17,1},{1,17},{18,2},{2,18},{19,3},{3,19},{20,4},{4,... | collective-permute-start | bytes 26120 | tf_op jit(solution)/shard_map/ppermute | solution.py:56
  8.2 3.8 %collective-permute-start.1 = (bf16[4,2176]{1,0:T(4,128)(2,1)S(1)}, bf16[4,2176]{1,0:T(4,128)(2,1)S(1)}, u32[]{:S(2)}, u32[]{:S(2)}) collective-permute-start(bf16[4,2176]{1,0:T(4,128)(2,1)S(1)} %pad_maximum_fusion.1), channel_id=1, source_target_pairs={{2,0},{3,1},{0,2},{1,3},{6,4},{7,5},{4,6},{5,7},{10,8},{11,9},{8,1... | collective-permute-start | bytes 52232 | tf_op jit(solution)/shard_map/ppermute | solution.py:56
  12.8 6.1 %collective-permute-start.4 = (bf16[8,2176]{1,0:T(8,128)(2,1)S(1)}, bf16[8,2176]{1,0:T(8,128)(2,1)S(1)}, u32[]{:S(2)}, u32[]{:S(2)}) collective-permute-start(bf16[8,2176]{1,0:T(8,128)(2,1)S(1)} %pad_maximum_fusion), channel_id=1, source_target_pairs={{12,0},{13,1},{14,2},{15,3},{8,4},{9,5},{10,6},{11,7},{4,8},{5,9},... | collective-permute-start | bytes 104456 | tf_op jit(solution)/shard_map/ppermute | solution.py:56
  16.9 4.8 %collective-permute-start.3 = (bf16[8,2176]{1,0:T(8,128)(2,1)S(1)}, bf16[8,2176]{1,0:T(8,128)(2,1)S(1)}, u32[]{:S(2)}, u32[]{:S(2)}) collective-permute-start(bf16[8,2176]{1,0:T(8,128)(2,1)S(1)} %pad_maximum_fusion), channel_id=1, source_target_pairs={{8,0},{9,1},{10,2},{11,3},{12,4},{13,5},{14,6},{15,7},{0,8},{1,9},... | collective-permute-start | bytes 104456 | tf_op jit(solution)/shard_map/ppermute | solution.py:56
  16.9 4.8 %collective-permute-start.2 = (bf16[8,2176]{1,0:T(8,128)(2,1)S(1)}, bf16[8,2176]{1,0:T(8,128)(2,1)S(1)}, u32[]{:S(2)}, u32[]{:S(2)}) collective-permute-start(bf16[8,2176]{1,0:T(8,128)(2,1)S(1)} %pad_maximum_fusion), channel_id=1, source_target_pairs={{4,0},{5,1},{6,2},{7,3},{0,4},{1,5},{2,6},{3,7},{12,8},{13,9},{14,... | collective-permute-start | bytes 104456 | tf_op jit(solution)/shard_map/ppermute | solution.py:56
  21.9 1.4 %collective-permute-start.5 = (bf16[32,2176]{1,0:T(8,128)(2,1)S(1)}, bf16[32,2176]{1,0:T(8,128)(2,1)S(1)}, u32[]{:S(2)}, u32[]{:S(2)}) collective-permute-start(bf16[32,2176]{1,0:T(8,128)(2,1)S(1)} %concatenate.33), channel_id=1, source_target_pairs={{1,0},{0,1},{3,2},{2,3},{5,4},{4,5},{7,6},{6,7},{9,8},{8,9},{11,10... | collective-permute-start | bytes 417800 | tf_op jit(solution)/shard_map/ppermute | solution.py:56
  27.9 1.5 %collective-permute-start.6 = (f32[40,1024]{1,0:T(8,128)S(1)}, f32[40,1024]{1,0:T(8,128)S(1)}, u32[]{:S(2)}, u32[]{:S(2)}) collective-permute-start(f32[40,1024]{1,0:T(8,128)S(1)} %constant_dynamic-slice_fusion.2), channel_id=1, source_target_pairs={{1,0},{0,1},{3,2},{2,3},{5,4},{4,5},{7,6},{6,7},{9,8},{8,9},{11,10... | collective-permute-start | bytes 491528 | tf_op jit(solution)/shard_map/ppermute | solution.py:56
  29.4 4.6 %collective-permute-start.7 = (bf16[40,1024]{1,0:T(8,128)(2,1)S(1)}, bf16[40,1024]{1,0:T(8,128)(2,1)S(1)}, u32[]{:S(2)}, u32[]{:S(2)}) collective-permute-start(bf16[40,1024]{1,0:T(8,128)(2,1)S(1)} %add_convert_fusion.6), channel_id=1, source_target_pairs={{2,0},{3,1},{0,2},{1,3},{6,4},{7,5},{4,6},{5,7},{10,8},{11,9},{8,1... | collective-permute-start | bytes 245768 | tf_op jit(solution)/shard_map/ppermute | solution.py:56
  34.0 7.2 %collective-permute-start.10 = (bf16[40,1024]{1,0:T(8,128)(2,1)S(1)}, bf16[40,1024]{1,0:T(8,128)(2,1)S(1)}, u32[]{:S(2)}, u32[]{:S(2)}) collective-permute-start(bf16[40,1024]{1,0:T(8,128)(2,1)S(1)} %add_convert_fusion.5), channel_id=1, source_target_pairs={{12,0},{13,1},{14,2},{15,3},{8,4},{9,5},{10,6},{11,7},{4,8},{5,9},... | collective-permute-start | bytes 245768 | tf_op jit(solution)/shard_map/ppermute | solution.py:56
  35.5 8.2 %collective-permute-start.9 = (bf16[40,1024]{1,0:T(8,128)(2,1)S(1)}, bf16[40,1024]{1,0:T(8,128)(2,1)S(1)}, u32[]{:S(2)}, u32[]{:S(2)}) collective-permute-start(bf16[40,1024]{1,0:T(8,128)(2,1)S(1)} %add_convert_fusion.5), channel_id=1, source_target_pairs={{8,0},{9,1},{10,2},{11,3},{12,4},{13,5},{14,6},{15,7},{0,8},{1,9},... | collective-permute-start | bytes 245768 | tf_op jit(solution)/shard_map/ppermute | solution.py:56
  36.2 7.6 %collective-permute-start.8 = (bf16[40,1024]{1,0:T(8,128)(2,1)S(1)}, bf16[40,1024]{1,0:T(8,128)(2,1)S(1)}, u32[]{:S(2)}, u32[]{:S(2)}) collective-permute-start(bf16[40,1024]{1,0:T(8,128)(2,1)S(1)} %add_convert_fusion.5), channel_id=1, source_target_pairs={{4,0},{5,1},{6,2},{7,3},{0,4},{1,5},{2,6},{3,7},{12,8},{13,9},{14,... | collective-permute-start | bytes 245768 | tf_op jit(solution)/shard_map/ppermute | solution.py:56
  43.9 1.3 %collective-permute-start.11 = (bf16[40,1024]{1,0:T(8,128)(2,1)S(1)}, bf16[40,1024]{1,0:T(8,128)(2,1)S(1)}, u32[]{:S(2)}, u32[]{:S(2)}) collective-permute-start(bf16[40,1024]{1,0:T(8,128)(2,1)S(1)} %get-tuple-element.10), channel_id=1, source_target_pairs={{1,0},{0,1},{3,2},{2,3},{5,4},{4,5},{7,6},{6,7},{9,8},{8,9},{11,10... | collective-permute-start | bytes 245768 | tf_op jit(solution)/shard_map/ppermute | solution.py:56
  49.9 1.5 %collective-permute-start.12 = (f32[40,1024]{1,0:T(8,128)S(1)}, f32[40,1024]{1,0:T(8,128)S(1)}, u32[]{:S(2)}, u32[]{:S(2)}) collective-permute-start(f32[40,1024]{1,0:T(8,128)S(1)} %constant_dynamic-slice_fusion.1), channel_id=1, source_target_pairs={{1,0},{0,1},{3,2},{2,3},{5,4},{4,5},{7,6},{6,7},{9,8},{8,9},{11,10... | collective-permute-start | bytes 491528 | tf_op jit(solution)/shard_map/ppermute | solution.py:56
  51.4 4.6 %collective-permute-start.13 = (bf16[40,1024]{1,0:T(8,128)(2,1)S(1)}, bf16[40,1024]{1,0:T(8,128)(2,1)S(1)}, u32[]{:S(2)}, u32[]{:S(2)}) collective-permute-start(bf16[40,1024]{1,0:T(8,128)(2,1)S(1)} %add_convert_fusion.4), channel_id=1, source_target_pairs={{2,0},{3,1},{0,2},{1,3},{6,4},{7,5},{4,6},{5,7},{10,8},{11,9},{8,1... | collective-permute-start | bytes 245768 | tf_op jit(solution)/shard_map/ppermute | solution.py:56
  56.0 7.0 %collective-permute-start.16 = (bf16[40,1024]{1,0:T(8,128)(2,1)S(1)}, bf16[40,1024]{1,0:T(8,128)(2,1)S(1)}, u32[]{:S(2)}, u32[]{:S(2)}) collective-permute-start(bf16[40,1024]{1,0:T(8,128)(2,1)S(1)} %add_convert_fusion.3), channel_id=1, source_target_pairs={{12,0},{13,1},{14,2},{15,3},{8,4},{9,5},{10,6},{11,7},{4,8},{5,9},... | collective-permute-start | bytes 245768 | tf_op jit(solution)/shard_map/ppermute | solution.py:56
  58.2 6.8 %collective-permute-start.15 = (bf16[40,1024]{1,0:T(8,128)(2,1)S(1)}, bf16[40,1024]{1,0:T(8,128)(2,1)S(1)}, u32[]{:S(2)}, u32[]{:S(2)}) collective-permute-start(bf16[40,1024]{1,0:T(8,128)(2,1)S(1)} %add_convert_fusion.3), channel_id=1, source_target_pairs={{8,0},{9,1},{10,2},{11,3},{12,4},{13,5},{14,6},{15,7},{0,8},{1,9},... | collective-permute-start | bytes 245768 | tf_op jit(solution)/shard_map/ppermute | solution.py:56
  58.2 6.8 %collective-permute-start.14 = (bf16[40,1024]{1,0:T(8,128)(2,1)S(1)}, bf16[40,1024]{1,0:T(8,128)(2,1)S(1)}, u32[]{:S(2)}, u32[]{:S(2)}) collective-permute-start(bf16[40,1024]{1,0:T(8,128)(2,1)S(1)} %add_convert_fusion.3), channel_id=1, source_target_pairs={{4,0},{5,1},{6,2},{7,3},{0,4},{1,5},{2,6},{3,7},{12,8},{13,9},{14,... | collective-permute-start | bytes 245768 | tf_op jit(solution)/shard_map/ppermute | solution.py:56
  65.1 1.3 %collective-permute-start.17 = (bf16[40,1024]{1,0:T(8,128)(2,1)S(1)}, bf16[40,1024]{1,0:T(8,128)(2,1)S(1)}, u32[]{:S(2)}, u32[]{:S(2)}) collective-permute-start(bf16[40,1024]{1,0:T(8,128)(2,1)S(1)} %get-tuple-element.8), channel_id=1, source_target_pairs={{1,0},{0,1},{3,2},{2,3},{5,4},{4,5},{7,6},{6,7},{9,8},{8,9},{11,10... | collective-permute-start | bytes 245768 | tf_op jit(solution)/shard_map/ppermute | solution.py:56
  68.0 1.5 %collective-permute-start.19 = (f32[40,1024]{1,0:T(8,128)S(1)}, f32[40,1024]{1,0:T(8,128)S(1)}, u32[]{:S(2)}, u32[]{:S(2)}) collective-permute-start(f32[40,1024]{1,0:T(8,128)S(1)} %constant_dynamic-slice_fusion), channel_id=1, source_target_pairs={{1,0},{0,1},{3,2},{2,3},{5,4},{4,5},{7,6},{6,7},{9,8},{8,9},{11,10... | collective-permute-start | bytes 491528 | tf_op jit(solution)/shard_map/ppermute | solution.py:56
  69.5 4.6 %collective-permute-start.20 = (bf16[40,1024]{1,0:T(8,128)(2,1)S(1)}, bf16[40,1024]{1,0:T(8,128)(2,1)S(1)}, u32[]{:S(2)}, u32[]{:S(2)}) collective-permute-start(bf16[40,1024]{1,0:T(8,128)(2,1)S(1)} %add_convert_fusion.1), channel_id=1, source_target_pairs={{2,0},{3,1},{0,2},{1,3},{6,4},{7,5},{4,6},{5,7},{10,8},{11,9},{8,1... | collective-permute-start | bytes 245768 | tf_op jit(solution)/shard_map/ppermute | solution.py:56
  74.1 7.1 %collective-permute-start.23 = (bf16[40,1024]{1,0:T(8,128)(2,1)S(1)}, bf16[40,1024]{1,0:T(8,128)(2,1)S(1)}, u32[]{:S(2)}, u32[]{:S(2)}) collective-permute-start(bf16[40,1024]{1,0:T(8,128)(2,1)S(1)} %add_convert_fusion), channel_id=1, source_target_pairs={{12,0},{13,1},{14,2},{15,3},{8,4},{9,5},{10,6},{11,7},{4,8},{5,9},... | collective-permute-start | bytes 245768 | tf_op jit(solution)/shard_map/ppermute | solution.py:56
  76.3 7.3 %collective-permute-start.22 = (bf16[40,1024]{1,0:T(8,128)(2,1)S(1)}, bf16[40,1024]{1,0:T(8,128)(2,1)S(1)}, u32[]{:S(2)}, u32[]{:S(2)}) collective-permute-start(bf16[40,1024]{1,0:T(8,128)(2,1)S(1)} %add_convert_fusion), channel_id=1, source_target_pairs={{8,0},{9,1},{10,2},{11,3},{12,4},{13,5},{14,6},{15,7},{0,8},{1,9},... | collective-permute-start | bytes 245768 | tf_op jit(solution)/shard_map/ppermute | solution.py:56
  76.3 7.3 %collective-permute-start.21 = (bf16[40,1024]{1,0:T(8,128)(2,1)S(1)}, bf16[40,1024]{1,0:T(8,128)(2,1)S(1)}, u32[]{:S(2)}, u32[]{:S(2)}) collective-permute-start(bf16[40,1024]{1,0:T(8,128)(2,1)S(1)} %add_convert_fusion), channel_id=1, source_target_pairs={{4,0},{5,1},{6,2},{7,3},{0,4},{1,5},{2,6},{3,7},{12,8},{13,9},{14,... | collective-permute-start | bytes 245768 | tf_op jit(solution)/shard_map/ppermute | solution.py:56
  78.7 5.1 %collective-permute-start.18 = (bf16[2,2048]{1,0:T(2,128)(2,1)S(1)}, bf16[2,2048]{1,0:T(2,128)(2,1)S(1)}, u32[]{:S(2)}, u32[]{:S(2)}) collective-permute-start(bf16[2,2048]{1,0:T(2,128)(2,1)S(1)} %convolution_convert_fusion.1), channel_id=1, source_target_pairs={{0,16},{16,0},{1,17},{17,1},{2,18},{18,2},{3,19},{19,3},{4,20},{20... | collective-permute-start | bytes 24584 | tf_op jit(solution)/shard_map/ppermute | solution.py:56
  (7 other events, 75.6 us)

commit v2 on v1

v2 whole, which is shorter than its diff:
```python
import functools
import itertools

import jax
import jax.numpy as jnp
from jax import lax
from jax.experimental import pallas as pl
from jax.experimental.pallas import tpu as pltpu
from jax.sharding import PartitionSpec as P

BF = jnp.bfloat16
F32 = jnp.float32


def contract_rows(left, right):
    return lax.dot_general(left, right, (((0,), (0,)), ((), ())), preferred_element_type=F32)


def contract_cols(left, right):
    return lax.dot_general(left, right, (((1,), (1,)), ((), ())), preferred_element_type=F32)


def dot(left, right):
    return jnp.dot(left, right, preferred_element_type=F32)


def digits(total):
    sizes = []
    rest = total
    if rest % 2 == 0:
        sizes.append(2)
        rest //= 2
    twos = 0
    while rest % 2 == 0:
        rest //= 2
        twos += 1
    sizes += [2] * (twos % 2) + [4] * (twos // 2)
    if rest > 1:
        sizes.append(rest)
    placed, stride = [], 1
    for size in sizes:
        placed.append((stride, size))
        stride *= size
    return placed


def moved(index, stride, size, offset):
    digit = (index // stride) % size
    if size & (size - 1) == 0:
        target = digit ^ offset
    else:
        target = (digit + offset) % size
    return index + (target - digit) * stride


def fetch(values, steps, back=False):
    axes = ("dp", "expert")
    pairs = []
    for here in range(lax.axis_size(axes)):
        there = here
        for stride, size, offset in steps:
            there = moved(there, stride, size, offset)
        pairs.append((here, there) if back else (there, here))
    return lax.ppermute(values, axes, pairs)


def offsets_of(stage):
    return list(itertools.product(*[range(size) for _, size in stage]))


def steps_of(stage, offset):
    return [(*digit, k) for digit, k in zip(stage, offset) if k > 0]


def gather_rows(values, stages, hold_first, hold_second):
    held, blocks, kept = [values], [()], [hold_first(values)]
    for at, stage in enumerate(stages):
        offsets = offsets_of(stage)
        if at == 1:
            held[0] = lax.optimization_barrier(held[0] + kept[0][1])
        if held[0].shape[0] < 8:
            held = [jnp.concatenate(held, axis=0)]
        if at == 1:
            kept.append(hold_second(held[0]))
        if at > 1 and at == len(stages) - 1:
            held[0] = held[0] + kept[1][1]
        held += [fetch(part, steps_of(stage, offset)) for offset in offsets[1:] for part in held]
        blocks = [block + tuple(steps_of(stage, offset)) for offset in offsets for block in blocks]
    return held, blocks, [first for first, _ in kept]


def chunks(total, step):
    return [(at, min(step, total - at)) for at in range(0, total, step)]


def padded(rows):
    return -(-rows // 16) * 16


def stack(ref, low, high, columns=slice(None)):
    rows = low.shape[0]
    space = padded(rows)
    for at, values in ((0, low), (space, high)):
        if space > rows:
            fill = jnp.zeros((space - rows, values.shape[1]), values.dtype)
            values = jnp.concatenate([values, fill], axis=0)
        ref[at : at + space, columns] = values


def own_and_other(size):
    core = lax.rem(lax.axis_index("expert"), 2)
    return tuple(pl.ds(pl.multiple_of(at * size, size), size) for at in (core, 1 - core))


def forward_kernel(local, found_at, capacity, *refs):
    *parts, w_in, w_out, rows_in, col, col_wide, hidden, slope, bend, mine, other, picks = refs
    rows, width = rows_in.shape
    gathered = jnp.concatenate([part[...] for part in parts], axis=0)
    meta = gathered[:, width:].astype(F32)
    me = lax.axis_index("dp").astype(F32)
    slot = meta[:, 1:2] * 128.0 + meta[:, 2:3]
    place = jnp.where(meta[:, 0:1] == me, meta[:, 4:5] * float(capacity) + slot, -1.0)
    place = jnp.where(slot >= 0.0, place, -1.0)
    wanted = lax.broadcasted_iota(jnp.int32, (meta.shape[0], rows), 1).astype(F32)
    onehot = (place == wanted).astype(F32)
    found = contract_rows(onehot.astype(BF), gathered)
    packed_rows = found[:, :width].astype(BF)
    weight = found[:, width + 3 : width + 4]
    rows_in[...] = packed_rows
    picks[...] = jnp.concatenate([onehot[at : at + local] for at in found_at], axis=0)
    col[...] = weight
    col_wide[...] = jnp.broadcast_to(weight, col_wide.shape)
    pre = dot(packed_rows, w_in[...])
    sigm = jax.nn.sigmoid(pre)
    slope[...] = sigm * (1.0 + pre * (1.0 - sigm))
    bend[...] = sigm * (1.0 - sigm) * (2.0 + pre * (1.0 - 2.0 * sigm))
    act = (pre * sigm).astype(BF)
    hidden[...] = act
    at_own, at_other = own_and_other(width // 2)
    other[...] = weight * dot(act, w_out[:, at_other])
    mine[...] = weight * dot(act, w_out[:, at_own])


def backward_kernel(up_own, up_other, col, slope, w_in, w_out, back_hidden, back_pre, mine, other):
    at_own, at_other = own_and_other(up_own.shape[1])
    back = contract_cols(up_own[...], w_out[:, at_own])
    back += contract_cols(up_other[...], w_out[:, at_other])
    back = col[...] * back
    back_hidden[...] = back
    back = (back * slope[...]).astype(BF)
    back_pre[...] = back
    other[...] = contract_cols(back, w_in[at_other, :])
    mine[...] = contract_cols(back, w_in[at_own, :])


def push_kernel(grad_own, grad_other, col, slope, picks, w_in, w_out, second, push, mine, other, *home):
    half = grad_own.shape[1]
    at_own, at_other = own_and_other(half)
    pick = picks[...].astype(BF)
    local = home[0].shape[0]
    for columns, grad in ((slice(0, half), grad_own), (slice(half, 2 * half), grad_other)):
        found = dot(pick, grad[...])
        for k, result in enumerate(home):
            result[:, columns] = found[k * local : (k + 1) * local].astype(BF)
    moved_rows = dot(grad_own[...], w_in[at_own, :]) + dot(grad_other[...], w_in[at_other, :])
    second[...] = moved_rows
    moved_rows = (col[...] * moved_rows * slope[...]).astype(BF)
    push[...] = moved_rows
    other[...] = dot(moved_rows, w_out[:, at_other])
    mine[...] = dot(moved_rows, w_out[:, at_own])


def final_kernel(
    echo_own, echo_other, up_own, up_other, grad_own, grad_other, rows_in, push, hidden, back_pre,
    slope, bend, second, back_hidden, w_out, grad_in, grad_out,
    left_out, right_out, left_in, right_in, made_in, made_out, sem_in, sem_out,
):
    ranges = own_and_other(echo_own.shape[1])
    stack(left_out, push[...], hidden[...])
    for at, up, echo in zip(ranges, (up_own, up_other), (echo_own, echo_other)):
        stack(right_out, up[...], echo[...], at)
    copies = []

    def product(left, right, made, result, sem, step):
        for i, (at, size) in enumerate(chunks(left.shape[1], step)):
            made[at : at + size, :] = contract_rows(left[:, at : at + size], right[...]).astype(BF)
            part = pl.ds(at, size)
            copy = pltpu.make_async_copy(made.at[part], result.at[part], sem.at[i])
            copy.start()
            copies.append(copy)

    product(left_out, right_out, made_out, grad_out, sem_out, 128)
    back = contract_cols(echo_own[...], w_out[:, ranges[0]])
    back += contract_cols(echo_other[...], w_out[:, ranges[1]])
    final_pre = (back * slope[...] + second[...] * back_hidden[...] * bend[...]).astype(BF)
    stack(right_in, back_pre[...], final_pre)
    rows = rows_in[...]
    for at, grad in zip(ranges, (grad_own, grad_other)):
        left_in[0 : grad.shape[0], at] = grad[...]
    if padded(rows.shape[0]) > rows.shape[0]:
        fill = jnp.zeros((padded(rows.shape[0]) - rows.shape[0], rows.shape[1]), BF)
        left_in[rows.shape[0] : padded(rows.shape[0]), :] = fill
        rows = jnp.concatenate([rows, fill], axis=0)
    left_in[rows.shape[0] :, :] = rows
    product(left_in, right_in, made_in, grad_in, sem_in, 256)
    for copy in copies:
        copy.wait()


def run(kernel, shapes, args, scratch=(), flops=0, hbm=False):
    space = pl.ANY if hbm else pltpu.VMEM
    return pl.pallas_call(
        kernel,
        out_shape=[jax.ShapeDtypeStruct(shape, kind) for shape, kind in shapes],
        in_specs=[pl.BlockSpec(memory_space=pltpu.VMEM)] * len(args),
        out_specs=[pl.BlockSpec(memory_space=space)] * len(shapes),
        scratch_shapes=list(scratch),
        compiler_params=pltpu.CompilerParams(vmem_limit_bytes=20 << 20),
        cost_estimate=pl.CostEstimate(flops=flops, bytes_accessed=0, transcendentals=0),
    )(*[pltpu.with_memory_space_constraint(arg, pltpu.VMEM) for arg in args])


def hold(matrix, after):
    def kernel(source, after_ref, held, there, sem):
        del after_ref
        copy = pltpu.make_async_copy(source, held, sem)
        copy.start()
        there[...] = jnp.zeros_like(there)
        copy.wait()

    vmem = pl.BlockSpec(memory_space=pltpu.VMEM)
    return pl.pallas_call(
        kernel,
        out_shape=(pltpu.VMEM(matrix.shape, matrix.dtype), pltpu.VMEM(after.shape, BF)),
        in_specs=[pl.BlockSpec(memory_space=pltpu.HBM), pl.BlockSpec(memory_space=pl.ANY)],
        out_specs=(vmem, vmem),
        scratch_shapes=[pltpu.SemaphoreType.DMA],
        compiler_params=pltpu.CompilerParams(vmem_limit_bytes=1 << 20),
        cost_estimate=pl.CostEstimate(flops=0, bytes_accessed=matrix.size * 4, transcendentals=0),
    )(pltpu.with_memory_space_constraint(matrix, pltpu.HBM), after)


def pack(tokens, combine, routes, capacity_slot):
    local, width = tokens.shape
    shape = (local, width + 128)
    column = lax.broadcasted_iota(jnp.int32, shape, 1) - width
    routes, slots, combine = (
        lax.broadcast_in_dim(values, shape, (0,)) for values in (routes, capacity_slot, combine)
    )
    numbers = jnp.where(column == 4, lax.axis_index("dp"), slots & 127)
    numbers = jnp.where(column == 1, slots >> 7, numbers)
    numbers = jnp.where(column == 0, routes, numbers).astype(BF)
    numbers = jnp.where(column == 3, combine, numbers)
    return jnp.where(column < 0, jnp.pad(tokens, ((0, 0), (0, 128))), numbers)


def shards(tokens, combine, routes, capacity_slot, readout, weight_in, weight_out):
    n_dp = lax.axis_size("dp")
    n_ex = lax.axis_size("expert")
    local, width = tokens.shape
    units = weight_in.shape[2]
    capacity = 5 * local * n_ex // (4 * n_dp)
    rows = n_dp * capacity
    splits = digits(n_ex)
    core, chips = splits[0], splits[1:]

    kept = capacity_slot >= 0
    packed = pack(tokens, combine, routes, capacity_slot)
    first_core = lax.axis_index("expert") % core[1] == 0
    packed, first_core = lax.optimization_barrier((packed, first_core))

    dp_digit = (n_ex, n_dp)
    if n_dp * chips[0][1] <= 4:
        stages = [[dp_digit, chips[0]]] + [[digit] for digit in chips[1:]]
    else:
        stages = [[dp_digit]] + [[digit] for digit in chips]
    stages += [[core]]
    gathered, blocks, (matrix_in, matrix_out) = gather_rows(
        packed,
        stages,
        functools.partial(hold, weight_in[0]),
        functools.partial(hold, weight_out[0]),
    )
    found_at = [blocks.index(((*dp_digit, k),) if k > 0 else ()) * local for k in range(n_dp)]

    half = width // 2
    head_part = jnp.where(first_core, readout[None, :half], readout[None, half:])
    wide, thin, part = (rows, width), (rows, units), (rows, half)
    flops = 4 * rows * width * units

    def swap(values):
        return fetch(values, [(*core, 1)])

    def shared_sum(mine, other):
        total = mine + swap(other)
        for digit in chips:
            own = total.astype(BF)
            parts = [own] + [fetch(own, [(*digit, k)]) for k in range(1, digit[1])]
            total = sum(part.astype(F32) for part in parts)
        return total

    rows_in, col, col_wide, hidden, slope, bend, mine, other, picks = run(
        functools.partial(forward_kernel, local, found_at, capacity),
        [(wide, BF), ((rows, 1), F32), (part, F32), (thin, BF), (thin, F32), (thin, F32),
         (part, F32), (part, F32), ((n_dp * local, rows), F32)],
        (*gathered, matrix_in, matrix_out),
        flops=flops,
    )
    mixed = shared_sum(mine, other)
    rows_part = jnp.where(first_core, rows_in[:, :half], rows_in[:, half:])
    tangent = jnp.tanh(rows_part.astype(F32) + mixed)
    sech_sq = 1.0 - tangent * tangent
    upstream = head_part * sech_sq
    up_own = upstream.astype(BF)
    up_other = swap(up_own)
    back_hidden, back_pre, mine, other = run(
        backward_kernel,
        [(thin, F32), (thin, BF), (part, F32), (part, F32)],
        (up_own, up_other, col, slope, matrix_in, matrix_out),
        flops=flops,
    )
    grad_own = (upstream + shared_sum(mine, other)).astype(BF)
    grad_other = swap(grad_own)
    second, push, mine, other, *home = run(
        push_kernel,
        [(thin, F32), (thin, BF), (part, F32), (part, F32)] + [((local, width), BF)] * n_dp,
        (grad_own, grad_other, col, slope, picks, matrix_in, matrix_out),
        flops=flops,
    )
    total_push = grad_own.astype(F32) + shared_sum(mine, other)
    curve_term = total_push * head_part * (-2.0 * tangent * sech_sq)
    echo_own = (col_wide * curve_term).astype(BF)
    echo_other = swap(echo_own)
    deep = 2 * padded(rows)
    grad_in, grad_out = run(
        final_kernel,
        [((width, units), BF), ((units, width), BF)],
        (echo_own, echo_other, up_own, up_other, grad_own, grad_other, rows_in, push, hidden,
         back_pre, slope, bend, second, back_hidden, matrix_out),
        scratch=[
            pltpu.VMEM((deep, units), BF),
            pltpu.VMEM((deep, width), BF),
            pltpu.VMEM((deep, width), BF),
            pltpu.VMEM((deep, units), BF),
            pltpu.VMEM((width, units), BF),
            pltpu.VMEM((units, width), BF),
            pltpu.SemaphoreType.DMA((len(chunks(width, 256)),)),
            pltpu.SemaphoreType.DMA((len(chunks(units, 128)),)),
        ],
        flops=flops,
        hbm=True,
    )

    picked = home[0].astype(F32)
    for k in range(1, n_dp):
        picked = picked + fetch(home[k], [(*dp_digit, k)], back=True).astype(F32)
    swapped = jnp.concatenate([picked[:, half:], picked[:, :half]], 1)
    picked = jnp.where(first_core, picked, swapped)
    tangent_home = jnp.tanh(tokens.astype(F32))
    dropped = readout[None, :] * (1.0 - tangent_home * tangent_home)
    r2_grad = jnp.where(kept[:, None], picked, dropped).astype(BF)
    return (r2_grad, grad_in[None], grad_out[None])


def solution(mesh):
    placed = (
        P(("dp", "expert"), None),
        P(("dp", "expert")),
        P(("dp", "expert")),
        P(("dp", "expert")),
        P(),
        P("dp", None, "expert"),
        P("dp", "expert", None),
    )
    return jax.shard_map(
        shards,
        mesh=mesh,
        in_specs=placed,
        out_specs=(P(("dp", "expert"), None), P("dp", None, "expert"), P("dp", "expert", None)),
        check_vma=False,
    )
```

time: 92.7 us -> 82.1 us (0.89)
  matrix products: 18.2 us -> 0 us
  Pallas kernels: 0 us -> 14.5 us
  starting transfers between devices: 30.5 us -> 27.1 us
  other arithmetic: 4.31 us -> 2.68 us
    dot_general x12 -> x0, matrix products: 18.2 us -> none  [the longest x7 6.47 us: dot(): return jnp.dot(left, right, preferred_element_type=F32)]
    pallas_call x0 -> x6, Pallas kernels: none -> 14.5 us  [the longest x4 10.5 us: run(): pl.pallas_call(kernel, out_shape=[jax.ShapeDtypeStruct(shape, kind) for s...]
    ppermute x25 -> x29, starting transfers between devices: 30.5 us -> 27.1 us  [fetch(): return lax.ppermute(values, axes, pairs)]
    concatenate x3 -> x1, other arithmetic: 2.16 us -> 0.05 us  [gather_rows(): held = [jnp.concatenate(held, axis=0)]]
    another operation x3 -> x0, other arithmetic: 1.36 us -> none  [shards(): jnp.stack([expert_id.astype(BF), (place // 128).astype(BF), (place % 128)...]
    ppermute x25 -> x29, waiting for transfers between devices: 37.6 us -> 36.7 us  [fetch(): return lax.ppermute(values, axes, pairs)]
    convert_element_type x1 -> x4, other arithmetic: 0.01 us -> 0.95 us  [the longest x1 0.68 us: shards(): r2_grad = jnp.where(kept[:, None], picked, dropped).astype(BF)]
  transfers between devices with their start and end apart: 25 -> 29, of which waited for: 20 -> 19; matrix products, arithmetic and copies ran while one was open for 1% -> 1% of each run, Pallas kernels for 0% -> 5%
where the time goes in v2:
time: 82.1 us; the launch traced here: 81.9 us
  waiting for transfers between devices  36.7 us (45%)
  starting transfers between devices  27.1 us (33%)
  Pallas kernels  14.5 us (18%)
  other arithmetic  2.68 us (3%)
  between operations  0.84 us (1%)
    ppermute x29, waiting for transfers between devices, fetch(): return lax.ppermute(values, axes, pairs)  36.7 us
    ppermute x29, starting transfers between devices, fetch(): return lax.ppermute(values, axes, pairs)  27.1 us
    pallas_call x4, Pallas kernels, run(): pl.pallas_call(kernel, out_shape=[jax.ShapeDtypeStruct(shape, kind) for s...  10.5 us
    pallas_call x2, Pallas kernels, hold(): pl.pallas_call(kernel, out_shape=(pltpu.VMEM(matrix.shape, matrix.dtype),...  4.09 us
  transfers between devices with their start and end apart: 29, of which 19 were waited for; matrix products, arithmetic and copies ran while one was open for 1% of the time, Pallas kernels for 5%

profile of v2, /device:TPU:0, one launch (start us, length us, event | category | flops | bytes accessed | tf_op | source)
XLA Modules:
  0.0 81.9 jit_solution(5438173008869211576)
XLA Ops:
  2.2 4.0 %collective-permute-start.2 = (bf16[2,2176]{1,0:T(2,128)(2,1)S(1)}, bf16[2,2176]{1,0:T(2,128)(2,1)S(1)}, u32[]{:S(2)}, u32[]{:S(2)}) collective-permute-start(bf16[2,2176]{1,0:T(2,128)(2,1)S(1)} %broadcast_select_fusion.1.after_ref), channel_id=1, source_target_pairs={{18,0},{19,1},{16,2},{17,3},{22,4},{23,5},{20,6},{21,7},{26,8},{27... | collective-permute-start | bytes 26120 | tf_op jit(solution)/shard_map/ppermute | solution.py:64
  6.8 2.0 %shard_map.94 = (bf16[2048,896]{1,0:T(8,128)(2,1)S(1)}, bf16[2,2176]{1,0:T(2,128)(2,1)S(1)}) custom-call(bf16[2048,896]{1,0:T(8,128)(2,1)} %bitcast.5, bf16[2,2176]{1,0:T(2,128)(2,1)S(1)} %broadcast_select_fusion.1.after_ref), custom_call_target="tpu_custom_call" | custom-call | bytes 7340032 | tf_op jit(solution)/shard_map/pallas_call | solution.py:232
  10.4 2.7 %collective-permute-start.4 = (bf16[8,2176]{1,0:T(8,128)(2,1)S(1)}, bf16[8,2176]{1,0:T(8,128)(2,1)S(1)}, u32[]{:S(2)}, u32[]{:S(2)}) collective-permute-start(bf16[8,2176]{1,0:T(8,128)(2,1)S(1)} %pad_maximum_fusion.after_ref), channel_id=1, source_target_pairs={{8,0},{9,1},{10,2},{11,3},{12,4},{13,5},{14,6},{15,7},{0,8},{1,9},... | collective-permute-start | bytes 104456 | tf_op jit(solution)/shard_map/ppermute | solution.py:64
  13.0 1.6 %collective-permute-start.3 = (bf16[8,2176]{1,0:T(8,128)(2,1)S(1)}, bf16[8,2176]{1,0:T(8,128)(2,1)S(1)}, u32[]{:S(2)}, u32[]{:S(2)}) collective-permute-start(bf16[8,2176]{1,0:T(8,128)(2,1)S(1)} %pad_maximum_fusion.after_ref), channel_id=1, source_target_pairs={{4,0},{5,1},{6,2},{7,3},{0,4},{1,5},{2,6},{3,7},{12,8},{13,9},{14,... | collective-permute-start | bytes 104456 | tf_op jit(solution)/shard_map/ppermute | solution.py:64
  14.8 2.0 %shard_map.95 = (bf16[896,2048]{1,0:T(8,128)(2,1)S(1)}, bf16[8,2176]{1,0:T(8,128)(2,1)S(1)}) custom-call(bf16[896,2048]{1,0:T(8,128)(2,1)} %bitcast.4, bf16[8,2176]{1,0:T(8,128)(2,1)S(1)} %pad_maximum_fusion.after_ref), custom_call_target="tpu_custom_call" | custom-call | bytes 7340032 | tf_op jit(solution)/shard_map/pallas_call | solution.py:232
  17.6 2.7 %collective-permute-done.5.refs_3_ = bf16[8,2176]{1,0:T(8,128)(2,1)S(1)} collective-permute-done((bf16[8,2176]{1,0:T(8,128)(2,1)S(1)}, bf16[8,2176]{1,0:T(8,128)(2,1)S(1)}, u32[]{:S(2)}, u32[]{:S(2)}) %collective-permute-start.5) | collective-permute-done | bytes 34848 | tf_op jit(solution)/shard_map/ppermute | solution.py:64
  21.5 2.0 %shard_map.96 = (bf16[40,2048]{1,0:T(8,128)(2,1)S(1)}, f32[40,1]{1,0:T(8,128)S(1)}, f32[40,1024]{1,0:T(8,128)S(1)}, bf16[40,896]{1,0:T(8,128)(2,1)S(1)}, f32[40,...) custom-call(bf16[8,2176]{1,0:T(8,128)(2,1)S(1)} %fusion.9.refs_0_, ...), custom_call_target="tpu_custom_call" | custom-call | flops 293601280 | tf_op jit(solution)/shard_map/pallas_call | solution.py:212
  25.6 4.0 %collective-permute-done.11 = bf16[40,1024]{1,0:T(8,128)(2,1)S(1)} collective-permute-done((bf16[40,1024]{1,0:T(8,128)(2,1)S(1)}, bf16[40,1024]{1,0:T(8,128)(2,1)S(1)}, u32[]{:S(2)}, u32[]{:S(2)}) %collective-permute-start.11) | collective-permute-done | bytes 81952 | tf_op jit(solution)/shard_map/ppermute | solution.py:64
  30.8 3.2 %collective-permute-start.12 = (bf16[40,1024]{1,0:T(8,128)(2,1)S(1)}, bf16[40,1024]{1,0:T(8,128)(2,1)S(1)}, u32[]{:S(2)}, u32[]{:S(2)}) collective-permute-start(bf16[40,1024]{1,0:T(8,128)(2,1)S(1)} %add_convert_fusion.5), channel_id=1, source_target_pairs={{4,0},{5,1},{6,2},{7,3},{0,4},{1,5},{2,6},{3,7},{12,8},{13,9},{14,... | collective-permute-start | bytes 245768 | tf_op jit(solution)/shard_map/ppermute | solution.py:64
  34.1 2.9 %collective-permute-done.14 = bf16[40,1024]{1,0:T(8,128)(2,1)S(1)} collective-permute-done((bf16[40,1024]{1,0:T(8,128)(2,1)S(1)}, bf16[40,1024]{1,0:T(8,128)(2,1)S(1)}, u32[]{:S(2)}, u32[]{:S(2)}) %collective-permute-start.14) | collective-permute-done | bytes 81952 | tf_op jit(solution)/shard_map/ppermute | solution.py:64
  37.0 1.7 %collective-permute-done.13 = bf16[40,1024]{1,0:T(8,128)(2,1)S(1)} collective-permute-done((bf16[40,1024]{1,0:T(8,128)(2,1)S(1)}, bf16[40,1024]{1,0:T(8,128)(2,1)S(1)}, u32[]{:S(2)}, u32[]{:S(2)}) %collective-permute-start.13) | collective-permute-done | bytes 81952 | tf_op jit(solution)/shard_map/ppermute | solution.py:64
  40.1 2.4 %shard_map.97 = (f32[40,896]{1,0:T(8,128)S(1)}, bf16[40,896]{1,0:T(8,128)(2,1)S(1)}, f32[40,1024]{1,0:T(8,128)S(1)}, f32[40,1024]{1,0:T(8,128)S(1)}) custom-call(bf16[40,1024]{1,0:T(8,128)(2,1)S(1)} %get-tuple-element.57.up_own, bf16[40,1024]{1,0:T(8,128)(2,1)S(1)} %collective-permute-done.15.up_other, f32[40,1]{1,0:T(8,128)S(1)} %get-tuple-element.39.col, ...), custom_call_target="tpu_custom_call" | custom-call | flops 293601280 | tf_op jit(solution)/shard_map/pallas_call | solution.py:212
  44.6 4.0 %collective-permute-done.17 = bf16[40,1024]{1,0:T(8,128)(2,1)S(1)} collective-permute-done((bf16[40,1024]{1,0:T(8,128)(2,1)S(1)}, bf16[40,1024]{1,0:T(8,128)(2,1)S(1)}, u32[]{:S(2)}, u32[]{:S(2)}) %collective-permute-start.17) | collective-permute-done | bytes 81952 | tf_op jit(solution)/shard_map/ppermute | solution.py:64
  50.0 3.0 %collective-permute-start.18 = (bf16[40,1024]{1,0:T(8,128)(2,1)S(1)}, bf16[40,1024]{1,0:T(8,128)(2,1)S(1)}, u32[]{:S(2)}, u32[]{:S(2)}) collective-permute-start(bf16[40,1024]{1,0:T(8,128)(2,1)S(1)} %add_convert_fusion.3), channel_id=1, source_target_pairs={{4,0},{5,1},{6,2},{7,3},{0,4},{1,5},{2,6},{3,7},{12,8},{13,9},{14,... | collective-permute-start | bytes 245768 | tf_op jit(solution)/shard_map/ppermute | solution.py:64
  53.0 2.9 %collective-permute-done.20 = bf16[40,1024]{1,0:T(8,128)(2,1)S(1)} collective-permute-done((bf16[40,1024]{1,0:T(8,128)(2,1)S(1)}, bf16[40,1024]{1,0:T(8,128)(2,1)S(1)}, u32[]{:S(2)}, u32[]{:S(2)}) %collective-permute-start.20) | collective-permute-done | bytes 81952 | tf_op jit(solution)/shard_map/ppermute | solution.py:64
  55.9 1.7 %collective-permute-done.19 = bf16[40,1024]{1,0:T(8,128)(2,1)S(1)} collective-permute-done((bf16[40,1024]{1,0:T(8,128)(2,1)S(1)}, bf16[40,1024]{1,0:T(8,128)(2,1)S(1)}, u32[]{:S(2)}, u32[]{:S(2)}) %collective-permute-start.19) | collective-permute-done | bytes 81952 | tf_op jit(solution)/shard_map/ppermute | solution.py:64
  60.7 1.5 %collective-permute-start.22 = (bf16[2,2048]{1,0:T(2,128)(2,1)S(1)}, bf16[2,2048]{1,0:T(2,128)(2,1)S(1)}, u32[]{:S(2)}, u32[]{:S(2)}) collective-permute-start(bf16[2,2048]{1,0:T(2,128)(2,1)S(1)} %get-tuple-element.45), channel_id=1, source_target_pairs={{0,16},{1,17},{2,18},{3,19},{4,20},{5,21},{6,22},{7,23},{8,24},{9,... | collective-permute-start | bytes 24584 | tf_op jit(solution)/shard_map/ppermute | solution.py:64
  62.8 1.6 %collective-permute-done.22 = bf16[2,2048]{1,0:T(2,128)(2,1)S(1)} collective-permute-done((bf16[2,2048]{1,0:T(2,128)(2,1)S(1)}, bf16[2,2048]{1,0:T(2,128)(2,1)S(1)}, u32[]{:S(2)}, u32[]{:S(2)}) %collective-permute-start.22) | collective-permute-done | bytes 8224 | tf_op jit(solution)/shard_map/ppermute | solution.py:64
  64.4 2.4 %collective-permute-done.24 = bf16[40,1024]{1,0:T(8,128)(2,1)S(1)} collective-permute-done((bf16[40,1024]{1,0:T(8,128)(2,1)S(1)}, bf16[40,1024]{1,0:T(8,128)(2,1)S(1)}, u32[]{:S(2)}, u32[]{:S(2)}) %collective-permute-start.24) | collective-permute-done | bytes 81952 | tf_op jit(solution)/shard_map/ppermute | solution.py:64
  66.8 2.3 %collective-permute-start.27 = (bf16[40,1024]{1,0:T(8,128)(2,1)S(1)}, bf16[40,1024]{1,0:T(8,128)(2,1)S(1)}, u32[]{:S(2)}, u32[]{:S(2)}) collective-permute-start(bf16[40,1024]{1,0:T(8,128)(2,1)S(1)} %add_convert_fusion), channel_id=1, source_target_pairs={{12,0},{13,1},{14,2},{15,3},{8,4},{9,5},{10,6},{11,7},{4,8},{5,9},... | collective-permute-start | bytes 245768 | tf_op jit(solution)/shard_map/ppermute | solution.py:64
  69.1 2.2 %collective-permute-start.25 = (bf16[40,1024]{1,0:T(8,128)(2,1)S(1)}, bf16[40,1024]{1,0:T(8,128)(2,1)S(1)}, u32[]{:S(2)}, u32[]{:S(2)}) collective-permute-start(bf16[40,1024]{1,0:T(8,128)(2,1)S(1)} %add_convert_fusion), channel_id=1, source_target_pairs={{4,0},{5,1},{6,2},{7,3},{0,4},{1,5},{2,6},{3,7},{12,8},{13,9},{14,... | collective-permute-start | bytes 245768 | tf_op jit(solution)/shard_map/ppermute | solution.py:64
  71.3 2.6 %collective-permute-done.27 = bf16[40,1024]{1,0:T(8,128)(2,1)S(1)} collective-permute-done((bf16[40,1024]{1,0:T(8,128)(2,1)S(1)}, bf16[40,1024]{1,0:T(8,128)(2,1)S(1)}, u32[]{:S(2)}, u32[]{:S(2)}) %collective-permute-start.27) | collective-permute-done | bytes 81952 | tf_op jit(solution)/shard_map/ppermute | solution.py:64
  73.9 1.9 %collective-permute-done.26 = bf16[40,1024]{1,0:T(8,128)(2,1)S(1)} collective-permute-done((bf16[40,1024]{1,0:T(8,128)(2,1)S(1)}, bf16[40,1024]{1,0:T(8,128)(2,1)S(1)}, u32[]{:S(2)}, u32[]{:S(2)}) %collective-permute-start.26) | collective-permute-done | bytes 81952 | tf_op jit(solution)/shard_map/ppermute | solution.py:64
  77.3 4.5 %shard_map.99 = (bf16[2048,896]{1,0:T(8,128)(2,1)}, bf16[896,2048]{1,0:T(8,128)(2,1)}) custom-call(bf16[40,1024]{1,0:T(8,128)(2,1)S(1)} %multiply_convert_fusion.echo_own, bf16[40,1024]{1,0:T(8,128)(2,1)S(1)} %collective-permute-done.28.echo_other, bf16[40,1024]{1,0:T(8,128)(2,1)S(1)} %get-tuple-element.57.up_own, ...), custom_call_target="tpu_custom_call" | custom-call | flops 293601280 | tf_op jit(solution)/shard_map/pallas_call | solution.py:212
  (68 shorter events, 19.1 us)
Async XLA Ops:
  2.2 6.7 %collective-permute-start.2 = (bf16[2,2176]{1,0:T(2,128)(2,1)S(1)}, bf16[2,2176]{1,0:T(2,128)(2,1)S(1)}, u32[]{:S(2)}, u32[]{:S(2)}) collective-permute-start(bf16[2,2176]{1,0:T(2,128)(2,1)S(1)} %broadcast_select_fusion.1.after_ref), channel_id=1, source_target_pairs={{18,0},{19,1},{16,2},{17,3},{22,4},{23,5},{20,6},{21,7},{26,8},{27... | collective-permute-start | bytes 26120 | tf_op jit(solution)/shard_map/ppermute | solution.py:64
  6.1 3.7 %collective-permute-start.1 = (bf16[2,2176]{1,0:T(2,128)(2,1)S(1)}, bf16[2,2176]{1,0:T(2,128)(2,1)S(1)}, u32[]{:S(2)}, u32[]{:S(2)}) collective-permute-start(bf16[2,2176]{1,0:T(2,128)(2,1)S(1)} %broadcast_select_fusion.1.after_ref), channel_id=1, source_target_pairs={{16,0},{17,1},{18,2},{19,3},{20,4},{21,5},{22,6},{23,7},{24,8},{25... | collective-permute-start | bytes 26120 | tf_op jit(solution)/shard_map/ppermute | solution.py:64
  6.6 3.7 %collective-permute-start = (bf16[2,2176]{1,0:T(2,128)(2,1)S(1)}, bf16[2,2176]{1,0:T(2,128)(2,1)S(1)}, u32[]{:S(2)}, u32[]{:S(2)}) collective-permute-start(bf16[2,2176]{1,0:T(2,128)(2,1)S(1)} %broadcast_select_fusion.1.after_ref), channel_id=1, source_target_pairs={{2,0},{3,1},{0,2},{1,3},{6,4},{7,5},{4,6},{5,7},{10,8},{11,9},{8,1... | collective-permute-start | bytes 26120 | tf_op jit(solution)/shard_map/ppermute | solution.py:64
  10.4 6.6 %collective-permute-start.4 = (bf16[8,2176]{1,0:T(8,128)(2,1)S(1)}, bf16[8,2176]{1,0:T(8,128)(2,1)S(1)}, u32[]{:S(2)}, u32[]{:S(2)}) collective-permute-start(bf16[8,2176]{1,0:T(8,128)(2,1)S(1)} %pad_maximum_fusion.after_ref), channel_id=1, source_target_pairs={{8,0},{9,1},{10,2},{11,3},{12,4},{13,5},{14,6},{15,7},{0,8},{1,9},... | collective-permute-start | bytes 104456 | tf_op jit(solution)/shard_map/ppermute | solution.py:64
  13.0 4.5 %collective-permute-start.3 = (bf16[8,2176]{1,0:T(8,128)(2,1)S(1)}, bf16[8,2176]{1,0:T(8,128)(2,1)S(1)}, u32[]{:S(2)}, u32[]{:S(2)}) collective-permute-start(bf16[8,2176]{1,0:T(8,128)(2,1)S(1)} %pad_maximum_fusion.after_ref), channel_id=1, source_target_pairs={{4,0},{5,1},{6,2},{7,3},{0,4},{1,5},{2,6},{3,7},{12,8},{13,9},{14,... | collective-permute-start | bytes 104456 | tf_op jit(solution)/shard_map/ppermute | solution.py:64
  14.6 5.7 %collective-permute-start.5 = (bf16[8,2176]{1,0:T(8,128)(2,1)S(1)}, bf16[8,2176]{1,0:T(8,128)(2,1)S(1)}, u32[]{:S(2)}, u32[]{:S(2)}) collective-permute-start(bf16[8,2176]{1,0:T(8,128)(2,1)S(1)} %pad_maximum_fusion.after_ref), channel_id=1, source_target_pairs={{12,0},{13,1},{14,2},{15,3},{8,4},{9,5},{10,6},{11,7},{4,8},{5,9},... | collective-permute-start | bytes 104456 | tf_op jit(solution)/shard_map/ppermute | solution.py:64
  16.9 3.4 %collective-permute-start.6 = (bf16[8,2176]{1,0:T(8,128)(2,1)S(1)}, bf16[8,2176]{1,0:T(8,128)(2,1)S(1)}, u32[]{:S(2)}, u32[]{:S(2)}) collective-permute-start(bf16[8,2176]{1,0:T(8,128)(2,1)S(1)} %fusion.9.refs_0_), channel_id=1, source_target_pairs={{1,0},{0,1},{3,2},{2,3},{5,4},{4,5},{7,6},{6,7},{9,8},{8,9},{11,10... | collective-permute-start | bytes 104456 | tf_op jit(solution)/shard_map/ppermute | solution.py:64
  17.0 3.3 %collective-permute-start.8 = (bf16[8,2176]{1,0:T(8,128)(2,1)S(1)}, bf16[8,2176]{1,0:T(8,128)(2,1)S(1)}, u32[]{:S(2)}, u32[]{:S(2)}) collective-permute-start(bf16[8,2176]{1,0:T(8,128)(2,1)S(1)} %collective-permute-done.4.refs_2_), channel_id=1, source_target_pairs={{1,0},{0,1},{3,2},{2,3},{5,4},{4,5},{7,6},{6,7},{9,8},{8,9},{11,10... | collective-permute-start | bytes 104456 | tf_op jit(solution)/shard_map/ppermute | solution.py:64
  17.5 2.8 %collective-permute-start.7 = (bf16[8,2176]{1,0:T(8,128)(2,1)S(1)}, bf16[8,2176]{1,0:T(8,128)(2,1)S(1)}, u32[]{:S(2)}, u32[]{:S(2)}) collective-permute-start(bf16[8,2176]{1,0:T(8,128)(2,1)S(1)} %collective-permute-done.3.refs_1_), channel_id=1, source_target_pairs={{1,0},{0,1},{3,2},{2,3},{5,4},{4,5},{7,6},{6,7},{9,8},{8,9},{11,10... | collective-permute-start | bytes 104456 | tf_op jit(solution)/shard_map/ppermute | solution.py:64
  23.5 1.5 %collective-permute-start.10 = (f32[40,1024]{1,0:T(8,128)S(1)}, f32[40,1024]{1,0:T(8,128)S(1)}, u32[]{:S(2)}, u32[]{:S(2)}) collective-permute-start(f32[40,1024]{1,0:T(8,128)S(1)} %get-tuple-element.38), channel_id=1, source_target_pairs={{1,0},{0,1},{3,2},{2,3},{5,4},{4,5},{7,6},{6,7},{9,8},{8,9},{11,10... | collective-permute-start | bytes 491528 | tf_op jit(solution)/shard_map/ppermute | solution.py:64
  25.0 4.6 %collective-permute-start.11 = (bf16[40,1024]{1,0:T(8,128)(2,1)S(1)}, bf16[40,1024]{1,0:T(8,128)(2,1)S(1)}, u32[]{:S(2)}, u32[]{:S(2)}) collective-permute-start(bf16[40,1024]{1,0:T(8,128)(2,1)S(1)} %add_convert_fusion.6), channel_id=1, source_target_pairs={{2,0},{3,1},{0,2},{1,3},{6,4},{7,5},{4,6},{5,7},{10,8},{11,9},{8,1... | collective-permute-start | bytes 245768 | tf_op jit(solution)/shard_map/ppermute | solution.py:64
  29.6 7.4 %collective-permute-start.14 = (bf16[40,1024]{1,0:T(8,128)(2,1)S(1)}, bf16[40,1024]{1,0:T(8,128)(2,1)S(1)}, u32[]{:S(2)}, u32[]{:S(2)}) collective-permute-start(bf16[40,1024]{1,0:T(8,128)(2,1)S(1)} %add_convert_fusion.5), channel_id=1, source_target_pairs={{12,0},{13,1},{14,2},{15,3},{8,4},{9,5},{10,6},{11,7},{4,8},{5,9},... | collective-permute-start | bytes 245768 | tf_op jit(solution)/shard_map/ppermute | solution.py:64
  30.8 7.9 %collective-permute-start.13 = (bf16[40,1024]{1,0:T(8,128)(2,1)S(1)}, bf16[40,1024]{1,0:T(8,128)(2,1)S(1)}, u32[]{:S(2)}, u32[]{:S(2)}) collective-permute-start(bf16[40,1024]{1,0:T(8,128)(2,1)S(1)} %add_convert_fusion.5), channel_id=1, source_target_pairs={{8,0},{9,1},{10,2},{11,3},{12,4},{13,5},{14,6},{15,7},{0,8},{1,9},... | collective-permute-start | bytes 245768 | tf_op jit(solution)/shard_map/ppermute | solution.py:64
  30.8 7.9 %collective-permute-start.12 = (bf16[40,1024]{1,0:T(8,128)(2,1)S(1)}, bf16[40,1024]{1,0:T(8,128)(2,1)S(1)}, u32[]{:S(2)}, u32[]{:S(2)}) collective-permute-start(bf16[40,1024]{1,0:T(8,128)(2,1)S(1)} %add_convert_fusion.5), channel_id=1, source_target_pairs={{4,0},{5,1},{6,2},{7,3},{0,4},{1,5},{2,6},{3,7},{12,8},{13,9},{14,... | collective-permute-start | bytes 245768 | tf_op jit(solution)/shard_map/ppermute | solution.py:64
  44.0 4.6 %collective-permute-start.17 = (bf16[40,1024]{1,0:T(8,128)(2,1)S(1)}, bf16[40,1024]{1,0:T(8,128)(2,1)S(1)}, u32[]{:S(2)}, u32[]{:S(2)}) collective-permute-start(bf16[40,1024]{1,0:T(8,128)(2,1)S(1)} %add_convert_fusion.4), channel_id=1, source_target_pairs={{2,0},{3,1},{0,2},{1,3},{6,4},{7,5},{4,6},{5,7},{10,8},{11,9},{8,1... | collective-permute-start | bytes 245768 | tf_op jit(solution)/shard_map/ppermute | solution.py:64
  48.6 7.4 %collective-permute-start.20 = (bf16[40,1024]{1,0:T(8,128)(2,1)S(1)}, bf16[40,1024]{1,0:T(8,128)(2,1)S(1)}, u32[]{:S(2)}, u32[]{:S(2)}) collective-permute-start(bf16[40,1024]{1,0:T(8,128)(2,1)S(1)} %add_convert_fusion.3), channel_id=1, source_target_pairs={{12,0},{13,1},{14,2},{15,3},{8,4},{9,5},{10,6},{11,7},{4,8},{5,9},... | collective-permute-start | bytes 245768 | tf_op jit(solution)/shard_map/ppermute | solution.py:64
  50.0 7.6 %collective-permute-start.19 = (bf16[40,1024]{1,0:T(8,128)(2,1)S(1)}, bf16[40,1024]{1,0:T(8,128)(2,1)S(1)}, u32[]{:S(2)}, u32[]{:S(2)}) collective-permute-start(bf16[40,1024]{1,0:T(8,128)(2,1)S(1)} %add_convert_fusion.3), channel_id=1, source_target_pairs={{8,0},{9,1},{10,2},{11,3},{12,4},{13,5},{14,6},{15,7},{0,8},{1,9},... | collective-permute-start | bytes 245768 | tf_op jit(solution)/shard_map/ppermute | solution.py:64
  50.0 7.6 %collective-permute-start.18 = (bf16[40,1024]{1,0:T(8,128)(2,1)S(1)}, bf16[40,1024]{1,0:T(8,128)(2,1)S(1)}, u32[]{:S(2)}, u32[]{:S(2)}) collective-permute-start(bf16[40,1024]{1,0:T(8,128)(2,1)S(1)} %add_convert_fusion.3), channel_id=1, source_target_pairs={{4,0},{5,1},{6,2},{7,3},{0,4},{1,5},{2,6},{3,7},{12,8},{13,9},{14,... | collective-permute-start | bytes 245768 | tf_op jit(solution)/shard_map/ppermute | solution.py:64
  60.6 1.7 %collective-permute-start.23 = (f32[40,1024]{1,0:T(8,128)S(1)}, f32[40,1024]{1,0:T(8,128)S(1)}, u32[]{:S(2)}, u32[]{:S(2)}) collective-permute-start(f32[40,1024]{1,0:T(8,128)S(1)} %get-tuple-element.48), channel_id=1, source_target_pairs={{1,0},{0,1},{3,2},{2,3},{5,4},{4,5},{7,6},{6,7},{9,8},{8,9},{11,10... | collective-permute-start | bytes 491528 | tf_op jit(solution)/shard_map/ppermute | solution.py:64
  60.7 3.7 %collective-permute-start.22 = (bf16[2,2048]{1,0:T(2,128)(2,1)S(1)}, bf16[2,2048]{1,0:T(2,128)(2,1)S(1)}, u32[]{:S(2)}, u32[]{:S(2)}) collective-permute-start(bf16[2,2048]{1,0:T(2,128)(2,1)S(1)} %get-tuple-element.45), channel_id=1, source_target_pairs={{0,16},{1,17},{2,18},{3,19},{4,20},{5,21},{6,22},{7,23},{8,24},{9,... | collective-permute-start | bytes 24584 | tf_op jit(solution)/shard_map/ppermute | solution.py:64
  62.3 4.5 %collective-permute-start.24 = (bf16[40,1024]{1,0:T(8,128)(2,1)S(1)}, bf16[40,1024]{1,0:T(8,128)(2,1)S(1)}, u32[]{:S(2)}, u32[]{:S(2)}) collective-permute-start(bf16[40,1024]{1,0:T(8,128)(2,1)S(1)} %add_convert_fusion.1), channel_id=1, source_target_pairs={{2,0},{3,1},{0,2},{1,3},{6,4},{7,5},{4,6},{5,7},{10,8},{11,9},{8,1... | collective-permute-start | bytes 245768 | tf_op jit(solution)/shard_map/ppermute | solution.py:64
  66.8 7.1 %collective-permute-start.27 = (bf16[40,1024]{1,0:T(8,128)(2,1)S(1)}, bf16[40,1024]{1,0:T(8,128)(2,1)S(1)}, u32[]{:S(2)}, u32[]{:S(2)}) collective-permute-start(bf16[40,1024]{1,0:T(8,128)(2,1)S(1)} %add_convert_fusion), channel_id=1, source_target_pairs={{12,0},{13,1},{14,2},{15,3},{8,4},{9,5},{10,6},{11,7},{4,8},{5,9},... | collective-permute-start | bytes 245768 | tf_op jit(solution)/shard_map/ppermute | solution.py:64
  69.1 6.8 %collective-permute-start.26 = (bf16[40,1024]{1,0:T(8,128)(2,1)S(1)}, bf16[40,1024]{1,0:T(8,128)(2,1)S(1)}, u32[]{:S(2)}, u32[]{:S(2)}) collective-permute-start(bf16[40,1024]{1,0:T(8,128)(2,1)S(1)} %add_convert_fusion), channel_id=1, source_target_pairs={{8,0},{9,1},{10,2},{11,3},{12,4},{13,5},{14,6},{15,7},{0,8},{1,9},... | collective-permute-start | bytes 245768 | tf_op jit(solution)/shard_map/ppermute | solution.py:64
  69.1 6.8 %collective-permute-start.25 = (bf16[40,1024]{1,0:T(8,128)(2,1)S(1)}, bf16[40,1024]{1,0:T(8,128)(2,1)S(1)}, u32[]{:S(2)}, u32[]{:S(2)}) collective-permute-start(bf16[40,1024]{1,0:T(8,128)(2,1)S(1)} %add_convert_fusion), channel_id=1, source_target_pairs={{4,0},{5,1},{6,2},{7,3},{0,4},{1,5},{2,6},{3,7},{12,8},{13,9},{14,... | collective-permute-start | bytes 245768 | tf_op jit(solution)/shard_map/ppermute | solution.py:64
  (8 other events, 37.9 us)

commit v3 on v2

v3 whole, which is shorter than its diff:
```python
import functools
import itertools

import jax
import jax.numpy as jnp
from jax import lax
from jax.experimental import pallas as pl
from jax.experimental.pallas import tpu as pltpu
from jax.sharding import PartitionSpec as P

BF = jnp.bfloat16
F32 = jnp.float32


def contract_rows(left, right):
    return lax.dot_general(left, right, (((0,), (0,)), ((), ())), preferred_element_type=F32)


def contract_cols(left, right):
    return lax.dot_general(left, right, (((1,), (1,)), ((), ())), preferred_element_type=F32)


def dot(left, right):
    return jnp.dot(left, right, preferred_element_type=F32)


def digits(total):
    placed, stride = [], 1
    while stride < total:
        size = 2 if total // stride % 2 == 0 else total // stride
        placed.append((stride, size))
        stride *= size
    return placed


def pairs(some):
    return [some[at : at + 2] for at in range(0, len(some), 2)]


def moved(index, stride, size, offset):
    digit = (index // stride) % size
    if size & (size - 1) == 0:
        target = digit ^ offset
    else:
        target = (digit + offset) % size
    return index + (target - digit) * stride


def fetch(values, steps, back=False):
    axes = ("dp", "expert")
    pairs = []
    for here in range(lax.axis_size(axes)):
        there = here
        for stride, size, offset in steps:
            there = moved(there, stride, size, offset)
        pairs.append((here, there) if back else (there, here))
    return lax.ppermute(values, axes, pairs)


def offsets_of(stage):
    return list(itertools.product(*[range(size) for _, size in stage]))


def steps_of(stage, offset):
    return [(*digit, k) for digit, k in zip(stage, offset) if k > 0]


def gather_rows(values, stages, hold_first, hold_second):
    held, blocks, kept = [values], [()], [hold_first(values)]
    for at, stage in enumerate(stages):
        offsets = offsets_of(stage)
        if at == 1:
            held[0] = lax.optimization_barrier(held[0] + kept[0][1])
        if held[0].shape[0] < 8:
            held = [jnp.concatenate(held, axis=0)]
        if at == 1:
            kept.append(hold_second(held[0]))
        if at > 1 and at == len(stages) - 1:
            held[0] = held[0] + kept[1][1]
        held += [fetch(part, steps_of(stage, offset)) for offset in offsets[1:] for part in held]
        blocks = [block + tuple(steps_of(stage, offset)) for offset in offsets for block in blocks]
    return held, blocks, [first for first, _ in kept]


def chunks(total, step):
    return [(at, min(step, total - at)) for at in range(0, total, step)]


def padded(rows):
    return -(-rows // 16) * 16


def stack(ref, low, high, columns=slice(None)):
    rows = low.shape[0]
    space = padded(rows)
    for at, values in ((0, low), (space, high)):
        if space > rows:
            fill = jnp.zeros((space - rows, values.shape[1]), values.dtype)
            values = jnp.concatenate([values, fill], axis=0)
        ref[at : at + space, columns] = values


def own_and_other(size):
    core = lax.rem(lax.axis_index("expert"), 2)
    return tuple(pl.ds(pl.multiple_of(at * size, size), size) for at in (core, 1 - core))


def forward_kernel(local, found_at, *refs):
    *parts, w_in, w_out, rows_in, col, hidden, pre_act, other, picks = refs
    rows, width = rows_in.shape
    gathered = jnp.concatenate([part[...] for part in parts], axis=0)
    meta = gathered[:, width:].astype(F32)
    me = lax.axis_index("dp").astype(F32)
    slot = meta[:, 1:2] * 128.0 + meta[:, 2:3]
    capacity = float(rows // lax.axis_size("dp"))
    place = jnp.where(meta[:, 0:1] == me, meta[:, 4:5] * capacity + slot, -1.0)
    place = jnp.where(slot >= 0.0, place, -1.0)
    wanted = lax.broadcasted_iota(jnp.int32, (meta.shape[0], rows), 1).astype(F32)
    onehot = (place == wanted).astype(F32)
    found = contract_rows(onehot.astype(BF), gathered)
    packed_rows = found[:, :width].astype(BF)
    weight = found[:, width + 3 : width + 4]
    rows_in[...] = packed_rows
    picks[...] = jnp.concatenate([onehot[at : at + local] for at in found_at], axis=0)
    col[...] = weight
    pre = dot(packed_rows, w_in[...])
    pre_act[...] = pre
    act = (pre * jax.nn.sigmoid(pre)).astype(BF)
    hidden[...] = act
    other[...] = (weight * dot(act, w_out[:, own_and_other(width // 2)[1]])).astype(BF)


def mix_kernel(hidden, pre_act, col, w_out, mine, slope, bend, col_wide):
    mine[...] = col[...] * dot(hidden[...], w_out[:, own_and_other(mine.shape[1])[0]])
    pre = pre_act[...]
    sigm = jax.nn.sigmoid(pre)
    slope[...] = sigm * (1.0 + pre * (1.0 - sigm))
    bend[...] = sigm * (1.0 - sigm) * (2.0 + pre * (1.0 - 2.0 * sigm))
    col_wide[...] = jnp.broadcast_to(col[...], col_wide.shape)


def back_own_kernel(up_own, w_out, back_own):
    back_own[...] = contract_cols(up_own[...], w_out[:, own_and_other(up_own.shape[1])[0]])


def backward_kernel(back_own, up_other, col, slope, w_in, w_out, back_hidden, back_pre, other):
    at_other = own_and_other(up_other.shape[1])[1]
    back = col[...] * (back_own[...] + contract_cols(up_other[...], w_out[:, at_other]))
    back_hidden[...] = back
    back = (back * slope[...]).astype(BF)
    back_pre[...] = back
    other[...] = contract_cols(back, w_in[at_other, :]).astype(BF)


def grad_kernel(back_pre, w_in, mine):
    mine[...] = contract_cols(back_pre[...], w_in[own_and_other(mine.shape[1])[0], :])


def second_own_kernel(grad_own, w_in, second_own):
    second_own[...] = dot(grad_own[...], w_in[own_and_other(grad_own.shape[1])[0], :])


def push_kernel(second_own, grad_other, col, slope, w_in, w_out, second, push, other):
    at_other = own_and_other(grad_other.shape[1])[1]
    moved_rows = second_own[...] + dot(grad_other[...], w_in[at_other, :])
    second[...] = moved_rows
    moved_rows = (col[...] * moved_rows * slope[...]).astype(BF)
    push[...] = moved_rows
    other[...] = dot(moved_rows, w_out[:, at_other]).astype(BF)


def pull_kernel(
    push, hidden, grad_own, grad_other, rows_in, picks, w_out, mine, left_out, left_in, *home
):
    half = mine.shape[1]
    mine[...] = dot(push[...], w_out[:, own_and_other(half)[0]])
    pick = picks[...].astype(BF)
    local = home[0].shape[0]
    for columns, grad in ((slice(0, half), grad_own), (slice(half, 2 * half), grad_other)):
        found = dot(pick, grad[...])
        for k, result in enumerate(home):
            result[:, columns] = found[k * local : (k + 1) * local].astype(BF)
    stack(left_out, push[...], hidden[...])
    for at, grad in zip(own_and_other(half), (grad_own, grad_other)):
        stack(left_in, grad[...], rows_in[:, at], at)


def product(left, right, made, result, columns, sem, step):
    copies = []
    for i, (at, size) in enumerate(chunks(left.shape[1], step)):
        made[at : at + size, :] = contract_rows(left[:, at : at + size], right[...]).astype(BF)
        target = result.at[pl.ds(at, size), columns]
        copies.append(pltpu.make_async_copy(made.at[pl.ds(at, size)], target, sem.at[i]))
        copies[-1].start()
    return copies


def out_own_kernel(echo_own, up_own, left, w_out, grad_out, back_own, right, made, sem):
    at_own = own_and_other(echo_own.shape[1])[0]
    stack(right, up_own[...], echo_own[...])
    copies = product(left, right, made, grad_out, at_own, sem, 128)
    back_own[...] = contract_cols(echo_own[...], w_out[:, at_own])
    for copy in copies:
        copy.wait()


def final_kernel(*refs):
    (
        echo_other, up_other, left_out, left_in, back_pre, slope, bend, second, back_hidden, back_own,
        w_out, packed, readout, *home, _, grad_out, grad_in, r2_grad,
        right_out, right_in, made_out, made_in, made_r2, sem_out, sem_in, sem_r2,
    ) = refs
    half = echo_other.shape[1]
    at_own, at_other = own_and_other(half)
    stack(right_out, up_other[...], echo_other[...])
    copies = product(left_out, right_out, made_out, grad_out, at_other, sem_out, 128)
    back = back_own[...] + contract_cols(echo_other[...], w_out[:, at_other])
    final_pre = (back * slope[...] + second[...] * back_hidden[...] * bend[...]).astype(BF)
    stack(right_in, back_pre[...], final_pre)
    copies += product(left_in, right_in, made_in, grad_in, slice(None), sem_in, 256)
    slot = packed[:, 2 * half :].astype(F32)
    slot = slot[:, 1:2] * 128.0 + slot[:, 2:3]
    for columns, at in ((slice(0, half), at_own), (slice(half, 2 * half), at_other)):
        picked = sum(found[:, columns].astype(F32) for found in home)
        tangent = jnp.tanh(packed[:, at].astype(F32))
        dropped = readout[:, at] * (1.0 - tangent * tangent)
        made_r2[:, at] = jnp.where(slot >= 0.0, picked, dropped).astype(BF)
    copies.append(pltpu.make_async_copy(made_r2, r2_grad, sem_r2))
    copies[-1].start()
    for copy in copies:
        copy.wait()


def run(kernel, shapes, args, flops, scratch=(), hbm=(), alias=None):
    spaces = [pl.ANY if at in hbm else pltpu.VMEM for at in range(len(shapes))]
    sources = [pl.ANY if alias and at in alias else pltpu.VMEM for at in range(len(args))]
    return pl.pallas_call(
        kernel,
        out_shape=[jax.ShapeDtypeStruct(shape, kind) for shape, kind in shapes],
        in_specs=[pl.BlockSpec(memory_space=space) for space in sources],
        out_specs=[pl.BlockSpec(memory_space=space) for space in spaces],
        scratch_shapes=list(scratch),
        input_output_aliases=alias or {},
        compiler_params=pltpu.CompilerParams(vmem_limit_bytes=20 << 20),
        cost_estimate=pl.CostEstimate(flops=flops, bytes_accessed=0, transcendentals=0),
    )(*[
        arg if space is pl.ANY else pltpu.with_memory_space_constraint(arg, pltpu.VMEM)
        for arg, space in zip(args, sources)
    ])


def hold(matrix, after):
    def kernel(source, after_ref, held, there, sem):
        del after_ref
        copy = pltpu.make_async_copy(source, held, sem)
        copy.start()
        there[...] = jnp.zeros_like(there)
        copy.wait()

    vmem = pl.BlockSpec(memory_space=pltpu.VMEM)
    return pl.pallas_call(
        kernel,
        out_shape=(pltpu.VMEM(matrix.shape, matrix.dtype), pltpu.VMEM(after.shape, BF)),
        in_specs=[pl.BlockSpec(memory_space=pltpu.HBM), pl.BlockSpec(memory_space=pl.ANY)],
        out_specs=(vmem, vmem),
        scratch_shapes=[pltpu.SemaphoreType.DMA],
        compiler_params=pltpu.CompilerParams(vmem_limit_bytes=1 << 20),
        cost_estimate=pl.CostEstimate(flops=0, bytes_accessed=matrix.size * 4, transcendentals=0),
    )(pltpu.with_memory_space_constraint(matrix, pltpu.HBM), after)


def pack(tokens, combine, routes, capacity_slot):
    local, width = tokens.shape
    shape = (local, width + 128)
    column = lax.broadcasted_iota(jnp.int32, shape, 1) - width
    routes, slots, combine = (
        lax.broadcast_in_dim(values, shape, (0,)) for values in (routes, capacity_slot, combine)
    )
    numbers = jnp.where(column == 4, lax.axis_index("dp"), jnp.where(column == 0, routes, slots))
    numbers = jnp.where(column == 1, numbers >> 7, numbers & 127).astype(BF)
    numbers = jnp.where(column == 3, combine, numbers)
    return jnp.where(column < 0, jnp.pad(tokens, ((0, 0), (0, 128))), numbers)


def shards(tokens, combine, routes, capacity_slot, readout, weight_in, weight_out):
    n_dp = lax.axis_size("dp")
    n_ex = lax.axis_size("expert")
    local, width = tokens.shape
    units = weight_in.shape[2]
    capacity = 5 * local * n_ex // (4 * n_dp)
    rows = n_dp * capacity
    splits = digits(n_ex)
    core, chips = splits[0], splits[1:]

    packed = pack(tokens, combine, routes, capacity_slot)
    first_core = lax.axis_index("expert") % core[1] == 0
    packed, first_core = lax.optimization_barrier((packed, first_core))

    dp_digit = (n_ex, n_dp)
    stages = [[dp_digit]] + pairs(chips) if n_dp > 2 else pairs([dp_digit] + chips)
    stages += [[core]]
    gathered, blocks, (matrix_in, matrix_out) = gather_rows(
        packed,
        stages,
        functools.partial(hold, weight_in[0]),
        functools.partial(hold, weight_out[0]),
    )
    found_at = [blocks.index(((*dp_digit, k),) if k > 0 else ()) * local for k in range(n_dp)]

    half = width // 2
    head_part = jnp.where(first_core, readout[None, :half], readout[None, half:])
    wide, thin, part = (rows, width), (rows, units), (rows, half)
    half_flops = rows * width * units

    def swap(values):
        return fetch(values, [(*core, 1)])

    def shared_sum(mine, other, home=()):
        total = mine + other.astype(F32)
        for stage in pairs(chips):
            own = total.astype(BF)
            last = home and stage == pairs(chips)[-1]
            if last:
                own, *home = lax.optimization_barrier((own, *home))
            parts = [fetch(own, steps_of(stage, offset)) for offset in offsets_of(stage)[1:]]
            if last:
                home[1:] = [fetch(home[k], [(*dp_digit, k)], back=True) for k in range(1, n_dp)]
                parts, home = lax.optimization_barrier((parts, home))
            total = own.astype(F32) + sum(part.astype(F32) for part in parts)
        return (total, *home) if home else total

    rows_in, col, hidden, pre_act, other, picks = run(
        functools.partial(forward_kernel, local, found_at),
        [(wide, BF), ((rows, 1), F32), (thin, BF), (thin, F32), (part, BF),
         ((n_dp * local, rows), F32)],
        (*gathered, matrix_in, matrix_out),
        3 * half_flops,
    )
    other = swap(other)
    mine, slope, bend, col_wide = run(
        mix_kernel,
        [(part, F32), (thin, F32), (thin, F32), (part, F32)],
        (hidden, pre_act, col, matrix_out),
        half_flops,
    )
    mixed = shared_sum(mine, other)
    rows_part = jnp.where(first_core, rows_in[:, :half], rows_in[:, half:])
    tangent = jnp.tanh(rows_part.astype(F32) + mixed)
    sech_sq = 1.0 - tangent * tangent
    upstream = head_part * sech_sq
    up_own = upstream.astype(BF)
    up_other = swap(up_own)
    (back_own,) = run(back_own_kernel, [(thin, F32)], (up_own, matrix_out), half_flops)
    back_hidden, back_pre, other = run(
        backward_kernel,
        [(thin, F32), (thin, BF), (part, BF)],
        (back_own, up_other, col, slope, matrix_in, matrix_out),
        2 * half_flops,
    )
    other = swap(other)
    (mine,) = run(grad_kernel, [(part, F32)], (back_pre, matrix_in), half_flops)
    grad_own = (upstream + shared_sum(mine, other)).astype(BF)
    grad_other = swap(grad_own)
    (second_own,) = run(second_own_kernel, [(thin, F32)], (grad_own, matrix_in), half_flops)
    second, push, other = run(
        push_kernel,
        [(thin, F32), (thin, BF), (part, BF)],
        (second_own, grad_other, col, slope, matrix_in, matrix_out),
        2 * half_flops,
    )
    other = swap(other)
    deep = 2 * padded(rows)
    mine, left_out, left_in, *home = run(
        pull_kernel,
        [(part, F32), ((deep, units), BF), ((deep, width), BF)] + [((local, width), BF)] * n_dp,
        (push, hidden, grad_own, grad_other, rows_in, picks, matrix_out),
        half_flops,
    )
    pushed, *home = shared_sum(mine, other, home)

    total_push = grad_own.astype(F32) + pushed
    curve_term = total_push * head_part * (-2.0 * tangent * sech_sq)
    echo_own = (col_wide * curve_term).astype(BF)
    echo_other = swap(echo_own)
    copies_in, copies_out = (
        pltpu.SemaphoreType.DMA((len(chunks(*size)),)) for size in ((width, 256), (units, 128))
    )
    grad_out, back_own = run(
        out_own_kernel,
        [((units, width), BF), (thin, F32)],
        (echo_own, up_own, left_out, matrix_out),
        2 * half_flops,
        scratch=[
            pltpu.VMEM((deep, half), BF),
            pltpu.VMEM((units, half), BF),
            copies_out,
        ],
        hbm=(0,),
    )
    args = (echo_other, up_other, left_out, left_in, back_pre, slope, bend, second,
            back_hidden, back_own, matrix_out, packed, readout[None, :], *home, grad_out)
    grad_out, grad_in, r2_grad = run(
        final_kernel,
        [((units, width), BF), ((width, units), BF), ((local, width), BF)],
        args,
        4 * half_flops,
        scratch=[
            pltpu.VMEM((deep, half), BF),
            pltpu.VMEM((deep, units), BF),
            pltpu.VMEM((units, half), BF),
            pltpu.VMEM((width, units), BF),
            pltpu.VMEM((local, width), BF),
            copies_out,
            copies_in,
            pltpu.SemaphoreType.DMA,
        ],
        hbm=(0, 1, 2),
        alias={len(args) - 1: 0},
    )

    return (r2_grad, grad_in[None], grad_out[None])


def solution(mesh):
    placed = (
        P(("dp", "expert"), None),
        P(("dp", "expert")),
        P(("dp", "expert")),
        P(("dp", "expert")),
        P(),
        P("dp", None, "expert"),
        P("dp", "expert", None),
    )
    return jax.shard_map(
        shards,
        mesh=mesh,
        in_specs=placed,
        out_specs=(P(("dp", "expert"), None), P("dp", None, "expert"), P("dp", "expert", None)),
        check_vma=False,
    )
```

time: 82.1 us -> 77 us (0.938)
  waiting for transfers between devices: 36.7 us -> 33.1 us
  starting transfers between devices: 27.1 us -> 25.7 us
  other arithmetic: 2.68 us -> 1.38 us
  Pallas kernels: 14.5 us -> 15.7 us
    ppermute x29, waiting for transfers between devices: 36.7 us -> 33.1 us  [fetch(): return lax.ppermute(values, axes, pairs)]
    ppermute x29, starting transfers between devices: 27.1 us -> 25.7 us  [fetch(): return lax.ppermute(values, axes, pairs)]
    pallas_call x4 -> x10, Pallas kernels: 10.5 us -> 11.6 us  [run(): pl.pallas_call(kernel, out_shape=[jax.ShapeDtypeStruct(shape, kind) for s...]
  transfers between devices with their start and end apart: 29 -> 29, of which waited for: 19 -> 21; matrix products, arithmetic and copies ran while one was open for 1% -> 0% of each run, Pallas kernels for 5% -> 11%
where the time goes in v3:
time: 77 us; the launch traced here: 76.7 us
  waiting for transfers between devices  33.1 us (43%)
  starting transfers between devices  25.7 us (33%)
  Pallas kernels  15.7 us (20%)
  other arithmetic  1.38 us (2%)
  between operations  0.89 us (1%)
    ppermute x29, waiting for transfers between devices, fetch(): return lax.ppermute(values, axes, pairs)  33.1 us
    ppermute x29, starting transfers between devices, fetch(): return lax.ppermute(values, axes, pairs)  25.7 us
    pallas_call x10, Pallas kernels, run(): pl.pallas_call(kernel, out_shape=[jax.ShapeDtypeStruct(shape, kind) for s...  11.6 us
    pallas_call x2, Pallas kernels, hold(): pl.pallas_call(kernel, out_shape=(pltpu.VMEM(matrix.shape, matrix.dtype),...  4.09 us
  transfers between devices with their start and end apart: 29, of which 21 were waited for; matrix products, arithmetic and copies ran while one was open for 0% of the time, Pallas kernels for 11%

profile of v3, /device:TPU:0, one launch (start us, length us, event | category | flops | bytes accessed | tf_op | source)
XLA Modules:
  0.0 76.7 jit_solution(7228367872160000173)
XLA Ops:
  1.5 4.0 %collective-permute-start.2 = (bf16[2,2176]{1,0:T(2,128)(2,1)S(1)}, bf16[2,2176]{1,0:T(2,128)(2,1)S(1)}, u32[]{:S(2)}, u32[]{:S(2)}) collective-permute-start(bf16[2,2176]{1,0:T(2,128)(2,1)S(1)} %broadcast_select_fusion.1.after_ref.refs_11_), channel_id=1, source_target_pairs={{18,0},{19,1},{16,2},{17,3},{22,4},{23,5},{20,6},{21,7},{26,8},{27... | collective-permute-start | bytes 26120 | tf_op jit(solution)/shard_map/ppermute | solution.py:57
  6.1 2.0 %shard_map.94 = (bf16[2048,896]{1,0:T(8,128)(2,1)S(1)}, bf16[2,2176]{1,0:T(2,128)(2,1)S(1)}) custom-call(bf16[2048,896]{1,0:T(8,128)(2,1)} %bitcast.7, bf16[2,2176]{1,0:T(2,128)(2,1)S(1)} %broadcast_select_fusion.1.after_ref.refs_11_), custom_call_target="tpu_custom_call" | custom-call | bytes 7340032 | tf_op jit(solution)/shard_map/pallas_call | solution.py:261
  9.7 1.6 %collective-permute-start.4 = (bf16[8,2176]{1,0:T(8,128)(2,1)S(1)}, bf16[8,2176]{1,0:T(8,128)(2,1)S(1)}, u32[]{:S(2)}, u32[]{:S(2)}) collective-permute-start(bf16[8,2176]{1,0:T(8,128)(2,1)S(1)} %pad_maximum_fusion.after_ref), channel_id=1, source_target_pairs={{4,0},{5,1},{6,2},{7,3},{0,4},{1,5},{2,6},{3,7},{12,8},{13,9},{14,... | collective-permute-start | bytes 104456 | tf_op jit(solution)/shard_map/ppermute | solution.py:57
  11.4 2.6 %collective-permute-start.3 = (bf16[8,2176]{1,0:T(8,128)(2,1)S(1)}, bf16[8,2176]{1,0:T(8,128)(2,1)S(1)}, u32[]{:S(2)}, u32[]{:S(2)}) collective-permute-start(bf16[8,2176]{1,0:T(8,128)(2,1)S(1)} %pad_maximum_fusion.after_ref), channel_id=1, source_target_pairs={{8,0},{9,1},{10,2},{11,3},{12,4},{13,5},{14,6},{15,7},{0,8},{1,9},... | collective-permute-start | bytes 104456 | tf_op jit(solution)/shard_map/ppermute | solution.py:57
  14.2 2.0 %shard_map.95 = (bf16[896,2048]{1,0:T(8,128)(2,1)S(1)}, bf16[8,2176]{1,0:T(8,128)(2,1)S(1)}) custom-call(bf16[896,2048]{1,0:T(8,128)(2,1)} %bitcast.6, bf16[8,2176]{1,0:T(8,128)(2,1)S(1)} %pad_maximum_fusion.after_ref), custom_call_target="tpu_custom_call" | custom-call | bytes 7340032 | tf_op jit(solution)/shard_map/pallas_call | solution.py:261
  17.0 2.7 %collective-permute-done.5.refs_3_ = bf16[8,2176]{1,0:T(8,128)(2,1)S(1)} collective-permute-done((bf16[8,2176]{1,0:T(8,128)(2,1)S(1)}, bf16[8,2176]{1,0:T(8,128)(2,1)S(1)}, u32[]{:S(2)}, u32[]{:S(2)}) %collective-permute-start.5) | collective-permute-done | bytes 34848 | tf_op jit(solution)/shard_map/ppermute | solution.py:57
  19.7 1.2 %collective-permute-done.9.refs_7_ = bf16[8,2176]{1,0:T(8,128)(2,1)S(1)} collective-permute-done((bf16[8,2176]{1,0:T(8,128)(2,1)S(1)}, bf16[8,2176]{1,0:T(8,128)(2,1)S(1)}, u32[]{:S(2)}, u32[]{:S(2)}) %collective-permute-start.9) | collective-permute-done | bytes 34848 | tf_op jit(solution)/shard_map/ppermute | solution.py:57
  20.9 1.7 %shard_map.96 = (bf16[40,2048]{1,0:T(8,128)(2,1)S(1)}, f32[40,1]{1,0:T(8,128)S(1)}, bf16[40,896]{1,0:T(8,128)(2,1)S(1)}, f32[40,896]{1,0:T(8,128)S(1)}, bf16[40,...) custom-call(bf16[8,2176]{1,0:T(8,128)(2,1)S(1)} %fusion.7.refs_0_, bf16[8,2176]{1,0:T(8,128)(2,1)S(1)} %collective-permute-done.3.refs_1_, ...), custom_call_target="tpu_custom_call" | custom-call | flops 220200960 | tf_op jit(solution)/shard_map/pallas_call | solution.py:237
  24.6 2.9 %collective-permute-start.11 = (bf16[40,1024]{1,0:T(8,128)(2,1)S(1)}, bf16[40,1024]{1,0:T(8,128)(2,1)S(1)}, u32[]{:S(2)}, u32[]{:S(2)}) collective-permute-start(bf16[40,1024]{1,0:T(8,128)(2,1)S(1)} %add_convert_fusion.6), channel_id=1, source_target_pairs={{4,0},{5,1},{6,2},{7,3},{0,4},{1,5},{2,6},{3,7},{12,8},{13,9},{14,... | collective-permute-start | bytes 245768 | tf_op jit(solution)/shard_map/ppermute | solution.py:57
  27.5 2.7 %collective-permute-done.13 = bf16[40,1024]{1,0:T(8,128)(2,1)S(1)} collective-permute-done((bf16[40,1024]{1,0:T(8,128)(2,1)S(1)}, bf16[40,1024]{1,0:T(8,128)(2,1)S(1)}, u32[]{:S(2)}, u32[]{:S(2)}) %collective-permute-start.13) | collective-permute-done | bytes 81952 | tf_op jit(solution)/shard_map/ppermute | solution.py:57
  30.4 1.1 %collective-permute-start.14 = (bf16[40,1024]{1,0:T(8,128)(2,1)S(1)}, bf16[40,1024]{1,0:T(8,128)(2,1)S(1)}, u32[]{:S(2)}, u32[]{:S(2)}) collective-permute-start(bf16[40,1024]{1,0:T(8,128)(2,1)S(1)} %add_convert_fusion.5), channel_id=1, source_target_pairs={{8,0},{9,1},{10,2},{11,3},{12,4},{13,5},{14,6},{15,7},{0,8},{1,9},... | collective-permute-start | bytes 245768 | tf_op jit(solution)/shard_map/ppermute | solution.py:57
  31.5 5.4 %collective-permute-done.14 = bf16[40,1024]{1,0:T(8,128)(2,1)S(1)} collective-permute-done((bf16[40,1024]{1,0:T(8,128)(2,1)S(1)}, bf16[40,1024]{1,0:T(8,128)(2,1)S(1)}, u32[]{:S(2)}, u32[]{:S(2)}) %collective-permute-start.14) | collective-permute-done | bytes 81952 | tf_op jit(solution)/shard_map/ppermute | solution.py:57
  38.4 1.2 %shard_map.99 = (f32[40,896]{1,0:T(8,128)S(1)}, bf16[40,896]{1,0:T(8,128)(2,1)S(1)}, bf16[40,1024]{1,0:T(8,128)(2,1)S(1)}) custom-call(f32[40,896]{1,0:T(8,128)S(1)} %shard_map.98.back_own, bf16[40,1024]{1,0:T(8,128)(2,1)S(1)} %collective-permute-done.15.up_other.refs_1_, f32[40,1]{1,0:T(8,128)S(1)} %get-tuple-element.48.col, ...), custom_call_target="tpu_custom_call" | custom-call | flops 146800640 | tf_op jit(solution)/shard_map/pallas_call | solution.py:237
  41.5 1.5 %collective-permute-start.18 = (bf16[40,1024]{1,0:T(8,128)(2,1)S(1)}, bf16[40,1024]{1,0:T(8,128)(2,1)S(1)}, u32[]{:S(2)}, u32[]{:S(2)}) collective-permute-start(bf16[40,1024]{1,0:T(8,128)(2,1)S(1)} %add_convert_fusion.4), channel_id=1, source_target_pairs={{2,0},{3,1},{0,2},{1,3},{6,4},{7,5},{4,6},{5,7},{10,8},{11,9},{8,1... | collective-permute-start | bytes 245768 | tf_op jit(solution)/shard_map/ppermute | solution.py:57
  43.0 1.5 %collective-permute-start.17 = (bf16[40,1024]{1,0:T(8,128)(2,1)S(1)}, bf16[40,1024]{1,0:T(8,128)(2,1)S(1)}, u32[]{:S(2)}, u32[]{:S(2)}) collective-permute-start(bf16[40,1024]{1,0:T(8,128)(2,1)S(1)} %add_convert_fusion.4), channel_id=1, source_target_pairs={{4,0},{5,1},{6,2},{7,3},{0,4},{1,5},{2,6},{3,7},{12,8},{13,9},{14,... | collective-permute-start | bytes 245768 | tf_op jit(solution)/shard_map/ppermute | solution.py:57
  44.5 2.7 %collective-permute-done.19 = bf16[40,1024]{1,0:T(8,128)(2,1)S(1)} collective-permute-done((bf16[40,1024]{1,0:T(8,128)(2,1)S(1)}, bf16[40,1024]{1,0:T(8,128)(2,1)S(1)}, u32[]{:S(2)}, u32[]{:S(2)}) %collective-permute-start.19) | collective-permute-done | bytes 81952 | tf_op jit(solution)/shard_map/ppermute | solution.py:57
  48.7 5.6 %collective-permute-done.20 = bf16[40,1024]{1,0:T(8,128)(2,1)S(1)} collective-permute-done((bf16[40,1024]{1,0:T(8,128)(2,1)S(1)}, bf16[40,1024]{1,0:T(8,128)(2,1)S(1)}, u32[]{:S(2)}, u32[]{:S(2)}) %collective-permute-start.20) | collective-permute-done | bytes 81952 | tf_op jit(solution)/shard_map/ppermute | solution.py:57
  59.4 2.0 %collective-permute-start.23 = (bf16[40,1024]{1,0:T(8,128)(2,1)S(1)}, bf16[40,1024]{1,0:T(8,128)(2,1)S(1)}, u32[]{:S(2)}, u32[]{:S(2)}) collective-permute-start(bf16[40,1024]{1,0:T(8,128)(2,1)S(1)} %add_convert_fusion.1), channel_id=1, source_target_pairs={{4,0},{5,1},{6,2},{7,3},{0,4},{1,5},{2,6},{3,7},{12,8},{13,9},{14,... | collective-permute-start | bytes 245768 | tf_op jit(solution)/shard_map/ppermute | solution.py:57
  61.4 2.7 %collective-permute-done.25 = bf16[40,1024]{1,0:T(8,128)(2,1)S(1)} collective-permute-done((bf16[40,1024]{1,0:T(8,128)(2,1)S(1)}, bf16[40,1024]{1,0:T(8,128)(2,1)S(1)}, u32[]{:S(2)}, u32[]{:S(2)}) %collective-permute-start.25) | collective-permute-done | bytes 81952 | tf_op jit(solution)/shard_map/ppermute | solution.py:57
  65.8 1.5 %collective-permute-start.27 = (bf16[2,2048]{1,0:T(2,128)(2,1)S(1)}, bf16[2,2048]{1,0:T(2,128)(2,1)S(1)}, u32[]{:S(2)}, u32[]{:S(2)}) collective-permute-start(bf16[2,2048]{1,0:T(2,128)(2,1)S(1)} %get-tuple-element.65), channel_id=1, source_target_pairs={{0,16},{1,17},{2,18},{3,19},{4,20},{5,21},{6,22},{7,23},{8,24},{9,... | collective-permute-start | bytes 24584 | tf_op jit(solution)/shard_map/ppermute | solution.py:57
  67.3 2.2 %collective-permute-done.27.refs_14_ = bf16[2,2048]{1,0:T(2,128)(2,1)S(1)} collective-permute-done((bf16[2,2048]{1,0:T(2,128)(2,1)S(1)}, bf16[2,2048]{1,0:T(2,128)(2,1)S(1)}, u32[]{:S(2)}, u32[]{:S(2)}) %collective-permute-start.27) | collective-permute-done | bytes 8224 | tf_op jit(solution)/shard_map/ppermute | solution.py:57
  69.5 1.7 %collective-permute-done.26 = bf16[40,1024]{1,0:T(8,128)(2,1)S(1)} collective-permute-done((bf16[40,1024]{1,0:T(8,128)(2,1)S(1)}, bf16[40,1024]{1,0:T(8,128)(2,1)S(1)}, u32[]{:S(2)}, u32[]{:S(2)}) %collective-permute-start.26) | collective-permute-done | bytes 81952 | tf_op jit(solution)/shard_map/ppermute | solution.py:57
  71.3 1.8 %shard_map.104 = (bf16[896,2048]{1,0:T(8,128)(2,1)}, f32[40,896]{1,0:T(8,128)S(1)}) custom-call(bf16[40,1024]{1,0:T(8,128)(2,1)S(1)} %multiply_convert_fusion.echo_own, bf16[40,1024]{1,0:T(8,128)(2,1)S(1)} %get-tuple-element.79.up_own, bf16[96,896]{1,0:T(8,128)(2,1)S(1)} %get-tuple-element.67.left.refs_2_, ...), custom_call_target="tpu_custom_call" | custom-call | flops 146800640 | tf_op jit(solution)/shard_map/pallas_call | solution.py:237
  73.1 3.6 %shard_map.105 = (bf16[896,2048]{1,0:T(8,128)(2,1)}, bf16[2048,896]{1,0:T(8,128)(2,1)}, bf16[2,2048]{1,0:T(2,128)(2,1)}) custom-call(bf16[40,1024]{1,0:T(8,128)(2,1)S(1)} %collective-permute-done.28.refs_0_, bf16[40,1024]{1,0:T(8,128)(2,1)S(1)} %collective-permute-done.15.up_other.refs_1_, ...), custom_call_target="tpu_custom_call", output_to_operand_aliasing={{0}: (15, {})} | custom-call | flops 293601280 | tf_op jit(solution)/shard_map/pallas_call | solution.py:237
  (65 shorter events, 17.8 us)
Async XLA Ops:
  1.5 6.7 %collective-permute-start.2 = (bf16[2,2176]{1,0:T(2,128)(2,1)S(1)}, bf16[2,2176]{1,0:T(2,128)(2,1)S(1)}, u32[]{:S(2)}, u32[]{:S(2)}) collective-permute-start(bf16[2,2176]{1,0:T(2,128)(2,1)S(1)} %broadcast_select_fusion.1.after_ref.refs_11_), channel_id=1, source_target_pairs={{18,0},{19,1},{16,2},{17,3},{22,4},{23,5},{20,6},{21,7},{26,8},{27... | collective-permute-start | bytes 26120 | tf_op jit(solution)/shard_map/ppermute | solution.py:57
  5.5 3.7 %collective-permute-start.1 = (bf16[2,2176]{1,0:T(2,128)(2,1)S(1)}, bf16[2,2176]{1,0:T(2,128)(2,1)S(1)}, u32[]{:S(2)}, u32[]{:S(2)}) collective-permute-start(bf16[2,2176]{1,0:T(2,128)(2,1)S(1)} %broadcast_select_fusion.1.after_ref.refs_11_), channel_id=1, source_target_pairs={{16,0},{17,1},{18,2},{19,3},{20,4},{21,5},{22,6},{23,7},{24,8},{25... | collective-permute-start | bytes 26120 | tf_op jit(solution)/shard_map/ppermute | solution.py:57
  6.0 3.7 %collective-permute-start = (bf16[2,2176]{1,0:T(2,128)(2,1)S(1)}, bf16[2,2176]{1,0:T(2,128)(2,1)S(1)}, u32[]{:S(2)}, u32[]{:S(2)}) collective-permute-start(bf16[2,2176]{1,0:T(2,128)(2,1)S(1)} %broadcast_select_fusion.1.after_ref.refs_11_), channel_id=1, source_target_pairs={{2,0},{3,1},{0,2},{1,3},{6,4},{7,5},{4,6},{5,7},{10,8},{11,9},{8,1... | collective-permute-start | bytes 26120 | tf_op jit(solution)/shard_map/ppermute | solution.py:57
  9.7 6.6 %collective-permute-start.4 = (bf16[8,2176]{1,0:T(8,128)(2,1)S(1)}, bf16[8,2176]{1,0:T(8,128)(2,1)S(1)}, u32[]{:S(2)}, u32[]{:S(2)}) collective-permute-start(bf16[8,2176]{1,0:T(8,128)(2,1)S(1)} %pad_maximum_fusion.after_ref), channel_id=1, source_target_pairs={{4,0},{5,1},{6,2},{7,3},{0,4},{1,5},{2,6},{3,7},{12,8},{13,9},{14,... | collective-permute-start | bytes 104456 | tf_op jit(solution)/shard_map/ppermute | solution.py:57
  11.4 5.5 %collective-permute-start.3 = (bf16[8,2176]{1,0:T(8,128)(2,1)S(1)}, bf16[8,2176]{1,0:T(8,128)(2,1)S(1)}, u32[]{:S(2)}, u32[]{:S(2)}) collective-permute-start(bf16[8,2176]{1,0:T(8,128)(2,1)S(1)} %pad_maximum_fusion.after_ref), channel_id=1, source_target_pairs={{8,0},{9,1},{10,2},{11,3},{12,4},{13,5},{14,6},{15,7},{0,8},{1,9},... | collective-permute-start | bytes 104456 | tf_op jit(solution)/shard_map/ppermute | solution.py:57
  14.0 5.7 %collective-permute-start.5 = (bf16[8,2176]{1,0:T(8,128)(2,1)S(1)}, bf16[8,2176]{1,0:T(8,128)(2,1)S(1)}, u32[]{:S(2)}, u32[]{:S(2)}) collective-permute-start(bf16[8,2176]{1,0:T(8,128)(2,1)S(1)} %pad_maximum_fusion.after_ref), channel_id=1, source_target_pairs={{12,0},{13,1},{14,2},{15,3},{8,4},{9,5},{10,6},{11,7},{4,8},{5,9},... | collective-permute-start | bytes 104456 | tf_op jit(solution)/shard_map/ppermute | solution.py:57
  16.3 3.4 %collective-permute-start.6 = (bf16[8,2176]{1,0:T(8,128)(2,1)S(1)}, bf16[8,2176]{1,0:T(8,128)(2,1)S(1)}, u32[]{:S(2)}, u32[]{:S(2)}) collective-permute-start(bf16[8,2176]{1,0:T(8,128)(2,1)S(1)} %fusion.7.refs_0_), channel_id=1, source_target_pairs={{1,0},{0,1},{3,2},{2,3},{5,4},{4,5},{7,6},{6,7},{9,8},{8,9},{11,10... | collective-permute-start | bytes 104456 | tf_op jit(solution)/shard_map/ppermute | solution.py:57
  16.4 3.3 %collective-permute-start.8 = (bf16[8,2176]{1,0:T(8,128)(2,1)S(1)}, bf16[8,2176]{1,0:T(8,128)(2,1)S(1)}, u32[]{:S(2)}, u32[]{:S(2)}) collective-permute-start(bf16[8,2176]{1,0:T(8,128)(2,1)S(1)} %collective-permute-done.4.refs_2_), channel_id=1, source_target_pairs={{1,0},{0,1},{3,2},{2,3},{5,4},{4,5},{7,6},{6,7},{9,8},{8,9},{11,10... | collective-permute-start | bytes 104456 | tf_op jit(solution)/shard_map/ppermute | solution.py:57
  16.9 2.8 %collective-permute-start.7 = (bf16[8,2176]{1,0:T(8,128)(2,1)S(1)}, bf16[8,2176]{1,0:T(8,128)(2,1)S(1)}, u32[]{:S(2)}, u32[]{:S(2)}) collective-permute-start(bf16[8,2176]{1,0:T(8,128)(2,1)S(1)} %collective-permute-done.3.refs_1_), channel_id=1, source_target_pairs={{1,0},{0,1},{3,2},{2,3},{5,4},{4,5},{7,6},{6,7},{9,8},{8,9},{11,10... | collective-permute-start | bytes 104456 | tf_op jit(solution)/shard_map/ppermute | solution.py:57
  22.6 1.3 %collective-permute-start.10 = (bf16[40,1024]{1,0:T(8,128)(2,1)S(1)}, bf16[40,1024]{1,0:T(8,128)(2,1)S(1)}, u32[]{:S(2)}, u32[]{:S(2)}) collective-permute-start(bf16[40,1024]{1,0:T(8,128)(2,1)S(1)} %get-tuple-element.53), channel_id=1, source_target_pairs={{1,0},{0,1},{3,2},{2,3},{5,4},{4,5},{7,6},{6,7},{9,8},{8,9},{11,10... | collective-permute-start | bytes 245768 | tf_op jit(solution)/shard_map/ppermute | solution.py:57
  23.9 6.3 %collective-permute-start.13 = (bf16[40,1024]{1,0:T(8,128)(2,1)S(1)}, bf16[40,1024]{1,0:T(8,128)(2,1)S(1)}, u32[]{:S(2)}, u32[]{:S(2)}) collective-permute-start(bf16[40,1024]{1,0:T(8,128)(2,1)S(1)} %add_convert_fusion.6), channel_id=1, source_target_pairs={{6,0},{7,1},{4,2},{5,3},{2,4},{3,5},{0,6},{1,7},{14,8},{15,9},{12,... | collective-permute-start | bytes 245768 | tf_op jit(solution)/shard_map/ppermute | solution.py:57
  24.0 6.3 %collective-permute-start.12 = (bf16[40,1024]{1,0:T(8,128)(2,1)S(1)}, bf16[40,1024]{1,0:T(8,128)(2,1)S(1)}, u32[]{:S(2)}, u32[]{:S(2)}) collective-permute-start(bf16[40,1024]{1,0:T(8,128)(2,1)S(1)} %add_convert_fusion.6), channel_id=1, source_target_pairs={{2,0},{3,1},{0,2},{1,3},{6,4},{7,5},{4,6},{5,7},{10,8},{11,9},{8,1... | collective-permute-start | bytes 245768 | tf_op jit(solution)/shard_map/ppermute | solution.py:57
  24.6 5.8 %collective-permute-start.11 = (bf16[40,1024]{1,0:T(8,128)(2,1)S(1)}, bf16[40,1024]{1,0:T(8,128)(2,1)S(1)}, u32[]{:S(2)}, u32[]{:S(2)}) collective-permute-start(bf16[40,1024]{1,0:T(8,128)(2,1)S(1)} %add_convert_fusion.6), channel_id=1, source_target_pairs={{4,0},{5,1},{6,2},{7,3},{0,4},{1,5},{2,6},{3,7},{12,8},{13,9},{14,... | collective-permute-start | bytes 245768 | tf_op jit(solution)/shard_map/ppermute | solution.py:57
  30.4 6.5 %collective-permute-start.14 = (bf16[40,1024]{1,0:T(8,128)(2,1)S(1)}, bf16[40,1024]{1,0:T(8,128)(2,1)S(1)}, u32[]{:S(2)}, u32[]{:S(2)}) collective-permute-start(bf16[40,1024]{1,0:T(8,128)(2,1)S(1)} %add_convert_fusion.5), channel_id=1, source_target_pairs={{8,0},{9,1},{10,2},{11,3},{12,4},{13,5},{14,6},{15,7},{0,8},{1,9},... | collective-permute-start | bytes 245768 | tf_op jit(solution)/shard_map/ppermute | solution.py:57
  40.9 6.3 %collective-permute-start.19 = (bf16[40,1024]{1,0:T(8,128)(2,1)S(1)}, bf16[40,1024]{1,0:T(8,128)(2,1)S(1)}, u32[]{:S(2)}, u32[]{:S(2)}) collective-permute-start(bf16[40,1024]{1,0:T(8,128)(2,1)S(1)} %add_convert_fusion.4), channel_id=1, source_target_pairs={{6,0},{7,1},{4,2},{5,3},{2,4},{3,5},{0,6},{1,7},{14,8},{15,9},{12,... | collective-permute-start | bytes 245768 | tf_op jit(solution)/shard_map/ppermute | solution.py:57
  41.5 6.0 %collective-permute-start.18 = (bf16[40,1024]{1,0:T(8,128)(2,1)S(1)}, bf16[40,1024]{1,0:T(8,128)(2,1)S(1)}, u32[]{:S(2)}, u32[]{:S(2)}) collective-permute-start(bf16[40,1024]{1,0:T(8,128)(2,1)S(1)} %add_convert_fusion.4), channel_id=1, source_target_pairs={{2,0},{3,1},{0,2},{1,3},{6,4},{7,5},{4,6},{5,7},{10,8},{11,9},{8,1... | collective-permute-start | bytes 245768 | tf_op jit(solution)/shard_map/ppermute | solution.py:57
  43.0 4.9 %collective-permute-start.17 = (bf16[40,1024]{1,0:T(8,128)(2,1)S(1)}, bf16[40,1024]{1,0:T(8,128)(2,1)S(1)}, u32[]{:S(2)}, u32[]{:S(2)}) collective-permute-start(bf16[40,1024]{1,0:T(8,128)(2,1)S(1)} %add_convert_fusion.4), channel_id=1, source_target_pairs={{4,0},{5,1},{6,2},{7,3},{0,4},{1,5},{2,6},{3,7},{12,8},{13,9},{14,... | collective-permute-start | bytes 245768 | tf_op jit(solution)/shard_map/ppermute | solution.py:57
  48.0 6.4 %collective-permute-start.20 = (bf16[40,1024]{1,0:T(8,128)(2,1)S(1)}, bf16[40,1024]{1,0:T(8,128)(2,1)S(1)}, u32[]{:S(2)}, u32[]{:S(2)}) collective-permute-start(bf16[40,1024]{1,0:T(8,128)(2,1)S(1)} %add_convert_fusion.3), channel_id=1, source_target_pairs={{8,0},{9,1},{10,2},{11,3},{12,4},{13,5},{14,6},{15,7},{0,8},{1,9},... | collective-permute-start | bytes 245768 | tf_op jit(solution)/shard_map/ppermute | solution.py:57
  57.9 6.3 %collective-permute-start.25 = (bf16[40,1024]{1,0:T(8,128)(2,1)S(1)}, bf16[40,1024]{1,0:T(8,128)(2,1)S(1)}, u32[]{:S(2)}, u32[]{:S(2)}) collective-permute-start(bf16[40,1024]{1,0:T(8,128)(2,1)S(1)} %add_convert_fusion.1), channel_id=1, source_target_pairs={{6,0},{7,1},{4,2},{5,3},{2,4},{3,5},{0,6},{1,7},{14,8},{15,9},{12,... | collective-permute-start | bytes 245768 | tf_op jit(solution)/shard_map/ppermute | solution.py:57
  58.7 6.0 %collective-permute-start.24 = (bf16[40,1024]{1,0:T(8,128)(2,1)S(1)}, bf16[40,1024]{1,0:T(8,128)(2,1)S(1)}, u32[]{:S(2)}, u32[]{:S(2)}) collective-permute-start(bf16[40,1024]{1,0:T(8,128)(2,1)S(1)} %add_convert_fusion.1), channel_id=1, source_target_pairs={{2,0},{3,1},{0,2},{1,3},{6,4},{7,5},{4,6},{5,7},{10,8},{11,9},{8,1... | collective-permute-start | bytes 245768 | tf_op jit(solution)/shard_map/ppermute | solution.py:57
  59.4 5.3 %collective-permute-start.23 = (bf16[40,1024]{1,0:T(8,128)(2,1)S(1)}, bf16[40,1024]{1,0:T(8,128)(2,1)S(1)}, u32[]{:S(2)}, u32[]{:S(2)}) collective-permute-start(bf16[40,1024]{1,0:T(8,128)(2,1)S(1)} %add_convert_fusion.1), channel_id=1, source_target_pairs={{4,0},{5,1},{6,2},{7,3},{0,4},{1,5},{2,6},{3,7},{12,8},{13,9},{14,... | collective-permute-start | bytes 245768 | tf_op jit(solution)/shard_map/ppermute | solution.py:57
  64.8 6.4 %collective-permute-start.26 = (bf16[40,1024]{1,0:T(8,128)(2,1)S(1)}, bf16[40,1024]{1,0:T(8,128)(2,1)S(1)}, u32[]{:S(2)}, u32[]{:S(2)}) collective-permute-start(bf16[40,1024]{1,0:T(8,128)(2,1)S(1)} %add_convert_fusion), channel_id=1, source_target_pairs={{8,0},{9,1},{10,2},{11,3},{12,4},{13,5},{14,6},{15,7},{0,8},{1,9},... | collective-permute-start | bytes 245768 | tf_op jit(solution)/shard_map/ppermute | solution.py:57
  65.8 3.7 %collective-permute-start.27 = (bf16[2,2048]{1,0:T(2,128)(2,1)S(1)}, bf16[2,2048]{1,0:T(2,128)(2,1)S(1)}, u32[]{:S(2)}, u32[]{:S(2)}) collective-permute-start(bf16[2,2048]{1,0:T(2,128)(2,1)S(1)} %get-tuple-element.65), channel_id=1, source_target_pairs={{0,16},{1,17},{2,18},{3,19},{4,20},{5,21},{6,22},{7,23},{8,24},{9,... | collective-permute-start | bytes 24584 | tf_op jit(solution)/shard_map/ppermute | solution.py:57
  71.3 1.9 %collective-permute-start.28 = (bf16[40,1024]{1,0:T(8,128)(2,1)S(1)}, bf16[40,1024]{1,0:T(8,128)(2,1)S(1)}, u32[]{:S(2)}, u32[]{:S(2)}) collective-permute-start(bf16[40,1024]{1,0:T(8,128)(2,1)S(1)} %multiply_convert_fusion.echo_own), channel_id=1, source_target_pairs={{1,0},{0,1},{3,2},{2,3},{5,4},{4,5},{7,6},{6,7},{9,8},{8,9},{11,10... | collective-permute-start | bytes 245768 | tf_op jit(solution)/shard_map/ppermute | solution.py:57
  (6 other events, 15.6 us)

commit v4 on v3

--- a/solution.py
+++ b/solution.py
@@ -14,10 +14,6 @@
 
 def contract_rows(left, right):
     return lax.dot_general(left, right, (((0,), (0,)), ((), ())), preferred_element_type=F32)
-
-
-def contract_cols(left, right):
-    return lax.dot_general(left, right, (((1,), (1,)), ((), ())), preferred_element_type=F32)
 
 
 def dot(left, right):
@@ -139,21 +135,28 @@
     col_wide[...] = jnp.broadcast_to(col[...], col_wide.shape)
 
 
-def back_own_kernel(up_own, w_out, back_own):
-    back_own[...] = contract_cols(up_own[...], w_out[:, own_and_other(up_own.shape[1])[0]])
-
-
-def backward_kernel(back_own, up_other, col, slope, w_in, w_out, back_hidden, back_pre, other):
+def turn_kernel(source, turned):
+    for at, size in chunks(source.shape[0], 128):
+        turned[:, at : at + size] = source[at : at + size, :].T
+
+
+def back_own_kernel(up_own, turned_out, back_own):
+    back_own[...] = dot(up_own[...], turned_out[own_and_other(up_own.shape[1])[0], :])
+
+
+def backward_kernel(
+    back_own, up_other, col, slope, turned_in, turned_out, back_hidden, back_pre, other
+):
     at_other = own_and_other(up_other.shape[1])[1]
-    back = col[...] * (back_own[...] + contract_cols(up_other[...], w_out[:, at_other]))
+    back = col[...] * (back_own[...] + dot(up_other[...], turned_out[at_other, :]))
     back_hidden[...] = back
     back = (back * slope[...]).astype(BF)
     back_pre[...] = back
-    other[...] = contract_cols(back, w_in[at_other, :]).astype(BF)
-
-
-def grad_kernel(back_pre, w_in, mine):
-    mine[...] = contract_cols(back_pre[...], w_in[own_and_other(mine.shape[1])[0], :])
+    other[...] = dot(back, turned_in[:, at_other]).astype(BF)
+
+
+def grad_kernel(back_pre, turned_in, mine):
+    mine[...] = dot(back_pre[...], turned_in[:, own_and_other(mine.shape[1])[0]])
 
 
 def second_own_kernel(grad_own, w_in, second_own):
@@ -195,11 +198,11 @@
     return copies
 
 
-def out_own_kernel(echo_own, up_own, left, w_out, grad_out, back_own, right, made, sem):
+def out_own_kernel(echo_own, up_own, left, turned_out, grad_out, back_own, right, made, sem):
     at_own = own_and_other(echo_own.shape[1])[0]
     stack(right, up_own[...], echo_own[...])
     copies = product(left, right, made, grad_out, at_own, sem, 128)
-    back_own[...] = contract_cols(echo_own[...], w_out[:, at_own])
+    back_own[...] = dot(echo_own[...], turned_out[at_own, :])
     for copy in copies:
         copy.wait()
 
@@ -207,14 +210,14 @@
 def final_kernel(*refs):
     (
         echo_other, up_other, left_out, left_in, back_pre, slope, bend, second, back_hidden, back_own,
-        w_out, packed, readout, *home, _, grad_out, grad_in, r2_grad,
+        turned_out, packed, readout, *home, _, grad_out, grad_in, r2_grad,
         right_out, right_in, made_out, made_in, made_r2, sem_out, sem_in, sem_r2,
     ) = refs
     half = echo_other.shape[1]
     at_own, at_other = own_and_other(half)
     stack(right_out, up_other[...], echo_other[...])
     copies = product(left_out, right_out, made_out, grad_out, at_other, sem_out, 128)
-    back = back_own[...] + contract_cols(echo_other[...], w_out[:, at_other])
+    back = back_own[...] + dot(echo_other[...], turned_out[at_other, :])
     final_pre = (back * slope[...] + second[...] * back_hidden[...] * bend[...]).astype(BF)
     stack(right_in, back_pre[...], final_pre)
     copies += product(left_in, right_in, made_in, grad_in, slice(None), sem_in, 256)
@@ -231,12 +234,15 @@
         copy.wait()
 
 
-def run(kernel, shapes, args, flops, scratch=(), hbm=(), alias=None):
+def run(kernel, shapes, args, flops, scratch=(), hbm=(), alias=None, kept=()):
     spaces = [pl.ANY if at in hbm else pltpu.VMEM for at in range(len(shapes))]
     sources = [pl.ANY if alias and at in alias else pltpu.VMEM for at in range(len(args))]
     return pl.pallas_call(
         kernel,
-        out_shape=[jax.ShapeDtypeStruct(shape, kind) for shape, kind in shapes],
+        out_shape=[
+            pltpu.VMEM(shape, kind) if at in kept else jax.ShapeDtypeStruct(shape, kind)
+            for at, (shape, kind) in enumerate(shapes)
+        ],
         in_specs=[pl.BlockSpec(memory_space=space) for space in sources],
         out_specs=[pl.BlockSpec(memory_space=space) for space in spaces],
         scratch_shapes=list(scratch),
@@ -315,19 +321,21 @@
     def swap(values):
         return fetch(values, [(*core, 1)])
 
-    def shared_sum(mine, other, home=()):
+    def shared_sum(mine, other, beside=(), home=()):
         total = mine + other.astype(F32)
         for stage in pairs(chips):
             own = total.astype(BF)
-            last = home and stage == pairs(chips)[-1]
-            if last:
+            last = stage == pairs(chips)[-1]
+            if last and home:
                 own, *home = lax.optimization_barrier((own, *home))
-            parts = [fetch(own, steps_of(stage, offset)) for offset in offsets_of(stage)[1:]]
-            if last:
+            parts = [fetch(own, steps_of(stage, offset)) for offset in offsets_of(stage)[:0:-1]]
+            if last and home:
                 home[1:] = [fetch(home[k], [(*dp_digit, k)], back=True) for k in range(1, n_dp)]
-                parts, home = lax.optimization_barrier((parts, home))
+                beside = home
+            if last and beside:
+                parts, beside = lax.optimization_barrier((parts, beside))
             total = own.astype(F32) + sum(part.astype(F32) for part in parts)
-        return (total, *home) if home else total
+        return (total, beside) if beside else total
 
     rows_in, col, hidden, pre_act, other, picks = run(
         functools.partial(forward_kernel, local, found_at),
@@ -343,22 +351,26 @@
         (hidden, pre_act, col, matrix_out),
         half_flops,
     )
-    mixed = shared_sum(mine, other)
+    turned = [
+        run(turn_kernel, [(matrix.shape[::-1], BF)], (matrix,), 8 * half_flops, kept=(0,))[0]
+        for matrix in (matrix_in, matrix_out)
+    ]
+    mixed, (turned_in, turned_out) = shared_sum(mine, other, turned)
     rows_part = jnp.where(first_core, rows_in[:, :half], rows_in[:, half:])
     tangent = jnp.tanh(rows_part.astype(F32) + mixed)
     sech_sq = 1.0 - tangent * tangent
     upstream = head_part * sech_sq
     up_own = upstream.astype(BF)
     up_other = swap(up_own)
-    (back_own,) = run(back_own_kernel, [(thin, F32)], (up_own, matrix_out), half_flops)
+    (back_own,) = run(back_own_kernel, [(thin, F32)], (up_own, turned_out), half_flops)
     back_hidden, back_pre, other = run(
         backward_kernel,
         [(thin, F32), (thin, BF), (part, BF)],
-        (back_own, up_other, col, slope, matrix_in, matrix_out),
+        (back_own, up_other, col, slope, turned_in, turned_out),
         2 * half_flops,
     )
     other = swap(other)
-    (mine,) = run(grad_kernel, [(part, F32)], (back_pre, matrix_in), half_flops)
+    (mine,) = run(grad_kernel, [(part, F32)], (back_pre, turned_in), half_flops)
     grad_own = (upstream + shared_sum(mine, other)).astype(BF)
     grad_other = swap(grad_own)
     (second_own,) = run(second_own_kernel, [(thin, F32)], (grad_own, matrix_in), half_flops)
@@ -376,7 +388,7 @@
         (push, hidden, grad_own, grad_other, rows_in, picks, matrix_out),
         half_flops,
     )
-    pushed, *home = shared_sum(mine, other, home)
+    pushed, home = shared_sum(mine, other, home=home)
 
     total_push = grad_own.astype(F32) + pushed
     curve_term = total_push * head_part * (-2.0 * tangent * sech_sq)
@@ -388,7 +400,7 @@
     grad_out, back_own = run(
         out_own_kernel,
         [((units, width), BF), (thin, F32)],
-        (echo_own, up_own, left_out, matrix_out),
+        (echo_own, up_own, left_out, turned_out),
         2 * half_flops,
         scratch=[
             pltpu.VMEM((deep, half), BF),
@@ -398,7 +410,7 @@
         hbm=(0,),
     )
     args = (echo_other, up_other, left_out, left_in, back_pre, slope, bend, second,
-            back_hidden, back_own, matrix_out, packed, readout[None, :], *home, grad_out)
+            back_hidden, back_own, turned_out, packed, readout[None, :], *home, grad_out)
     grad_out, grad_in, r2_grad = run(
         final_kernel,
         [((units, width), BF), ((width, units), BF), ((local, width), BF)],

time: 77 us -> 75.4 us (0.979)
  waiting for transfers between devices: 33.1 us -> 30.6 us
    ppermute x29, waiting for transfers between devices: 33.1 us -> 30.6 us  [fetch(): return lax.ppermute(values, axes, pairs)]
    pallas_call x10 -> x12, Pallas kernels: 11.6 us -> 12.3 us  [run(): pl.pallas_call(kernel, out_shape=[pltpu.VMEM(shape, kind) if at in kept e...]
  transfers between devices with their start and end apart: 29 -> 29, of which waited for: 21 -> 20; matrix products, arithmetic and copies ran while one was open for 0% -> 0% of each run, Pallas kernels for 11% -> 13%
where the time goes in v4:
time: 75.4 us; the launch traced here: 75.1 us
  waiting for transfers between devices  30.6 us (41%)
  starting transfers between devices  25.8 us (34%)
  Pallas kernels  16.4 us (22%)
  other arithmetic  1.36 us (2%)
  between operations  0.92 us (1%)
    ppermute x29, waiting for transfers between devices, fetch(): return lax.ppermute(values, axes, pairs)  30.6 us
    ppermute x29, starting transfers between devices, fetch(): return lax.ppermute(values, axes, pairs)  25.8 us
    pallas_call x12, Pallas kernels, run(): pl.pallas_call(kernel, out_shape=[pltpu.VMEM(shape, kind) if at in kept e...  12.3 us
    pallas_call x2, Pallas kernels, hold(): pl.pallas_call(kernel, out_shape=(pltpu.VMEM(matrix.shape, matrix.dtype),...  4.09 us
  transfers between devices with their start and end apart: 29, of which 20 were waited for; matrix products, arithmetic and copies ran while one was open for 0% of the time, Pallas kernels for 13%

profile of v4, /device:TPU:0, one launch (start us, length us, event | category | flops | bytes accessed | tf_op | source)
XLA Modules:
  0.0 75.1 jit_solution(15848486160666060391)
XLA Ops:
  1.5 4.0 %collective-permute-start.2 = (bf16[2,2176]{1,0:T(2,128)(2,1)S(1)}, bf16[2,2176]{1,0:T(2,128)(2,1)S(1)}, u32[]{:S(2)}, u32[]{:S(2)}) collective-permute-start(bf16[2,2176]{1,0:T(2,128)(2,1)S(1)} %broadcast_select_fusion.1.after_ref.refs_11_), channel_id=1, source_target_pairs={{18,0},{19,1},{16,2},{17,3},{22,4},{23,5},{20,6},{21,7},{26,8},{27... | collective-permute-start | bytes 26120 | tf_op jit(solution)/shard_map/ppermute | solution.py:53
  6.1 2.0 %shard_map.94 = (bf16[2048,896]{1,0:T(8,128)(2,1)S(1)}, bf16[2,2176]{1,0:T(2,128)(2,1)S(1)}) custom-call(bf16[2048,896]{1,0:T(8,128)(2,1)} %bitcast.7, bf16[2,2176]{1,0:T(2,128)(2,1)S(1)} %broadcast_select_fusion.1.after_ref.refs_11_), custom_call_target="tpu_custom_call" | custom-call | bytes 7340032 | tf_op jit(solution)/shard_map/pallas_call | solution.py:267
  9.7 1.6 %collective-permute-start.4 = (bf16[8,2176]{1,0:T(8,128)(2,1)S(1)}, bf16[8,2176]{1,0:T(8,128)(2,1)S(1)}, u32[]{:S(2)}, u32[]{:S(2)}) collective-permute-start(bf16[8,2176]{1,0:T(8,128)(2,1)S(1)} %pad_maximum_fusion.after_ref), channel_id=1, source_target_pairs={{4,0},{5,1},{6,2},{7,3},{0,4},{1,5},{2,6},{3,7},{12,8},{13,9},{14,... | collective-permute-start | bytes 104456 | tf_op jit(solution)/shard_map/ppermute | solution.py:53
  11.4 2.6 %collective-permute-start.3 = (bf16[8,2176]{1,0:T(8,128)(2,1)S(1)}, bf16[8,2176]{1,0:T(8,128)(2,1)S(1)}, u32[]{:S(2)}, u32[]{:S(2)}) collective-permute-start(bf16[8,2176]{1,0:T(8,128)(2,1)S(1)} %pad_maximum_fusion.after_ref), channel_id=1, source_target_pairs={{8,0},{9,1},{10,2},{11,3},{12,4},{13,5},{14,6},{15,7},{0,8},{1,9},... | collective-permute-start | bytes 104456 | tf_op jit(solution)/shard_map/ppermute | solution.py:53
  14.2 2.0 %shard_map.95 = (bf16[896,2048]{1,0:T(8,128)(2,1)S(1)}, bf16[8,2176]{1,0:T(8,128)(2,1)S(1)}) custom-call(bf16[896,2048]{1,0:T(8,128)(2,1)} %bitcast.6, bf16[8,2176]{1,0:T(8,128)(2,1)S(1)} %pad_maximum_fusion.after_ref), custom_call_target="tpu_custom_call" | custom-call | bytes 7340032 | tf_op jit(solution)/shard_map/pallas_call | solution.py:267
  17.0 2.7 %collective-permute-done.5.refs_3_ = bf16[8,2176]{1,0:T(8,128)(2,1)S(1)} collective-permute-done((bf16[8,2176]{1,0:T(8,128)(2,1)S(1)}, bf16[8,2176]{1,0:T(8,128)(2,1)S(1)}, u32[]{:S(2)}, u32[]{:S(2)}) %collective-permute-start.5) | collective-permute-done | bytes 34848 | tf_op jit(solution)/shard_map/ppermute | solution.py:53
  20.9 1.7 %shard_map.96 = (bf16[40,2048]{1,0:T(8,128)(2,1)S(1)}, f32[40,1]{1,0:T(8,128)S(1)}, bf16[40,896]{1,0:T(8,128)(2,1)S(1)}, f32[40,896]{1,0:T(8,128)S(1)}, bf16[40,...) custom-call(bf16[8,2176]{1,0:T(8,128)(2,1)S(1)} %fusion.7.refs_0_, bf16[8,2176]{1,0:T(8,128)(2,1)S(1)} %collective-permute-done.3.refs_1_, ...), custom_call_target="tpu_custom_call" | custom-call | flops 220200960 | tf_op jit(solution)/shard_map/pallas_call | solution.py:240
  24.6 2.9 %collective-permute-start.11 = (bf16[40,1024]{1,0:T(8,128)(2,1)S(1)}, bf16[40,1024]{1,0:T(8,128)(2,1)S(1)}, u32[]{:S(2)}, u32[]{:S(2)}) collective-permute-start(bf16[40,1024]{1,0:T(8,128)(2,1)S(1)} %add_convert_fusion.6), channel_id=1, source_target_pairs={{6,0},{7,1},{4,2},{5,3},{2,4},{3,5},{0,6},{1,7},{14,8},{15,9},{12,... | collective-permute-start | bytes 245768 | tf_op jit(solution)/shard_map/ppermute | solution.py:53
  27.5 1.6 %collective-permute-done.13 = bf16[40,1024]{1,0:T(8,128)(2,1)S(1)} collective-permute-done((bf16[40,1024]{1,0:T(8,128)(2,1)S(1)}, bf16[40,1024]{1,0:T(8,128)(2,1)S(1)}, u32[]{:S(2)}, u32[]{:S(2)}) %collective-permute-start.13) | collective-permute-done | bytes 81952 | tf_op jit(solution)/shard_map/ppermute | solution.py:53
  29.1 1.3 %collective-permute-done.12 = bf16[40,1024]{1,0:T(8,128)(2,1)S(1)} collective-permute-done((bf16[40,1024]{1,0:T(8,128)(2,1)S(1)}, bf16[40,1024]{1,0:T(8,128)(2,1)S(1)}, u32[]{:S(2)}, u32[]{:S(2)}) %collective-permute-start.12) | collective-permute-done | bytes 81952 | tf_op jit(solution)/shard_map/ppermute | solution.py:53
  30.4 1.4 %collective-permute-start.14 = (bf16[40,1024]{1,0:T(8,128)(2,1)S(1)}, bf16[40,1024]{1,0:T(8,128)(2,1)S(1)}, u32[]{:S(2)}, u32[]{:S(2)}) collective-permute-start(bf16[40,1024]{1,0:T(8,128)(2,1)S(1)} %add_convert_fusion.5), channel_id=1, source_target_pairs={{8,0},{9,1},{10,2},{11,3},{12,4},{13,5},{14,6},{15,7},{0,8},{1,9},... | collective-permute-start | bytes 245768 | tf_op jit(solution)/shard_map/ppermute | solution.py:53
  34.0 2.0 %collective-permute-done.14 = bf16[40,1024]{1,0:T(8,128)(2,1)S(1)} collective-permute-done((bf16[40,1024]{1,0:T(8,128)(2,1)S(1)}, bf16[40,1024]{1,0:T(8,128)(2,1)S(1)}, u32[]{:S(2)}, u32[]{:S(2)}) %collective-permute-start.14) | collective-permute-done | bytes 81952 | tf_op jit(solution)/shard_map/ppermute | solution.py:53
  39.5 1.8 %collective-permute-start.19 = (bf16[40,1024]{1,0:T(8,128)(2,1)S(1)}, bf16[40,1024]{1,0:T(8,128)(2,1)S(1)}, u32[]{:S(2)}, u32[]{:S(2)}) collective-permute-start(bf16[40,1024]{1,0:T(8,128)(2,1)S(1)} %add_convert_fusion.4), channel_id=1, source_target_pairs={{4,0},{5,1},{6,2},{7,3},{0,4},{1,5},{2,6},{3,7},{12,8},{13,9},{14,... | collective-permute-start | bytes 245768 | tf_op jit(solution)/shard_map/ppermute | solution.py:53
  44.1 2.5 %collective-permute-done.18 = bf16[40,1024]{1,0:T(8,128)(2,1)S(1)} collective-permute-done((bf16[40,1024]{1,0:T(8,128)(2,1)S(1)}, bf16[40,1024]{1,0:T(8,128)(2,1)S(1)}, u32[]{:S(2)}, u32[]{:S(2)}) %collective-permute-start.18) | collective-permute-done | bytes 81952 | tf_op jit(solution)/shard_map/ppermute | solution.py:53
  46.6 1.3 %collective-permute-done.17 = bf16[40,1024]{1,0:T(8,128)(2,1)S(1)} collective-permute-done((bf16[40,1024]{1,0:T(8,128)(2,1)S(1)}, bf16[40,1024]{1,0:T(8,128)(2,1)S(1)}, u32[]{:S(2)}, u32[]{:S(2)}) %collective-permute-start.17) | collective-permute-done | bytes 81952 | tf_op jit(solution)/shard_map/ppermute | solution.py:53
  49.2 5.0 %collective-permute-done.20 = bf16[40,1024]{1,0:T(8,128)(2,1)S(1)} collective-permute-done((bf16[40,1024]{1,0:T(8,128)(2,1)S(1)}, bf16[40,1024]{1,0:T(8,128)(2,1)S(1)}, u32[]{:S(2)}, u32[]{:S(2)}) %collective-permute-start.20) | collective-permute-done | bytes 81952 | tf_op jit(solution)/shard_map/ppermute | solution.py:53
  58.8 2.5 %collective-permute-start.23 = (bf16[40,1024]{1,0:T(8,128)(2,1)S(1)}, bf16[40,1024]{1,0:T(8,128)(2,1)S(1)}, u32[]{:S(2)}, u32[]{:S(2)}) collective-permute-start(bf16[40,1024]{1,0:T(8,128)(2,1)S(1)} %add_convert_fusion.1), channel_id=1, source_target_pairs={{6,0},{7,1},{4,2},{5,3},{2,4},{3,5},{0,6},{1,7},{14,8},{15,9},{12,... | collective-permute-start | bytes 245768 | tf_op jit(solution)/shard_map/ppermute | solution.py:53
  61.3 1.6 %collective-permute-done.25 = bf16[40,1024]{1,0:T(8,128)(2,1)S(1)} collective-permute-done((bf16[40,1024]{1,0:T(8,128)(2,1)S(1)}, bf16[40,1024]{1,0:T(8,128)(2,1)S(1)}, u32[]{:S(2)}, u32[]{:S(2)}) %collective-permute-start.25) | collective-permute-done | bytes 81952 | tf_op jit(solution)/shard_map/ppermute | solution.py:53
  62.9 1.5 %collective-permute-done.23 = bf16[40,1024]{1,0:T(8,128)(2,1)S(1)} collective-permute-done((bf16[40,1024]{1,0:T(8,128)(2,1)S(1)}, bf16[40,1024]{1,0:T(8,128)(2,1)S(1)}, u32[]{:S(2)}, u32[]{:S(2)}) %collective-permute-start.23) | collective-permute-done | bytes 81952 | tf_op jit(solution)/shard_map/ppermute | solution.py:53
  64.8 1.5 %collective-permute-start.27 = (bf16[2,2048]{1,0:T(2,128)(2,1)S(1)}, bf16[2,2048]{1,0:T(2,128)(2,1)S(1)}, u32[]{:S(2)}, u32[]{:S(2)}) collective-permute-start(bf16[2,2048]{1,0:T(2,128)(2,1)S(1)} %get-tuple-element.71), channel_id=1, source_target_pairs={{0,16},{1,17},{2,18},{3,19},{4,20},{5,21},{6,22},{7,23},{8,24},{9,... | collective-permute-start | bytes 24584 | tf_op jit(solution)/shard_map/ppermute | solution.py:53
  66.3 2.2 %collective-permute-done.27.refs_14_ = bf16[2,2048]{1,0:T(2,128)(2,1)S(1)} collective-permute-done((bf16[2,2048]{1,0:T(2,128)(2,1)S(1)}, bf16[2,2048]{1,0:T(2,128)(2,1)S(1)}, u32[]{:S(2)}, u32[]{:S(2)}) %collective-permute-start.27) | collective-permute-done | bytes 8224 | tf_op jit(solution)/shard_map/ppermute | solution.py:53
  68.4 1.7 %collective-permute-done.26 = bf16[40,1024]{1,0:T(8,128)(2,1)S(1)} collective-permute-done((bf16[40,1024]{1,0:T(8,128)(2,1)S(1)}, bf16[40,1024]{1,0:T(8,128)(2,1)S(1)}, u32[]{:S(2)}, u32[]{:S(2)}) %collective-permute-start.26) | collective-permute-done | bytes 81952 | tf_op jit(solution)/shard_map/ppermute | solution.py:53
  70.3 1.6 %shard_map.106 = (bf16[896,2048]{1,0:T(8,128)(2,1)}, f32[40,896]{1,0:T(8,128)S(1)}) custom-call(bf16[40,1024]{1,0:T(8,128)(2,1)S(1)} %multiply_convert_fusion.echo_own, bf16[40,1024]{1,0:T(8,128)(2,1)S(1)} %get-tuple-element.85.up_own, bf16[96,896]{1,0:T(8,128)(2,1)S(1)} %get-tuple-element.73.left.refs_2_, bf16[2048,896]{1,0:T(8,128)(2,1)S(1)} %shard_map.99.turned_out.refs_10_), custom_call_target="tpu_custom_call" | custom-call | flops 146800640 | tf_op jit(solution)/shard_map/pallas_call | solution.py:240
  71.9 3.2 %shard_map.107 = (bf16[896,2048]{1,0:T(8,128)(2,1)}, bf16[2048,896]{1,0:T(8,128)(2,1)}, bf16[2,2048]{1,0:T(2,128)(2,1)}) custom-call(bf16[40,1024]{1,0:T(8,128)(2,1)S(1)} %collective-permute-done.28.refs_0_, bf16[40,1024]{1,0:T(8,128)(2,1)S(1)} %collective-permute-done.15.up_other.refs_1_, ...), custom_call_target="tpu_custom_call", output_to_operand_aliasing={{0}: (15, {})} | custom-call | flops 293601280 | tf_op jit(solution)/shard_map/pallas_call | solution.py:240
  (67 shorter events, 22.0 us)
Async XLA Ops:
  1.5 6.7 %collective-permute-start.2 = (bf16[2,2176]{1,0:T(2,128)(2,1)S(1)}, bf16[2,2176]{1,0:T(2,128)(2,1)S(1)}, u32[]{:S(2)}, u32[]{:S(2)}) collective-permute-start(bf16[2,2176]{1,0:T(2,128)(2,1)S(1)} %broadcast_select_fusion.1.after_ref.refs_11_), channel_id=1, source_target_pairs={{18,0},{19,1},{16,2},{17,3},{22,4},{23,5},{20,6},{21,7},{26,8},{27... | collective-permute-start | bytes 26120 | tf_op jit(solution)/shard_map/ppermute | solution.py:53
  5.5 3.7 %collective-permute-start.1 = (bf16[2,2176]{1,0:T(2,128)(2,1)S(1)}, bf16[2,2176]{1,0:T(2,128)(2,1)S(1)}, u32[]{:S(2)}, u32[]{:S(2)}) collective-permute-start(bf16[2,2176]{1,0:T(2,128)(2,1)S(1)} %broadcast_select_fusion.1.after_ref.refs_11_), channel_id=1, source_target_pairs={{16,0},{17,1},{18,2},{19,3},{20,4},{21,5},{22,6},{23,7},{24,8},{25... | collective-permute-start | bytes 26120 | tf_op jit(solution)/shard_map/ppermute | solution.py:53
  6.0 3.7 %collective-permute-start = (bf16[2,2176]{1,0:T(2,128)(2,1)S(1)}, bf16[2,2176]{1,0:T(2,128)(2,1)S(1)}, u32[]{:S(2)}, u32[]{:S(2)}) collective-permute-start(bf16[2,2176]{1,0:T(2,128)(2,1)S(1)} %broadcast_select_fusion.1.after_ref.refs_11_), channel_id=1, source_target_pairs={{2,0},{3,1},{0,2},{1,3},{6,4},{7,5},{4,6},{5,7},{10,8},{11,9},{8,1... | collective-permute-start | bytes 26120 | tf_op jit(solution)/shard_map/ppermute | solution.py:53
  9.7 6.6 %collective-permute-start.4 = (bf16[8,2176]{1,0:T(8,128)(2,1)S(1)}, bf16[8,2176]{1,0:T(8,128)(2,1)S(1)}, u32[]{:S(2)}, u32[]{:S(2)}) collective-permute-start(bf16[8,2176]{1,0:T(8,128)(2,1)S(1)} %pad_maximum_fusion.after_ref), channel_id=1, source_target_pairs={{4,0},{5,1},{6,2},{7,3},{0,4},{1,5},{2,6},{3,7},{12,8},{13,9},{14,... | collective-permute-start | bytes 104456 | tf_op jit(solution)/shard_map/ppermute | solution.py:53
  11.4 5.5 %collective-permute-start.3 = (bf16[8,2176]{1,0:T(8,128)(2,1)S(1)}, bf16[8,2176]{1,0:T(8,128)(2,1)S(1)}, u32[]{:S(2)}, u32[]{:S(2)}) collective-permute-start(bf16[8,2176]{1,0:T(8,128)(2,1)S(1)} %pad_maximum_fusion.after_ref), channel_id=1, source_target_pairs={{8,0},{9,1},{10,2},{11,3},{12,4},{13,5},{14,6},{15,7},{0,8},{1,9},... | collective-permute-start | bytes 104456 | tf_op jit(solution)/shard_map/ppermute | solution.py:53
  14.0 5.7 %collective-permute-start.5 = (bf16[8,2176]{1,0:T(8,128)(2,1)S(1)}, bf16[8,2176]{1,0:T(8,128)(2,1)S(1)}, u32[]{:S(2)}, u32[]{:S(2)}) collective-permute-start(bf16[8,2176]{1,0:T(8,128)(2,1)S(1)} %pad_maximum_fusion.after_ref), channel_id=1, source_target_pairs={{12,0},{13,1},{14,2},{15,3},{8,4},{9,5},{10,6},{11,7},{4,8},{5,9},... | collective-permute-start | bytes 104456 | tf_op jit(solution)/shard_map/ppermute | solution.py:53
  16.3 3.4 %collective-permute-start.6 = (bf16[8,2176]{1,0:T(8,128)(2,1)S(1)}, bf16[8,2176]{1,0:T(8,128)(2,1)S(1)}, u32[]{:S(2)}, u32[]{:S(2)}) collective-permute-start(bf16[8,2176]{1,0:T(8,128)(2,1)S(1)} %fusion.7.refs_0_), channel_id=1, source_target_pairs={{1,0},{0,1},{3,2},{2,3},{5,4},{4,5},{7,6},{6,7},{9,8},{8,9},{11,10... | collective-permute-start | bytes 104456 | tf_op jit(solution)/shard_map/ppermute | solution.py:53
  16.4 3.3 %collective-permute-start.8 = (bf16[8,2176]{1,0:T(8,128)(2,1)S(1)}, bf16[8,2176]{1,0:T(8,128)(2,1)S(1)}, u32[]{:S(2)}, u32[]{:S(2)}) collective-permute-start(bf16[8,2176]{1,0:T(8,128)(2,1)S(1)} %collective-permute-done.4.refs_2_), channel_id=1, source_target_pairs={{1,0},{0,1},{3,2},{2,3},{5,4},{4,5},{7,6},{6,7},{9,8},{8,9},{11,10... | collective-permute-start | bytes 104456 | tf_op jit(solution)/shard_map/ppermute | solution.py:53
  16.9 2.8 %collective-permute-start.7 = (bf16[8,2176]{1,0:T(8,128)(2,1)S(1)}, bf16[8,2176]{1,0:T(8,128)(2,1)S(1)}, u32[]{:S(2)}, u32[]{:S(2)}) collective-permute-start(bf16[8,2176]{1,0:T(8,128)(2,1)S(1)} %collective-permute-done.3.refs_1_), channel_id=1, source_target_pairs={{1,0},{0,1},{3,2},{2,3},{5,4},{4,5},{7,6},{6,7},{9,8},{8,9},{11,10... | collective-permute-start | bytes 104456 | tf_op jit(solution)/shard_map/ppermute | solution.py:53
  22.6 1.3 %collective-permute-start.10 = (bf16[40,1024]{1,0:T(8,128)(2,1)S(1)}, bf16[40,1024]{1,0:T(8,128)(2,1)S(1)}, u32[]{:S(2)}, u32[]{:S(2)}) collective-permute-start(bf16[40,1024]{1,0:T(8,128)(2,1)S(1)} %get-tuple-element.56), channel_id=1, source_target_pairs={{1,0},{0,1},{3,2},{2,3},{5,4},{4,5},{7,6},{6,7},{9,8},{8,9},{11,10... | collective-permute-start | bytes 245768 | tf_op jit(solution)/shard_map/ppermute | solution.py:53
  23.9 5.1 %collective-permute-start.13 = (bf16[40,1024]{1,0:T(8,128)(2,1)S(1)}, bf16[40,1024]{1,0:T(8,128)(2,1)S(1)}, u32[]{:S(2)}, u32[]{:S(2)}) collective-permute-start(bf16[40,1024]{1,0:T(8,128)(2,1)S(1)} %add_convert_fusion.6), channel_id=1, source_target_pairs={{4,0},{5,1},{6,2},{7,3},{0,4},{1,5},{2,6},{3,7},{12,8},{13,9},{14,... | collective-permute-start | bytes 245768 | tf_op jit(solution)/shard_map/ppermute | solution.py:53
  24.0 6.3 %collective-permute-start.12 = (bf16[40,1024]{1,0:T(8,128)(2,1)S(1)}, bf16[40,1024]{1,0:T(8,128)(2,1)S(1)}, u32[]{:S(2)}, u32[]{:S(2)}) collective-permute-start(bf16[40,1024]{1,0:T(8,128)(2,1)S(1)} %add_convert_fusion.6), channel_id=1, source_target_pairs={{2,0},{3,1},{0,2},{1,3},{6,4},{7,5},{4,6},{5,7},{10,8},{11,9},{8,1... | collective-permute-start | bytes 245768 | tf_op jit(solution)/shard_map/ppermute | solution.py:53
  24.6 5.8 %collective-permute-start.11 = (bf16[40,1024]{1,0:T(8,128)(2,1)S(1)}, bf16[40,1024]{1,0:T(8,128)(2,1)S(1)}, u32[]{:S(2)}, u32[]{:S(2)}) collective-permute-start(bf16[40,1024]{1,0:T(8,128)(2,1)S(1)} %add_convert_fusion.6), channel_id=1, source_target_pairs={{6,0},{7,1},{4,2},{5,3},{2,4},{3,5},{0,6},{1,7},{14,8},{15,9},{12,... | collective-permute-start | bytes 245768 | tf_op jit(solution)/shard_map/ppermute | solution.py:53
  30.4 5.6 %collective-permute-start.14 = (bf16[40,1024]{1,0:T(8,128)(2,1)S(1)}, bf16[40,1024]{1,0:T(8,128)(2,1)S(1)}, u32[]{:S(2)}, u32[]{:S(2)}) collective-permute-start(bf16[40,1024]{1,0:T(8,128)(2,1)S(1)} %add_convert_fusion.5), channel_id=1, source_target_pairs={{8,0},{9,1},{10,2},{11,3},{12,4},{13,5},{14,6},{15,7},{0,8},{1,9},... | collective-permute-start | bytes 245768 | tf_op jit(solution)/shard_map/ppermute | solution.py:53
  39.5 4.6 %collective-permute-start.19 = (bf16[40,1024]{1,0:T(8,128)(2,1)S(1)}, bf16[40,1024]{1,0:T(8,128)(2,1)S(1)}, u32[]{:S(2)}, u32[]{:S(2)}) collective-permute-start(bf16[40,1024]{1,0:T(8,128)(2,1)S(1)} %add_convert_fusion.4), channel_id=1, source_target_pairs={{4,0},{5,1},{6,2},{7,3},{0,4},{1,5},{2,6},{3,7},{12,8},{13,9},{14,... | collective-permute-start | bytes 245768 | tf_op jit(solution)/shard_map/ppermute | solution.py:53
  41.3 5.3 %collective-permute-start.18 = (bf16[40,1024]{1,0:T(8,128)(2,1)S(1)}, bf16[40,1024]{1,0:T(8,128)(2,1)S(1)}, u32[]{:S(2)}, u32[]{:S(2)}) collective-permute-start(bf16[40,1024]{1,0:T(8,128)(2,1)S(1)} %add_convert_fusion.4), channel_id=1, source_target_pairs={{2,0},{3,1},{0,2},{1,3},{6,4},{7,5},{4,6},{5,7},{10,8},{11,9},{8,1... | collective-permute-start | bytes 245768 | tf_op jit(solution)/shard_map/ppermute | solution.py:53
  42.5 5.3 %collective-permute-start.17 = (bf16[40,1024]{1,0:T(8,128)(2,1)S(1)}, bf16[40,1024]{1,0:T(8,128)(2,1)S(1)}, u32[]{:S(2)}, u32[]{:S(2)}) collective-permute-start(bf16[40,1024]{1,0:T(8,128)(2,1)S(1)} %add_convert_fusion.4), channel_id=1, source_target_pairs={{6,0},{7,1},{4,2},{5,3},{2,4},{3,5},{0,6},{1,7},{14,8},{15,9},{12,... | collective-permute-start | bytes 245768 | tf_op jit(solution)/shard_map/ppermute | solution.py:53
  47.9 6.3 %collective-permute-start.20 = (bf16[40,1024]{1,0:T(8,128)(2,1)S(1)}, bf16[40,1024]{1,0:T(8,128)(2,1)S(1)}, u32[]{:S(2)}, u32[]{:S(2)}) collective-permute-start(bf16[40,1024]{1,0:T(8,128)(2,1)S(1)} %add_convert_fusion.3), channel_id=1, source_target_pairs={{8,0},{9,1},{10,2},{11,3},{12,4},{13,5},{14,6},{15,7},{0,8},{1,9},... | collective-permute-start | bytes 245768 | tf_op jit(solution)/shard_map/ppermute | solution.py:53
  57.7 5.1 %collective-permute-start.25 = (bf16[40,1024]{1,0:T(8,128)(2,1)S(1)}, bf16[40,1024]{1,0:T(8,128)(2,1)S(1)}, u32[]{:S(2)}, u32[]{:S(2)}) collective-permute-start(bf16[40,1024]{1,0:T(8,128)(2,1)S(1)} %add_convert_fusion.1), channel_id=1, source_target_pairs={{4,0},{5,1},{6,2},{7,3},{0,4},{1,5},{2,6},{3,7},{12,8},{13,9},{14,... | collective-permute-start | bytes 245768 | tf_op jit(solution)/shard_map/ppermute | solution.py:53
  57.8 5.1 %collective-permute-start.24 = (bf16[40,1024]{1,0:T(8,128)(2,1)S(1)}, bf16[40,1024]{1,0:T(8,128)(2,1)S(1)}, u32[]{:S(2)}, u32[]{:S(2)}) collective-permute-start(bf16[40,1024]{1,0:T(8,128)(2,1)S(1)} %add_convert_fusion.1), channel_id=1, source_target_pairs={{2,0},{3,1},{0,2},{1,3},{6,4},{7,5},{4,6},{5,7},{10,8},{11,9},{8,1... | collective-permute-start | bytes 245768 | tf_op jit(solution)/shard_map/ppermute | solution.py:53
  58.8 5.6 %collective-permute-start.23 = (bf16[40,1024]{1,0:T(8,128)(2,1)S(1)}, bf16[40,1024]{1,0:T(8,128)(2,1)S(1)}, u32[]{:S(2)}, u32[]{:S(2)}) collective-permute-start(bf16[40,1024]{1,0:T(8,128)(2,1)S(1)} %add_convert_fusion.1), channel_id=1, source_target_pairs={{6,0},{7,1},{4,2},{5,3},{2,4},{3,5},{0,6},{1,7},{14,8},{15,9},{12,... | collective-permute-start | bytes 245768 | tf_op jit(solution)/shard_map/ppermute | solution.py:53
  64.4 5.7 %collective-permute-start.26 = (bf16[40,1024]{1,0:T(8,128)(2,1)S(1)}, bf16[40,1024]{1,0:T(8,128)(2,1)S(1)}, u32[]{:S(2)}, u32[]{:S(2)}) collective-permute-start(bf16[40,1024]{1,0:T(8,128)(2,1)S(1)} %add_convert_fusion), channel_id=1, source_target_pairs={{8,0},{9,1},{10,2},{11,3},{12,4},{13,5},{14,6},{15,7},{0,8},{1,9},... | collective-permute-start | bytes 245768 | tf_op jit(solution)/shard_map/ppermute | solution.py:53
  64.8 3.7 %collective-permute-start.27 = (bf16[2,2048]{1,0:T(2,128)(2,1)S(1)}, bf16[2,2048]{1,0:T(2,128)(2,1)S(1)}, u32[]{:S(2)}, u32[]{:S(2)}) collective-permute-start(bf16[2,2048]{1,0:T(2,128)(2,1)S(1)} %get-tuple-element.71), channel_id=1, source_target_pairs={{0,16},{1,17},{2,18},{3,19},{4,20},{5,21},{6,22},{7,23},{8,24},{9,... | collective-permute-start | bytes 24584 | tf_op jit(solution)/shard_map/ppermute | solution.py:53
  70.2 1.7 %collective-permute-start.28 = (bf16[40,1024]{1,0:T(8,128)(2,1)S(1)}, bf16[40,1024]{1,0:T(8,128)(2,1)S(1)}, u32[]{:S(2)}, u32[]{:S(2)}) collective-permute-start(bf16[40,1024]{1,0:T(8,128)(2,1)S(1)} %multiply_convert_fusion.echo_own), channel_id=1, source_target_pairs={{1,0},{0,1},{3,2},{2,3},{5,4},{4,5},{7,6},{6,7},{9,8},{8,9},{11,10... | collective-permute-start | bytes 245768 | tf_op jit(solution)/shard_map/ppermute | solution.py:53
  (6 other events, 11.5 us)

commit v5 on v4

--- a/solution.py
+++ b/solution.py
@@ -72,7 +72,8 @@
         if at == 1:
             kept.append(hold_second(held[0]))
         if at > 1 and at == len(stages) - 1:
-            held[0] = held[0] + kept[1][1]
+            late = min(2, len(held) - 1)
+            held[late] = held[late] + kept[1][1]
         held += [fetch(part, steps_of(stage, offset)) for offset in offsets[1:] for part in held]
         blocks = [block + tuple(steps_of(stage, offset)) for offset in offsets for block in blocks]
     return held, blocks, [first for first, _ in kept]
@@ -220,7 +221,6 @@
     back = back_own[...] + dot(echo_other[...], turned_out[at_other, :])
     final_pre = (back * slope[...] + second[...] * back_hidden[...] * bend[...]).astype(BF)
     stack(right_in, back_pre[...], final_pre)
-    copies += product(left_in, right_in, made_in, grad_in, slice(None), sem_in, 256)
     slot = packed[:, 2 * half :].astype(F32)
     slot = slot[:, 1:2] * 128.0 + slot[:, 2:3]
     for columns, at in ((slice(0, half), at_own), (slice(half, 2 * half), at_other)):
@@ -230,6 +230,7 @@
         made_r2[:, at] = jnp.where(slot >= 0.0, picked, dropped).astype(BF)
     copies.append(pltpu.make_async_copy(made_r2, r2_grad, sem_r2))
     copies[-1].start()
+    copies += product(left_in, right_in, made_in, grad_in, slice(None), sem_in, 256)
     for copy in copies:
         copy.wait()
 

time: 75.4 us -> 75 us (level)
  waiting for transfers between devices: 30.6 us -> 25.5 us
  starting transfers between devices: 25.8 us -> 30.6 us
    ppermute x29, waiting for transfers between devices: 30.6 us -> 25.5 us  [fetch(): return lax.ppermute(values, axes, pairs)]
    ppermute x29, starting transfers between devices: 25.8 us -> 30.6 us  [fetch(): return lax.ppermute(values, axes, pairs)]
  transfers between devices with their start and end apart: 29 -> 29, of which waited for: 20 -> 21; matrix products, arithmetic and copies ran while one was open for 0% -> 0% of each run, Pallas kernels for 13% -> 13%
where the time goes in v5:
time: 75 us; the launch traced here: 74.7 us
  starting transfers between devices  30.6 us (41%)
  waiting for transfers between devices  25.5 us (34%)
  Pallas kernels  16.4 us (22%)
  other arithmetic  1.32 us (2%)
  between operations  0.89 us (1%)
    ppermute x29, starting transfers between devices, fetch(): return lax.ppermute(values, axes, pairs)  30.6 us
    ppermute x29, waiting for transfers between devices, fetch(): return lax.ppermute(values, axes, pairs)  25.5 us
    pallas_call x12, Pallas kernels, run(): pl.pallas_call(kernel, out_shape=[pltpu.VMEM(shape, kind) if at in kept e...  12.3 us
    pallas_call x2, Pallas kernels, hold(): pl.pallas_call(kernel, out_shape=(pltpu.VMEM(matrix.shape, matrix.dtype),...  4.09 us
  transfers between devices with their start and end apart: 29, of which 21 were waited for; matrix products, arithmetic and copies ran while one was open for 0% of the time, Pallas kernels for 13%

profile of v5, /device:TPU:0, one launch (start us, length us, event | category | flops | bytes accessed | tf_op | source)
XLA Modules:
  0.0 74.7 jit_solution(16830803569781946511)
XLA Ops:
  1.5 4.0 %collective-permute-start.2 = (bf16[2,2176]{1,0:T(2,128)(2,1)S(1)}, bf16[2,2176]{1,0:T(2,128)(2,1)S(1)}, u32[]{:S(2)}, u32[]{:S(2)}) collective-permute-start(bf16[2,2176]{1,0:T(2,128)(2,1)S(1)} %broadcast_select_fusion.1.after_ref.refs_11_), channel_id=1, source_target_pairs={{18,0},{19,1},{16,2},{17,3},{22,4},{23,5},{20,6},{21,7},{26,8},{27... | collective-permute-start | bytes 26120 | tf_op jit(solution)/shard_map/ppermute | solution.py:53
  6.1 2.0 %shard_map.94 = (bf16[2048,896]{1,0:T(8,128)(2,1)S(1)}, bf16[2,2176]{1,0:T(2,128)(2,1)S(1)}) custom-call(bf16[2048,896]{1,0:T(8,128)(2,1)} %bitcast.7, bf16[2,2176]{1,0:T(2,128)(2,1)S(1)} %broadcast_select_fusion.1.after_ref.refs_11_), custom_call_target="tpu_custom_call" | custom-call | bytes 7340032 | tf_op jit(solution)/shard_map/pallas_call | solution.py:268
  9.7 3.7 %collective-permute-start.5 = (bf16[8,2176]{1,0:T(8,128)(2,1)S(1)}, bf16[8,2176]{1,0:T(8,128)(2,1)S(1)}, u32[]{:S(2)}, u32[]{:S(2)}) collective-permute-start(bf16[8,2176]{1,0:T(8,128)(2,1)S(1)} %pad_maximum_fusion.after_ref.refs_0_), channel_id=1, source_target_pairs={{12,0},{13,1},{14,2},{15,3},{8,4},{9,5},{10,6},{11,7},{4,8},{5,9},... | collective-permute-start | bytes 104456 | tf_op jit(solution)/shard_map/ppermute | solution.py:53
  14.2 2.0 %shard_map.95 = (bf16[896,2048]{1,0:T(8,128)(2,1)S(1)}, bf16[8,2176]{1,0:T(8,128)(2,1)S(1)}) custom-call(bf16[896,2048]{1,0:T(8,128)(2,1)} %bitcast.6, bf16[8,2176]{1,0:T(8,128)(2,1)S(1)} %pad_maximum_fusion.after_ref.refs_0_), custom_call_target="tpu_custom_call" | custom-call | bytes 7340032 | tf_op jit(solution)/shard_map/pallas_call | solution.py:268
  16.8 1.4 %collective-permute-done.3.refs_1_ = bf16[8,2176]{1,0:T(8,128)(2,1)S(1)} collective-permute-done((bf16[8,2176]{1,0:T(8,128)(2,1)S(1)}, bf16[8,2176]{1,0:T(8,128)(2,1)S(1)}, u32[]{:S(2)}, u32[]{:S(2)}) %collective-permute-start.3) | collective-permute-done | bytes 34848 | tf_op jit(solution)/shard_map/ppermute | solution.py:53
  19.7 1.6 %shard_map.96 = (bf16[40,2048]{1,0:T(8,128)(2,1)S(1)}, f32[40,1]{1,0:T(8,128)S(1)}, bf16[40,896]{1,0:T(8,128)(2,1)S(1)}, f32[40,896]{1,0:T(8,128)S(1)}, bf16[40,...) custom-call(bf16[8,2176]{1,0:T(8,128)(2,1)S(1)} %pad_maximum_fusion.after_ref.refs_0_, ...), custom_call_target="tpu_custom_call" | custom-call | flops 220200960 | tf_op jit(solution)/shard_map/pallas_call | solution.py:241
  23.4 2.9 %collective-permute-start.11 = (bf16[40,1024]{1,0:T(8,128)(2,1)S(1)}, bf16[40,1024]{1,0:T(8,128)(2,1)S(1)}, u32[]{:S(2)}, u32[]{:S(2)}) collective-permute-start(bf16[40,1024]{1,0:T(8,128)(2,1)S(1)} %add_convert_fusion.6), channel_id=1, source_target_pairs={{6,0},{7,1},{4,2},{5,3},{2,4},{3,5},{0,6},{1,7},{14,8},{15,9},{12,... | collective-permute-start | bytes 245768 | tf_op jit(solution)/shard_map/ppermute | solution.py:53
  26.3 1.8 %collective-permute-done.13 = bf16[40,1024]{1,0:T(8,128)(2,1)S(1)} collective-permute-done((bf16[40,1024]{1,0:T(8,128)(2,1)S(1)}, bf16[40,1024]{1,0:T(8,128)(2,1)S(1)}, u32[]{:S(2)}, u32[]{:S(2)}) %collective-permute-start.13) | collective-permute-done | bytes 81952 | tf_op jit(solution)/shard_map/ppermute | solution.py:53
  28.0 1.3 %collective-permute-done.12 = bf16[40,1024]{1,0:T(8,128)(2,1)S(1)} collective-permute-done((bf16[40,1024]{1,0:T(8,128)(2,1)S(1)}, bf16[40,1024]{1,0:T(8,128)(2,1)S(1)}, u32[]{:S(2)}, u32[]{:S(2)}) %collective-permute-start.12) | collective-permute-done | bytes 81952 | tf_op jit(solution)/shard_map/ppermute | solution.py:53
  29.4 2.5 %collective-permute-start.14 = (bf16[40,1024]{1,0:T(8,128)(2,1)S(1)}, bf16[40,1024]{1,0:T(8,128)(2,1)S(1)}, u32[]{:S(2)}, u32[]{:S(2)}) collective-permute-start(bf16[40,1024]{1,0:T(8,128)(2,1)S(1)} %add_convert_fusion.5), channel_id=1, source_target_pairs={{8,0},{9,1},{10,2},{11,3},{12,4},{13,5},{14,6},{15,7},{0,8},{1,9},... | collective-permute-start | bytes 245768 | tf_op jit(solution)/shard_map/ppermute | solution.py:53
  38.5 1.5 %collective-permute-start.19 = (bf16[40,1024]{1,0:T(8,128)(2,1)S(1)}, bf16[40,1024]{1,0:T(8,128)(2,1)S(1)}, u32[]{:S(2)}, u32[]{:S(2)}) collective-permute-start(bf16[40,1024]{1,0:T(8,128)(2,1)S(1)} %add_convert_fusion.4), channel_id=1, source_target_pairs={{4,0},{5,1},{6,2},{7,3},{0,4},{1,5},{2,6},{3,7},{12,8},{13,9},{14,... | collective-permute-start | bytes 245768 | tf_op jit(solution)/shard_map/ppermute | solution.py:53
  40.1 1.3 %collective-permute-start.18 = (bf16[40,1024]{1,0:T(8,128)(2,1)S(1)}, bf16[40,1024]{1,0:T(8,128)(2,1)S(1)}, u32[]{:S(2)}, u32[]{:S(2)}) collective-permute-start(bf16[40,1024]{1,0:T(8,128)(2,1)S(1)} %add_convert_fusion.4), channel_id=1, source_target_pairs={{2,0},{3,1},{0,2},{1,3},{6,4},{7,5},{4,6},{5,7},{10,8},{11,9},{8,1... | collective-permute-start | bytes 245768 | tf_op jit(solution)/shard_map/ppermute | solution.py:53
  43.1 1.4 %collective-permute-done.18 = bf16[40,1024]{1,0:T(8,128)(2,1)S(1)} collective-permute-done((bf16[40,1024]{1,0:T(8,128)(2,1)S(1)}, bf16[40,1024]{1,0:T(8,128)(2,1)S(1)}, u32[]{:S(2)}, u32[]{:S(2)}) %collective-permute-start.18) | collective-permute-done | bytes 81952 | tf_op jit(solution)/shard_map/ppermute | solution.py:53
  44.5 2.2 %collective-permute-done.17 = bf16[40,1024]{1,0:T(8,128)(2,1)S(1)} collective-permute-done((bf16[40,1024]{1,0:T(8,128)(2,1)S(1)}, bf16[40,1024]{1,0:T(8,128)(2,1)S(1)}, u32[]{:S(2)}, u32[]{:S(2)}) %collective-permute-start.17) | collective-permute-done | bytes 81952 | tf_op jit(solution)/shard_map/ppermute | solution.py:53
  46.7 2.7 %collective-permute-start.20 = (bf16[40,1024]{1,0:T(8,128)(2,1)S(1)}, bf16[40,1024]{1,0:T(8,128)(2,1)S(1)}, u32[]{:S(2)}, u32[]{:S(2)}) collective-permute-start(bf16[40,1024]{1,0:T(8,128)(2,1)S(1)} %add_convert_fusion.3), channel_id=1, source_target_pairs={{8,0},{9,1},{10,2},{11,3},{12,4},{13,5},{14,6},{15,7},{0,8},{1,9},... | collective-permute-start | bytes 245768 | tf_op jit(solution)/shard_map/ppermute | solution.py:53
  49.4 2.7 %collective-permute-done.20 = bf16[40,1024]{1,0:T(8,128)(2,1)S(1)} collective-permute-done((bf16[40,1024]{1,0:T(8,128)(2,1)S(1)}, bf16[40,1024]{1,0:T(8,128)(2,1)S(1)}, u32[]{:S(2)}, u32[]{:S(2)}) %collective-permute-start.20) | collective-permute-done | bytes 81952 | tf_op jit(solution)/shard_map/ppermute | solution.py:53
  55.7 1.7 %collective-permute-start.25 = (bf16[40,1024]{1,0:T(8,128)(2,1)S(1)}, bf16[40,1024]{1,0:T(8,128)(2,1)S(1)}, u32[]{:S(2)}, u32[]{:S(2)}) collective-permute-start(bf16[40,1024]{1,0:T(8,128)(2,1)S(1)} %add_convert_fusion.1), channel_id=1, source_target_pairs={{4,0},{5,1},{6,2},{7,3},{0,4},{1,5},{2,6},{3,7},{12,8},{13,9},{14,... | collective-permute-start | bytes 245768 | tf_op jit(solution)/shard_map/ppermute | solution.py:53
  58.1 1.1 %collective-permute-start.23 = (bf16[40,1024]{1,0:T(8,128)(2,1)S(1)}, bf16[40,1024]{1,0:T(8,128)(2,1)S(1)}, u32[]{:S(2)}, u32[]{:S(2)}) collective-permute-start(bf16[40,1024]{1,0:T(8,128)(2,1)S(1)} %add_convert_fusion.1), channel_id=1, source_target_pairs={{6,0},{7,1},{4,2},{5,3},{2,4},{3,5},{0,6},{1,7},{14,8},{15,9},{12,... | collective-permute-start | bytes 245768 | tf_op jit(solution)/shard_map/ppermute | solution.py:53
  60.2 3.4 %collective-permute-done.24 = bf16[40,1024]{1,0:T(8,128)(2,1)S(1)} collective-permute-done((bf16[40,1024]{1,0:T(8,128)(2,1)S(1)}, bf16[40,1024]{1,0:T(8,128)(2,1)S(1)}, u32[]{:S(2)}, u32[]{:S(2)}) %collective-permute-start.24) | collective-permute-done | bytes 81952 | tf_op jit(solution)/shard_map/ppermute | solution.py:53
  63.7 1.6 %collective-permute-start.26 = (bf16[40,1024]{1,0:T(8,128)(2,1)S(1)}, bf16[40,1024]{1,0:T(8,128)(2,1)S(1)}, u32[]{:S(2)}, u32[]{:S(2)}) collective-permute-start(bf16[40,1024]{1,0:T(8,128)(2,1)S(1)} %add_convert_fusion), channel_id=1, source_target_pairs={{8,0},{9,1},{10,2},{11,3},{12,4},{13,5},{14,6},{15,7},{0,8},{1,9},... | collective-permute-start | bytes 245768 | tf_op jit(solution)/shard_map/ppermute | solution.py:53
  65.3 1.5 %collective-permute-start.27 = (bf16[2,2048]{1,0:T(2,128)(2,1)S(1)}, bf16[2,2048]{1,0:T(2,128)(2,1)S(1)}, u32[]{:S(2)}, u32[]{:S(2)}) collective-permute-start(bf16[2,2048]{1,0:T(2,128)(2,1)S(1)} %get-tuple-element.71), channel_id=1, source_target_pairs={{0,16},{1,17},{2,18},{3,19},{4,20},{5,21},{6,22},{7,23},{8,24},{9,... | collective-permute-start | bytes 24584 | tf_op jit(solution)/shard_map/ppermute | solution.py:53
  66.8 2.2 %collective-permute-done.27.refs_14_ = bf16[2,2048]{1,0:T(2,128)(2,1)S(1)} collective-permute-done((bf16[2,2048]{1,0:T(2,128)(2,1)S(1)}, bf16[2,2048]{1,0:T(2,128)(2,1)S(1)}, u32[]{:S(2)}, u32[]{:S(2)}) %collective-permute-start.27) | collective-permute-done | bytes 8224 | tf_op jit(solution)/shard_map/ppermute | solution.py:53
  69.9 1.6 %shard_map.106 = (bf16[896,2048]{1,0:T(8,128)(2,1)}, f32[40,896]{1,0:T(8,128)S(1)}) custom-call(bf16[40,1024]{1,0:T(8,128)(2,1)S(1)} %multiply_convert_fusion.echo_own, bf16[40,1024]{1,0:T(8,128)(2,1)S(1)} %get-tuple-element.85.up_own, bf16[96,896]{1,0:T(8,128)(2,1)S(1)} %get-tuple-element.73.left.refs_2_, bf16[2048,896]{1,0:T(8,128)(2,1)S(1)} %shard_map.99.turned_out.refs_10_), custom_call_target="tpu_custom_call" | custom-call | flops 146800640 | tf_op jit(solution)/shard_map/pallas_call | solution.py:241
  71.5 3.2 %shard_map.107 = (bf16[896,2048]{1,0:T(8,128)(2,1)}, bf16[2048,896]{1,0:T(8,128)(2,1)}, bf16[2,2048]{1,0:T(2,128)(2,1)}) custom-call(bf16[40,1024]{1,0:T(8,128)(2,1)S(1)} %collective-permute-done.28.refs_0_, bf16[40,1024]{1,0:T(8,128)(2,1)S(1)} %collective-permute-done.15.up_other.refs_1_, ...), custom_call_target="tpu_custom_call", output_to_operand_aliasing={{0}: (15, {})} | custom-call | flops 293601280 | tf_op jit(solution)/shard_map/pallas_call | solution.py:241
  (67 shorter events, 22.5 us)
Async XLA Ops:
  1.5 6.7 %collective-permute-start.2 = (bf16[2,2176]{1,0:T(2,128)(2,1)S(1)}, bf16[2,2176]{1,0:T(2,128)(2,1)S(1)}, u32[]{:S(2)}, u32[]{:S(2)}) collective-permute-start(bf16[2,2176]{1,0:T(2,128)(2,1)S(1)} %broadcast_select_fusion.1.after_ref.refs_11_), channel_id=1, source_target_pairs={{18,0},{19,1},{16,2},{17,3},{22,4},{23,5},{20,6},{21,7},{26,8},{27... | collective-permute-start | bytes 26120 | tf_op jit(solution)/shard_map/ppermute | solution.py:53
  5.5 3.7 %collective-permute-start.1 = (bf16[2,2176]{1,0:T(2,128)(2,1)S(1)}, bf16[2,2176]{1,0:T(2,128)(2,1)S(1)}, u32[]{:S(2)}, u32[]{:S(2)}) collective-permute-start(bf16[2,2176]{1,0:T(2,128)(2,1)S(1)} %broadcast_select_fusion.1.after_ref.refs_11_), channel_id=1, source_target_pairs={{16,0},{17,1},{18,2},{19,3},{20,4},{21,5},{22,6},{23,7},{24,8},{25... | collective-permute-start | bytes 26120 | tf_op jit(solution)/shard_map/ppermute | solution.py:53
  6.0 3.7 %collective-permute-start = (bf16[2,2176]{1,0:T(2,128)(2,1)S(1)}, bf16[2,2176]{1,0:T(2,128)(2,1)S(1)}, u32[]{:S(2)}, u32[]{:S(2)}) collective-permute-start(bf16[2,2176]{1,0:T(2,128)(2,1)S(1)} %broadcast_select_fusion.1.after_ref.refs_11_), channel_id=1, source_target_pairs={{2,0},{3,1},{0,2},{1,3},{6,4},{7,5},{4,6},{5,7},{10,8},{11,9},{8,1... | collective-permute-start | bytes 26120 | tf_op jit(solution)/shard_map/ppermute | solution.py:53
  9.7 6.5 %collective-permute-start.5 = (bf16[8,2176]{1,0:T(8,128)(2,1)S(1)}, bf16[8,2176]{1,0:T(8,128)(2,1)S(1)}, u32[]{:S(2)}, u32[]{:S(2)}) collective-permute-start(bf16[8,2176]{1,0:T(8,128)(2,1)S(1)} %pad_maximum_fusion.after_ref.refs_0_), channel_id=1, source_target_pairs={{12,0},{13,1},{14,2},{15,3},{8,4},{9,5},{10,6},{11,7},{4,8},{5,9},... | collective-permute-start | bytes 104456 | tf_op jit(solution)/shard_map/ppermute | solution.py:53
  13.4 4.8 %collective-permute-start.3 = (bf16[8,2176]{1,0:T(8,128)(2,1)S(1)}, bf16[8,2176]{1,0:T(8,128)(2,1)S(1)}, u32[]{:S(2)}, u32[]{:S(2)}) collective-permute-start(bf16[8,2176]{1,0:T(8,128)(2,1)S(1)} %pad_maximum_fusion.after_ref.refs_0_), channel_id=1, source_target_pairs={{8,0},{9,1},{10,2},{11,3},{12,4},{13,5},{14,6},{15,7},{0,8},{1,9},... | collective-permute-start | bytes 104456 | tf_op jit(solution)/shard_map/ppermute | solution.py:53
  13.4 4.8 %collective-permute-start.4 = (bf16[8,2176]{1,0:T(8,128)(2,1)S(1)}, bf16[8,2176]{1,0:T(8,128)(2,1)S(1)}, u32[]{:S(2)}, u32[]{:S(2)}) collective-permute-start(bf16[8,2176]{1,0:T(8,128)(2,1)S(1)} %pad_maximum_fusion.after_ref.refs_0_), channel_id=1, source_target_pairs={{4,0},{5,1},{6,2},{7,3},{0,4},{1,5},{2,6},{3,7},{12,8},{13,9},{14,... | collective-permute-start | bytes 104456 | tf_op jit(solution)/shard_map/ppermute | solution.py:53
  14.2 4.6 %collective-permute-start.6 = (bf16[8,2176]{1,0:T(8,128)(2,1)S(1)}, bf16[8,2176]{1,0:T(8,128)(2,1)S(1)}, u32[]{:S(2)}, u32[]{:S(2)}) collective-permute-start(bf16[8,2176]{1,0:T(8,128)(2,1)S(1)} %pad_maximum_fusion.after_ref.refs_0_), channel_id=1, source_target_pairs={{1,0},{0,1},{3,2},{2,3},{5,4},{4,5},{7,6},{6,7},{9,8},{8,9},{11,10... | collective-permute-start | bytes 104456 | tf_op jit(solution)/shard_map/ppermute | solution.py:53
  16.2 2.6 %collective-permute-start.9 = (bf16[8,2176]{1,0:T(8,128)(2,1)S(1)}, bf16[8,2176]{1,0:T(8,128)(2,1)S(1)}, u32[]{:S(2)}, u32[]{:S(2)}) collective-permute-start(bf16[8,2176]{1,0:T(8,128)(2,1)S(1)} %collective-permute-done.5.refs_3_), channel_id=1, source_target_pairs={{1,0},{0,1},{3,2},{2,3},{5,4},{4,5},{7,6},{6,7},{9,8},{8,9},{11,10... | collective-permute-start | bytes 104456 | tf_op jit(solution)/shard_map/ppermute | solution.py:53
  18.3 1.4 %collective-permute-start.8 = (bf16[8,2176]{1,0:T(8,128)(2,1)S(1)}, bf16[8,2176]{1,0:T(8,128)(2,1)S(1)}, u32[]{:S(2)}, u32[]{:S(2)}) collective-permute-start(bf16[8,2176]{1,0:T(8,128)(2,1)S(1)} %add.70.refs_2_), channel_id=1, source_target_pairs={{1,0},{0,1},{3,2},{2,3},{5,4},{4,5},{7,6},{6,7},{9,8},{8,9},{11,10... | collective-permute-start | bytes 104456 | tf_op jit(solution)/shard_map/ppermute | solution.py:53
  21.3 1.3 %collective-permute-start.10 = (bf16[40,1024]{1,0:T(8,128)(2,1)S(1)}, bf16[40,1024]{1,0:T(8,128)(2,1)S(1)}, u32[]{:S(2)}, u32[]{:S(2)}) collective-permute-start(bf16[40,1024]{1,0:T(8,128)(2,1)S(1)} %get-tuple-element.56), channel_id=1, source_target_pairs={{1,0},{0,1},{3,2},{2,3},{5,4},{4,5},{7,6},{6,7},{9,8},{8,9},{11,10... | collective-permute-start | bytes 245768 | tf_op jit(solution)/shard_map/ppermute | solution.py:53
  22.7 5.3 %collective-permute-start.13 = (bf16[40,1024]{1,0:T(8,128)(2,1)S(1)}, bf16[40,1024]{1,0:T(8,128)(2,1)S(1)}, u32[]{:S(2)}, u32[]{:S(2)}) collective-permute-start(bf16[40,1024]{1,0:T(8,128)(2,1)S(1)} %add_convert_fusion.6), channel_id=1, source_target_pairs={{4,0},{5,1},{6,2},{7,3},{0,4},{1,5},{2,6},{3,7},{12,8},{13,9},{14,... | collective-permute-start | bytes 245768 | tf_op jit(solution)/shard_map/ppermute | solution.py:53
  22.8 6.5 %collective-permute-start.12 = (bf16[40,1024]{1,0:T(8,128)(2,1)S(1)}, bf16[40,1024]{1,0:T(8,128)(2,1)S(1)}, u32[]{:S(2)}, u32[]{:S(2)}) collective-permute-start(bf16[40,1024]{1,0:T(8,128)(2,1)S(1)} %add_convert_fusion.6), channel_id=1, source_target_pairs={{2,0},{3,1},{0,2},{1,3},{6,4},{7,5},{4,6},{5,7},{10,8},{11,9},{8,1... | collective-permute-start | bytes 245768 | tf_op jit(solution)/shard_map/ppermute | solution.py:53
  23.4 5.9 %collective-permute-start.11 = (bf16[40,1024]{1,0:T(8,128)(2,1)S(1)}, bf16[40,1024]{1,0:T(8,128)(2,1)S(1)}, u32[]{:S(2)}, u32[]{:S(2)}) collective-permute-start(bf16[40,1024]{1,0:T(8,128)(2,1)S(1)} %add_convert_fusion.6), channel_id=1, source_target_pairs={{6,0},{7,1},{4,2},{5,3},{2,4},{3,5},{0,6},{1,7},{14,8},{15,9},{12,... | collective-permute-start | bytes 245768 | tf_op jit(solution)/shard_map/ppermute | solution.py:53
  29.4 5.6 %collective-permute-start.14 = (bf16[40,1024]{1,0:T(8,128)(2,1)S(1)}, bf16[40,1024]{1,0:T(8,128)(2,1)S(1)}, u32[]{:S(2)}, u32[]{:S(2)}) collective-permute-start(bf16[40,1024]{1,0:T(8,128)(2,1)S(1)} %add_convert_fusion.5), channel_id=1, source_target_pairs={{8,0},{9,1},{10,2},{11,3},{12,4},{13,5},{14,6},{15,7},{0,8},{1,9},... | collective-permute-start | bytes 245768 | tf_op jit(solution)/shard_map/ppermute | solution.py:53
  38.5 4.6 %collective-permute-start.19 = (bf16[40,1024]{1,0:T(8,128)(2,1)S(1)}, bf16[40,1024]{1,0:T(8,128)(2,1)S(1)}, u32[]{:S(2)}, u32[]{:S(2)}) collective-permute-start(bf16[40,1024]{1,0:T(8,128)(2,1)S(1)} %add_convert_fusion.4), channel_id=1, source_target_pairs={{4,0},{5,1},{6,2},{7,3},{0,4},{1,5},{2,6},{3,7},{12,8},{13,9},{14,... | collective-permute-start | bytes 245768 | tf_op jit(solution)/shard_map/ppermute | solution.py:53
  40.1 4.5 %collective-permute-start.18 = (bf16[40,1024]{1,0:T(8,128)(2,1)S(1)}, bf16[40,1024]{1,0:T(8,128)(2,1)S(1)}, u32[]{:S(2)}, u32[]{:S(2)}) collective-permute-start(bf16[40,1024]{1,0:T(8,128)(2,1)S(1)} %add_convert_fusion.4), channel_id=1, source_target_pairs={{2,0},{3,1},{0,2},{1,3},{6,4},{7,5},{4,6},{5,7},{10,8},{11,9},{8,1... | collective-permute-start | bytes 245768 | tf_op jit(solution)/shard_map/ppermute | solution.py:53
  41.3 5.3 %collective-permute-start.17 = (bf16[40,1024]{1,0:T(8,128)(2,1)S(1)}, bf16[40,1024]{1,0:T(8,128)(2,1)S(1)}, u32[]{:S(2)}, u32[]{:S(2)}) collective-permute-start(bf16[40,1024]{1,0:T(8,128)(2,1)S(1)} %add_convert_fusion.4), channel_id=1, source_target_pairs={{6,0},{7,1},{4,2},{5,3},{2,4},{3,5},{0,6},{1,7},{14,8},{15,9},{12,... | collective-permute-start | bytes 245768 | tf_op jit(solution)/shard_map/ppermute | solution.py:53
  46.7 5.4 %collective-permute-start.20 = (bf16[40,1024]{1,0:T(8,128)(2,1)S(1)}, bf16[40,1024]{1,0:T(8,128)(2,1)S(1)}, u32[]{:S(2)}, u32[]{:S(2)}) collective-permute-start(bf16[40,1024]{1,0:T(8,128)(2,1)S(1)} %add_convert_fusion.3), channel_id=1, source_target_pairs={{8,0},{9,1},{10,2},{11,3},{12,4},{13,5},{14,6},{15,7},{0,8},{1,9},... | collective-permute-start | bytes 245768 | tf_op jit(solution)/shard_map/ppermute | solution.py:53
  55.7 4.6 %collective-permute-start.25 = (bf16[40,1024]{1,0:T(8,128)(2,1)S(1)}, bf16[40,1024]{1,0:T(8,128)(2,1)S(1)}, u32[]{:S(2)}, u32[]{:S(2)}) collective-permute-start(bf16[40,1024]{1,0:T(8,128)(2,1)S(1)} %add_convert_fusion.1), channel_id=1, source_target_pairs={{4,0},{5,1},{6,2},{7,3},{0,4},{1,5},{2,6},{3,7},{12,8},{13,9},{14,... | collective-permute-start | bytes 245768 | tf_op jit(solution)/shard_map/ppermute | solution.py:53
  57.4 6.2 %collective-permute-start.24 = (bf16[40,1024]{1,0:T(8,128)(2,1)S(1)}, bf16[40,1024]{1,0:T(8,128)(2,1)S(1)}, u32[]{:S(2)}, u32[]{:S(2)}) collective-permute-start(bf16[40,1024]{1,0:T(8,128)(2,1)S(1)} %add_convert_fusion.1), channel_id=1, source_target_pairs={{2,0},{3,1},{0,2},{1,3},{6,4},{7,5},{4,6},{5,7},{10,8},{11,9},{8,1... | collective-permute-start | bytes 245768 | tf_op jit(solution)/shard_map/ppermute | solution.py:53
  58.1 5.5 %collective-permute-start.23 = (bf16[40,1024]{1,0:T(8,128)(2,1)S(1)}, bf16[40,1024]{1,0:T(8,128)(2,1)S(1)}, u32[]{:S(2)}, u32[]{:S(2)}) collective-permute-start(bf16[40,1024]{1,0:T(8,128)(2,1)S(1)} %add_convert_fusion.1), channel_id=1, source_target_pairs={{6,0},{7,1},{4,2},{5,3},{2,4},{3,5},{0,6},{1,7},{14,8},{15,9},{12,... | collective-permute-start | bytes 245768 | tf_op jit(solution)/shard_map/ppermute | solution.py:53
  63.7 6.1 %collective-permute-start.26 = (bf16[40,1024]{1,0:T(8,128)(2,1)S(1)}, bf16[40,1024]{1,0:T(8,128)(2,1)S(1)}, u32[]{:S(2)}, u32[]{:S(2)}) collective-permute-start(bf16[40,1024]{1,0:T(8,128)(2,1)S(1)} %add_convert_fusion), channel_id=1, source_target_pairs={{8,0},{9,1},{10,2},{11,3},{12,4},{13,5},{14,6},{15,7},{0,8},{1,9},... | collective-permute-start | bytes 245768 | tf_op jit(solution)/shard_map/ppermute | solution.py:53
  65.3 3.7 %collective-permute-start.27 = (bf16[2,2048]{1,0:T(2,128)(2,1)S(1)}, bf16[2,2048]{1,0:T(2,128)(2,1)S(1)}, u32[]{:S(2)}, u32[]{:S(2)}) collective-permute-start(bf16[2,2048]{1,0:T(2,128)(2,1)S(1)} %get-tuple-element.71), channel_id=1, source_target_pairs={{0,16},{1,17},{2,18},{3,19},{4,20},{5,21},{6,22},{7,23},{8,24},{9,... | collective-permute-start | bytes 24584 | tf_op jit(solution)/shard_map/ppermute | solution.py:53
  69.8 1.7 %collective-permute-start.28 = (bf16[40,1024]{1,0:T(8,128)(2,1)S(1)}, bf16[40,1024]{1,0:T(8,128)(2,1)S(1)}, u32[]{:S(2)}, u32[]{:S(2)}) collective-permute-start(bf16[40,1024]{1,0:T(8,128)(2,1)S(1)} %multiply_convert_fusion.echo_own), channel_id=1, source_target_pairs={{1,0},{0,1},{3,2},{2,3},{5,4},{4,5},{7,6},{6,7},{9,8},{8,9},{11,10... | collective-permute-start | bytes 245768 | tf_op jit(solution)/shard_map/ppermute | solution.py:53
  (6 other events, 11.5 us)
